TPU v7x, 32 devices: a whole 2x2x4 slice. The times are simulated.
32 devices in a mesh: ctx: 8 (over y, x, core), fsdp: 4 (over z).
Axes of the slice: x: 2, y: 2, z: 4, core: 2. Of those that a mesh axis runs over, the one named last changes fastest.
Arguments:
- layer_input: bfloat16 [4, 2048, 576], P('fsdp', 'ctx'), may hold values from -6 to 6
- slot_table: int32 [8], replicated, may hold values from 0 to 7, each once
- seq_ids: int32 [4, 2048], P('fsdp'), may hold values from 0 to 3, as said below
- w_query: bfloat16 [576, 576], P('fsdp'), may hold values from -0.5 to 0.5
- w_key: bfloat16 [576, 192], P('fsdp'), may hold values from -0.25 to 0.25
- w_value: bfloat16 [576, 192], P('fsdp'), may hold values from -0.25 to 0.25
- w_out: bfloat16 [576, 576], P('fsdp'), may hold values from -3 to 3
- w_gate: bfloat16 [576, 1536], P('fsdp'), may hold values from -0.25 to 0.25
- w_up: bfloat16 [576, 1536], P('fsdp'), may hold values from -0.25 to 0.25
- w_down: bfloat16 [1536, 576], P('fsdp'), may hold values from -0.15625 to 0.15625
- attn_gain: bfloat16 [576], P('fsdp'), may hold values from 0.5 to 1.5
- ffn_gain: bfloat16 [576], P('fsdp'), may hold values from 0.5 to 1.5
- cotangent: bfloat16 [4, 2048, 576], P('fsdp', 'ctx'), may hold values from -6 to 6
Outputs:
- output: bfloat16 [4, 2048, 576], P('fsdp', 'ctx')
- grad_input: bfloat16 [4, 2048, 576], P('fsdp', 'ctx')
- grad_wq: float32 [576, 576], P('fsdp')
- grad_wk: float32 [576, 192], P('fsdp')
- grad_wv: float32 [576, 192], P('fsdp')
- grad_wo: float32 [576, 576], P('fsdp')
- grad_w_gate: float32 [576, 1536], P('fsdp')
- grad_w_up: float32 [576, 1536], P('fsdp')
- grad_w_down: float32 [1536, 576], P('fsdp')
- grad_attn_gain: float32 [576], P('fsdp')
- grad_ffn_gain: float32 [576], P('fsdp')
Inputs may be any that keep to these rules, and one draw needn't show every extreme that they name: A permutation: context slot c holds blocks slot_table[c] and 15 - slot_table[c] of every sequence. `seq_ids`: never falls along natural positions; in each sequence one document starts at the first position or ends at the last and covers at least 1152 positions.
All inputs are finite; a program needn't handle non-finite values.
Results may differ from a plain program's by a relative error of at most 0.024.
Values may be sent and summed in bfloat16 or wider, within the bound.
No kernel may reach another device: no remote copies, remote signals or barrier semaphores. Data moves between devices by JAX's collectives and lax.ppermute only.
A program may use at most 128 MiB of HBM per device.

v0:
```python
import jax
import jax.numpy as jnp
from jax import lax
from jax.sharding import PartitionSpec as P

D = 576
HEADS = 9
KV_HEADS = 3
HEAD = 64


epsilon = 1e-05
rope_base = 100000.0


def rotary_tables(positions):
    half_width = HEAD // 2
    frequencies = rope_base ** (-(jnp.arange(half_width, dtype=jnp.float32) * 2.0 / HEAD))
    angles = positions.astype(jnp.float32)[:, None] * frequencies[None, :]
    return (jnp.cos(angles), jnp.sin(angles))


def rotate(values, cos_table, sin_table):
    half_width = HEAD // 2
    first_half = values[..., :half_width]
    second_half = values[..., half_width:]
    cos_part = cos_table[:, None, :]
    sin_part = sin_table[:, None, :]
    return jnp.concatenate(
        [
            first_half * cos_part - second_half * sin_part,
            second_half * cos_part + first_half * sin_part,
        ],
        axis=-1,
    )


def rotate_back(values, cos_table, sin_table):
    half_width = HEAD // 2
    first_half = values[..., :half_width]
    second_half = values[..., half_width:]
    cos_part = cos_table[:, None, :]
    sin_part = sin_table[:, None, :]
    return jnp.concatenate(
        [
            first_half * cos_part + second_half * sin_part,
            second_half * cos_part - first_half * sin_part,
        ],
        axis=-1,
    )


def matmul(first_matrix, second_matrix):
    return jnp.dot(first_matrix, second_matrix, preferred_element_type=jnp.float32)


def contract_rows(first_matrix, second_matrix):
    return lax.dot_general(
        first_matrix, second_matrix, (((0,), (0,)), ((), ())), preferred_element_type=jnp.float32
    )


def times_transposed(first_matrix, second_matrix):
    return lax.dot_general(
        first_matrix, second_matrix, (((1,), (1,)), ((), ())), preferred_element_type=jnp.float32
    )


def norm_back(grad_normed, unit_rows, inv_root, gain_vec):
    scaled_grad = grad_normed * gain_vec
    return inv_root * (
        scaled_grad - unit_rows * jnp.mean(scaled_grad * unit_rows, axis=-1, keepdims=True)
    )


def local(
    layer_input,
    slot_table,
    seq_ids,
    w_query,
    w_key,
    w_value,
    w_out,
    w_gate,
    w_up,
    w_down,
    attn_gain,
    ffn_gain,
    cotangent,
):
    ctx_count = lax.axis_size("ctx")
    ctx_index = lax.axis_index("ctx")
    row_count = layer_input.shape[1]
    block_len = row_count // 2
    key_count = row_count * ctx_count
    groups = HEADS // KV_HEADS
    kv_width = KV_HEADS * HEAD
    scaling = HEAD ** (-0.5)
    wq_all, wk_all, wv_all, wo_all, gate_all, up_all, down_all, gain_one, gain_two = (
        lax.all_gather(w_query, "fsdp", axis=0, tiled=True),
        lax.all_gather(w_key, "fsdp", axis=0, tiled=True),
        lax.all_gather(w_value, "fsdp", axis=0, tiled=True),
        lax.all_gather(w_out, "fsdp", axis=0, tiled=True),
        lax.all_gather(w_gate, "fsdp", axis=0, tiled=True),
        lax.all_gather(w_up, "fsdp", axis=0, tiled=True),
        lax.all_gather(w_down, "fsdp", axis=0, tiled=True),
        lax.all_gather(attn_gain, "fsdp", axis=0, tiled=True),
        lax.all_gather(ffn_gain, "fsdp", axis=0, tiled=True),
    )
    gain_one = gain_one.astype(jnp.float32)
    gain_two = gain_two.astype(jnp.float32)
    offsets = jnp.arange(row_count, dtype=jnp.int32)
    blocks = jnp.where(
        offsets[None, :] < block_len, slot_table[:, None], 2 * ctx_count - 1 - slot_table[:, None]
    )
    slot_pos = blocks * block_len + offsets[None, :] % block_len
    key_pos = slot_pos.reshape(key_count)
    key_doc = jnp.take(seq_ids[0], key_pos)
    query_pos = lax.dynamic_index_in_dim(slot_pos, ctx_index, 0, keepdims=False)
    query_doc = lax.dynamic_index_in_dim(
        key_doc.reshape(ctx_count, row_count), ctx_index, 0, keepdims=False
    )
    cos_table, sin_table = rotary_tables(query_pos)
    per_block = 1
    while per_block * 2 * row_count <= 512 and ctx_count % (per_block * 2) == 0:
        per_block = per_block * 2
    key_block = per_block * row_count
    block_count = key_count // key_block
    tokens = layer_input[0].astype(jnp.float32)
    inv_one = lax.rsqrt(jnp.mean(tokens * tokens, axis=-1, keepdims=True) + epsilon)
    unit_one = tokens * inv_one
    hidden_one = (unit_one * gain_one).astype(jnp.bfloat16)
    query_raw = matmul(hidden_one, wq_all).reshape(row_count, HEADS, HEAD)
    key_raw = matmul(hidden_one, wk_all).reshape(row_count, KV_HEADS, HEAD)
    value_low = matmul(hidden_one, wv_all).astype(jnp.bfloat16)
    query_rot = (
        (rotate(query_raw, cos_table, sin_table) * scaling)
        .astype(jnp.bfloat16)
        .reshape(row_count, KV_HEADS, groups, HEAD)
    )
    key_rot = (
        rotate(key_raw, cos_table, sin_table).astype(jnp.bfloat16).reshape(row_count, kv_width)
    )
    keys_all, values_all = (
        lax.all_gather(key_rot, "ctx", axis=0, tiled=True),
        lax.all_gather(value_low, "ctx", axis=0, tiled=True),
    )

    def key_blocks(keys_in, values_in):
        return (
            keys_in.reshape(block_count, key_block, KV_HEADS, HEAD),
            values_in.reshape(block_count, key_block, KV_HEADS, HEAD),
            key_pos.reshape(block_count, key_block),
            key_doc.reshape(block_count, key_block),
        )

    def visible_of(block_pos, block_doc):
        return (block_pos[None, :] <= query_pos[:, None]) & (
            block_doc[None, :] == query_doc[:, None]
        )

    def attend(state_in, pieces):
        running_top, total_weight, accumulated = state_in
        key_piece, value_piece, block_pos, block_doc = pieces
        visible = visible_of(block_pos, block_doc)
        scores = jnp.einsum(
            "qhgd,khd->hgqk", query_rot, key_piece, preferred_element_type=jnp.float32
        )
        scores = jnp.where(visible, scores, -1e30)
        new_top = jnp.maximum(running_top, jnp.max(scores, axis=-1))
        weights = jnp.where(visible, jnp.exp(scores - new_top[..., None]), 0.0)
        rescale = jnp.exp(running_top - new_top)
        total_weight = total_weight * rescale + jnp.sum(weights, axis=-1)
        accumulated = accumulated * rescale[..., None] + jnp.einsum(
            "hgqk,khd->hgqd",
            weights.astype(jnp.bfloat16),
            value_piece,
            preferred_element_type=jnp.float32,
        )
        return ((new_top, total_weight, accumulated), None)

    start_state = (
        jnp.full((KV_HEADS, groups, row_count), -1e30, jnp.float32),
        jnp.zeros((KV_HEADS, groups, row_count), jnp.float32),
        jnp.zeros((KV_HEADS, groups, row_count, HEAD), jnp.float32),
    )
    (running_top, total_weight, accumulated), _ = lax.scan(
        attend, start_state, key_blocks(keys_all, values_all)
    )
    attended = (accumulated / total_weight[..., None]).transpose(2, 0, 1, 3)
    log_total = running_top + jnp.log(total_weight)
    attn_low = attended.reshape(row_count, D).astype(jnp.bfloat16)
    residual = tokens + matmul(attn_low, wo_all)
    inv_two = lax.rsqrt(jnp.mean(residual * residual, axis=-1, keepdims=True) + epsilon)
    unit_two = residual * inv_two
    hidden_two = (unit_two * gain_two).astype(jnp.bfloat16)
    gate_value = matmul(hidden_two, gate_all)
    up_value = matmul(hidden_two, up_all)
    gate_sigmoid = jax.nn.sigmoid(gate_value)
    silu_gate = gate_value * gate_sigmoid
    activation = (silu_gate * up_value).astype(jnp.bfloat16)
    output = (residual + matmul(activation, down_all)).astype(jnp.bfloat16)
    grad_out = cotangent[0]
    grad_down_w = contract_rows(activation, grad_out)
    grad_activation = times_transposed(grad_out, down_all)
    grad_gate_low = (
        grad_activation * up_value * gate_sigmoid * (1.0 + gate_value * (1.0 - gate_sigmoid))
    ).astype(jnp.bfloat16)
    grad_up_low = (grad_activation * silu_gate).astype(jnp.bfloat16)
    grad_gate_w = contract_rows(hidden_two, grad_gate_low)
    grad_up_w = contract_rows(hidden_two, grad_up_low)
    grad_hidden_two = times_transposed(grad_gate_low, gate_all) + times_transposed(
        grad_up_low, up_all
    )
    grad_gain_two = jnp.sum(grad_hidden_two * unit_two, axis=0)
    grad_residual = grad_out.astype(jnp.float32) + norm_back(
        grad_hidden_two, unit_two, inv_two, gain_two
    )
    grad_branch = grad_residual.astype(jnp.bfloat16)
    grad_out_w = contract_rows(attn_low, grad_branch)
    grad_attended = (
        times_transposed(grad_branch, wo_all)
        .astype(jnp.bfloat16)
        .reshape(row_count, KV_HEADS, groups, HEAD)
    )
    grad_dot = jnp.sum(grad_attended.astype(jnp.float32) * attended, axis=-1).transpose(1, 2, 0)
    keys_back, values_back = (keys_all, values_all)

    def score_part(key_piece, value_piece, block_pos, block_doc):
        visible = visible_of(block_pos, block_doc)
        scores = jnp.einsum(
            "qhgd,khd->hgqk", query_rot, key_piece, preferred_element_type=jnp.float32
        )
        weights = jnp.where(visible, jnp.exp(scores - log_total[..., None]), 0.0)
        weight_grad = jnp.einsum(
            "qhgd,khd->hgqk", grad_attended, value_piece, preferred_element_type=jnp.float32
        )
        score_grad = (weights * (weight_grad - grad_dot[..., None])).astype(jnp.bfloat16)
        return (weights, score_grad)

    def key_part(weights, score_grad, piece_rows):
        value_grad = jnp.einsum(
            "hgqk,qhgd->khd",
            weights.astype(jnp.bfloat16),
            grad_attended,
            preferred_element_type=jnp.float32,
        )
        key_grad = jnp.einsum(
            "hgqk,qhgd->khd", score_grad, query_rot, preferred_element_type=jnp.float32
        )
        return jnp.concatenate(
            [key_grad.reshape(piece_rows, kv_width), value_grad.reshape(piece_rows, kv_width)],
            axis=1,
        )

    def query_add(query_grad, score_grad, key_piece):
        return query_grad + jnp.einsum(
            "hgqk,khd->qhgd", score_grad, key_piece, preferred_element_type=jnp.float32
        )

    query_start = jnp.zeros((row_count, KV_HEADS, groups, HEAD), jnp.float32)

    def backward_block(query_grad, pieces):
        weights, score_grad = score_part(*pieces)
        return (
            query_add(query_grad, score_grad, pieces[0]),
            key_part(weights, score_grad, key_block),
        )

    query_grad, key_terms = lax.scan(
        backward_block, query_start, key_blocks(keys_back, values_back)
    )
    owned_grads = lax.psum_scatter(
        key_terms.reshape(key_count, 2 * kv_width).astype(jnp.bfloat16),
        "ctx",
        scatter_dimension=0,
        tiled=True,
    ).astype(jnp.float32)
    grad_query_low = (
        (rotate_back(query_grad.reshape(row_count, HEADS, HEAD), cos_table, sin_table) * scaling)
        .reshape(row_count, D)
        .astype(jnp.bfloat16)
    )
    grad_key_low = (
        rotate_back(
            owned_grads[:, :kv_width].reshape(row_count, KV_HEADS, HEAD), cos_table, sin_table
        )
        .reshape(row_count, kv_width)
        .astype(jnp.bfloat16)
    )
    grad_value_low = owned_grads[:, kv_width:].astype(jnp.bfloat16)
    grad_query_w = contract_rows(hidden_one, grad_query_low)
    grad_key_w = contract_rows(hidden_one, grad_key_low)
    grad_value_w = contract_rows(hidden_one, grad_value_low)
    grad_hidden_one = (
        times_transposed(grad_query_low, wq_all)
        + times_transposed(grad_key_low, wk_all)
        + times_transposed(grad_value_low, wv_all)
    )
    grad_gain_one = jnp.sum(grad_hidden_one * unit_one, axis=0)
    grad_input = (grad_residual + norm_back(grad_hidden_one, unit_one, inv_one, gain_one)).astype(
        jnp.bfloat16
    )
    part_q, part_k, part_v, part_o, part_gate, part_up, part_down, part_one, part_two = (
        lax.psum_scatter(
            grad_query_w.astype(jnp.bfloat16), "fsdp", scatter_dimension=0, tiled=True
        ).astype(jnp.float32),
        lax.psum_scatter(
            grad_key_w.astype(jnp.bfloat16), "fsdp", scatter_dimension=0, tiled=True
        ).astype(jnp.float32),
        lax.psum_scatter(
            grad_value_w.astype(jnp.bfloat16), "fsdp", scatter_dimension=0, tiled=True
        ).astype(jnp.float32),
        lax.psum_scatter(
            grad_out_w.astype(jnp.bfloat16), "fsdp", scatter_dimension=0, tiled=True
        ).astype(jnp.float32),
        lax.psum_scatter(
            grad_gate_w.astype(jnp.bfloat16), "fsdp", scatter_dimension=0, tiled=True
        ).astype(jnp.float32),
        lax.psum_scatter(
            grad_up_w.astype(jnp.bfloat16), "fsdp", scatter_dimension=0, tiled=True
        ).astype(jnp.float32),
        lax.psum_scatter(
            grad_down_w.astype(jnp.bfloat16), "fsdp", scatter_dimension=0, tiled=True
        ).astype(jnp.float32),
        lax.psum_scatter(
            grad_gain_one.astype(jnp.bfloat16), "fsdp", scatter_dimension=0, tiled=True
        ).astype(jnp.float32),
        lax.psum_scatter(
            grad_gain_two.astype(jnp.bfloat16), "fsdp", scatter_dimension=0, tiled=True
        ).astype(jnp.float32),
    )
    shards = (
        lax.psum(part_q.astype(jnp.bfloat16), "ctx").astype(jnp.float32),
        lax.psum(part_k.astype(jnp.bfloat16), "ctx").astype(jnp.float32),
        lax.psum(part_v.astype(jnp.bfloat16), "ctx").astype(jnp.float32),
        lax.psum(part_o.astype(jnp.bfloat16), "ctx").astype(jnp.float32),
        lax.psum(part_gate.astype(jnp.bfloat16), "ctx").astype(jnp.float32),
        lax.psum(part_up.astype(jnp.bfloat16), "ctx").astype(jnp.float32),
        lax.psum(part_down.astype(jnp.bfloat16), "ctx").astype(jnp.float32),
        lax.psum(part_one.astype(jnp.bfloat16), "ctx").astype(jnp.float32),
        lax.psum(part_two.astype(jnp.bfloat16), "ctx").astype(jnp.float32),
    )
    return (
        output[None],
        grad_input[None],
        shards[0],
        shards[1],
        shards[2],
        shards[3],
        shards[4],
        shards[5],
        shards[6],
        shards[7],
        shards[8],
    )


def solution(mesh):
    placed = (
        P("fsdp", "ctx", None),
        P(),
        P("fsdp", None),
        P("fsdp", None),
        P("fsdp", None),
        P("fsdp", None),
        P("fsdp", None),
        P("fsdp", None),
        P("fsdp", None),
        P("fsdp", None),
        P("fsdp"),
        P("fsdp"),
        P("fsdp", "ctx", None),
    )
    return jax.shard_map(
        local,
        mesh=mesh,
        in_specs=placed,
        out_specs=(
            P("fsdp", "ctx", None),
            P("fsdp", "ctx", None),
            P("fsdp", None),
            P("fsdp", None),
            P("fsdp", None),
            P("fsdp", None),
            P("fsdp", None),
            P("fsdp", None),
            P("fsdp", None),
            P("fsdp"),
            P("fsdp"),
        ),
        check_vma=False,
    )
```

profile of v0, /device:TPU:0, one launch (start us, length us, event | category | flops | bytes accessed | tf_op | source)
XLA Modules:
  0.0 606.1 jit_solution(8433083913528616105)
XLA Ops:
  11.8 11.8 %gather_fusion = s32[2048]{0:T(1024)S(1)} fusion(s32[2048]{0:T(1024)S(1)} %bitcast.273, s32[2048]{0:T(1024)S(1)} %broadcast_clamp_fusion), kind=kCustom, calls=%fused_computation | custom fusion | bytes 24576 | tf_op jit(solution)/shard_map/jit(_take)/gather | solution.py:118
  26.7 14.4 %all-reduce.7 = (bf16[576]{0:T(1024)(128)(2,1)S(1)}, bf16[576]{0:T(1024)(128)(2,1)}) all-reduce(bf16[576]{0:T(1024)(128)(2,1)S(1)} %dynamic-update-slice, bf16[576]{0:T(1024)(128)(2,1)S(1)} %dynamic-update-slice.1), channel_id=1, replica_groups=mesh['ctx'=8,'fsdp'=4] {'fsdp'}, use_global_device_ids=true, to_apply=%add | all-reduce | flops 1152 | bytes 4608
  41.2 16.3 %all_gather.34 = bf16[576,192]{1,0:T(8,128)(2,1)S(1)} all-gather(bf16[144,192]{1,0:T(8,128)(2,1)S(1)} %copy-done.40), channel_id=1, replica_groups=mesh['ctx'=8,'fsdp'=4] {'fsdp'}, dimensions={0}, use_global_device_ids=true | all-gather | bytes 276480 | tf_op jit(solution)/shard_map/all_gather | solution.py:101
  57.7 15.0 %all_gather.37 = bf16[576,192]{1,0:T(8,128)(2,1)S(1)} all-gather(bf16[144,192]{1,0:T(8,128)(2,1)S(1)} %copy-done.41), channel_id=1, replica_groups=mesh['ctx'=8,'fsdp'=4] {'fsdp'}, dimensions={0}, use_global_device_ids=true | all-gather | bytes 276480 | tf_op jit(solution)/shard_map/all_gather | solution.py:102
  73.8 13.6 %all_gather.38 = bf16[2048,192]{0,1:T(8,128)(2,1)S(1)} all-gather(bf16[256,192]{0,1:T(8,128)(2,1)S(1)} %convolution_convert_fusion.8), channel_id=1, replica_groups=mesh['ctx'=8,'fsdp'=4] {'ctx'}, dimensions={0}, use_global_device_ids=true | all-gather | bytes 884736 | tf_op jit(solution)/shard_map/all_gather | solution.py:146
  89.3 11.8 %all_gather.35 = bf16[2048,192]{0,1:T(8,128)(2,1)S(1)} all-gather(bf16[256,192]{0,1:T(8,128)(2,1)S(1)} %bitcast.287), channel_id=1, replica_groups=mesh['ctx'=8,'fsdp'=4] {'ctx'}, dimensions={0}, use_global_device_ids=true | all-gather | bytes 884736 | tf_op jit(solution)/shard_map/all_gather | solution.py:145
  102.0 24.2 %all_gather.36 = bf16[576,576]{1,0:T(8,128)(2,1)S(1)} all-gather(bf16[144,576]{1,0:T(8,128)(2,1)S(1)} %copy-done.38), channel_id=1, replica_groups=mesh['ctx'=8,'fsdp'=4] {'fsdp'}, dimensions={0}, use_global_device_ids=true | all-gather | bytes 829440 | tf_op jit(solution)/shard_map/all_gather | solution.py:100
  128.2 17.5 %while.28 = (s32[]{:T(128)}, f32[3,3,256]{2,1,0:T(4,128)S(1)}, f32[3,3,256]{2,1,0:T(4,128)S(1)}, f32[3,3,256,64]{2,3,1,0:T(8,128)S(1)}, s32[4,512]{1,0:T(4,128)S...) while((s32[]{:T(128)}, f32[3,3,256]{2,1,0:T(4,128)S(1)}, ...), condition=%wide.region_4.5_spmd.clone, body=%wide.region_1.4_spmd.clone.sunk | while | flops 314633472 | bytes 16709789 | solution.py:187
  130.4 2.2 fusion.155
  134.8 2.2 fusion.155
  139.1 2.2 fusion.155
  143.5 2.2 fusion.155
  145.9 18.4 %all_gather.39 = bf16[576,576]{1,0:T(8,128)(2,1)S(1)} all-gather(bf16[144,576]{1,0:T(8,128)(2,1)S(1)} %copy-done.39), channel_id=1, replica_groups=mesh['ctx'=8,'fsdp'=4] {'fsdp'}, dimensions={0}, use_global_device_ids=true | all-gather | bytes 829440 | tf_op jit(solution)/shard_map/all_gather | solution.py:103
  165.3 3.5 fusion.87
  168.9 3.5 fusion.86
  172.4 4.8 multiply_convert_fusion
  183.9 31.6 %while.29 = (s32[]{:T(128)}, f32[256,3,3,64]{0,3,2,1:T(8,128)S(1)}, bf16[4,512,384]{2,1,0:T(8,128)(2,1)}, bf16[4,512,3,64]{1,3,2,0:T(8,128)(2,1)S(1)}, s32[4,512...) while((s32[]{:T(128)}, f32[256,3,3,64]{0,3,2,1:T(8,128)S(1)}, ...), condition=%wide.region_9.10_spmd.clone, body=%wide.region_8.9_spmd.clone.sunk | while | flops 765886464 | bytes 27370676 | solution.py:270
  185.0 1.9 fusion.169
  186.9 2.5 fusion.167
  192.9 1.9 fusion.169
  194.8 2.5 fusion.167
  200.8 1.9 fusion.169
  202.7 2.5 fusion.167
  208.7 1.9 fusion.169
  210.6 2.5 fusion.167
  215.5 2.6 copy.67
  218.3 38.3 %reduce-scatter.11.cloned.1.call-done = bf16[256,384]{0,1:T(8,128)(2,1)} async-done(((bf16[2048,384]{0,1:T(8,128)(2,1)}), bf16[256,384]{0,1:T(8,128)(2,1)}) %reduce-scatter.11.cloned.1.call-update) | async-done | bytes 196624 | tf_op jit(solution)/shard_map/reduce_scatter | solution.py:273
  259.8 1.8 convolution_convert_fusion
  261.6 2.3 copy.78
  265.0 1.4 convolution_convert_fusion.3
  268.0 3.0 convolution_convert_fusion.1
  271.2 1.8 convolution_convert_fusion.2
  275.9 11.9 %all-reduce.6 = (bf16[576]{0:T(1024)(128)(2,1)S(1)}, bf16[576]{0:T(1024)(128)(2,1)S(1)}) all-reduce(bf16[576]{0:T(1024)(128)(2,1)S(1)} %get-tuple-element.319, bf16[576]{0:T(1024)(128)(2,1)S(1)} %copy-done.42), channel_id=10, replica_groups=mesh['ctx'=8,'fsdp'=4] {'fsdp'}, use_global_device_ids=true, to_apply=%region_27.28.clone | all-reduce | flops 1152 | bytes 4608
  289.0 10.4 %reduce-scatter.17.cloned.1.call-done = bf16[144,192]{1,0:T(8,128)(2,1)} async-done(((bf16[576,192]{1,0:T(8,128)(2,1)}), bf16[144,192]{1,0:T(8,128)(2,1)}) %reduce-scatter.17.cloned.1.call-update) | async-done | bytes 55312 | tf_op jit(solution)/shard_map/reduce_scatter | solution.py:311
  299.5 41.9 %reduce-scatter.25.cloned.1.call-done = bf16[384,576]{1,0:T(8,128)(2,1)} async-done(((bf16[1536,576]{1,0:T(8,128)(2,1)}), bf16[384,576]{1,0:T(8,128)(2,1)}) %reduce-scatter.25.cloned.1.call-update) | async-done | bytes 442384
  341.4 2.0 copy.79
  343.4 22.5 %reduce-scatter.19.cloned.1.call-done = bf16[144,576]{1,0:T(8,128)(2,1)} async-done(((bf16[576,576]{1,0:T(8,128)(2,1)}), bf16[144,576]{1,0:T(8,128)(2,1)}) %reduce-scatter.19.cloned.1.call-update) | async-done | bytes 165904 | tf_op jit(solution)/shard_map/reduce_scatter | solution.py:314
  365.9 24.9 %reduce-scatter.13.cloned.1.call-done = bf16[144,576]{1,0:T(8,128)(2,1)} async-done(((bf16[576,576]{1,0:T(8,128)(2,1)}), bf16[144,576]{1,0:T(8,128)(2,1)}) %reduce-scatter.13.cloned.1.call-update) | async-done | bytes 165904 | tf_op jit(solution)/shard_map/reduce_scatter | solution.py:305
  390.9 39.7 %reduce-scatter.23.cloned.1.call-done = bf16[144,1536]{1,0:T(8,128)(2,1)} async-done(((bf16[576,1536]{1,0:T(8,128)(2,1)}), bf16[144,1536]{1,0:T(8,128)(2,1)}) %reduce-scatter.23.cloned.1.call-update) | async-done | bytes 442384 | tf_op jit(solution)/shard_map/reduce_scatter | solution.py:320
  430.5 40.0 %reduce-scatter.21.cloned.1.call-done = bf16[144,1536]{1,0:T(8,128)(2,1)} async-done(((bf16[576,1536]{1,0:T(8,128)(2,1)}), bf16[144,1536]{1,0:T(8,128)(2,1)}) %reduce-scatter.21.cloned.1.call-update) | async-done | bytes 442384 | tf_op jit(solution)/shard_map/reduce_scatter | solution.py:317
  470.5 2.8 fusion.43
  474.3 51.9 %all-reduce.11.cloned.1.call-done = (bf16[144,192]{1,0:T(8,128)(2,1)}, bf16[144,192]{1,0:T(8,128)(2,1)}, bf16[144]{0:T(256)(128)(2,1)}, bf16[144]{0:T(256)(128)(2,1)}) async-done(((bf16[144,192]{1,0:T(8,128)(2,1)}, bf16[144,192]{1,0:T(8,128)(2,1)}, bf16[144]{0:T(256)(128)(2,1)}, bf16[144]{0:T(256)(128)(2,1)}), (bf16[144,192]{1,0:T(8,128)(2,1)}, bf16[144,192]{1,0:T(8,128)(2,1)}, bf16[144]{0:T(256)(128)(2,1)}, ...) | async-done | bytes 111184 | tf_op jit(solution)/shard_map/psum | solution.py:335
  528.6 1.6 convert_element_type.232
  530.2 1.6 convert_element_type.234
  531.7 60.4 %all-reduce.13.cloned.1.call-done = (bf16[144,576]{1,0:T(8,128)(2,1)}, bf16[144,576]{1,0:T(8,128)(2,1)}, bf16[144,1536]{1,0:T(8,128)(2,1)}, bf16[144,1536]{1,0:T(8,128)(2,1)}, bf16[384,576]{0,1:T(8,128)(2,1)}) async-done(((bf16[144,576]{1,0:T(8,128)(2,1)}, bf16[144,576]{1,0:T(8,128)(2,1)}, bf16[144,1536]{1,0:T(8,128)(2,1)}, bf16[144,1536]{1,0:T(8,128)(2,1)}, bf16[384,576]{0,1:T(8,128)(2,1)}), ...) | async-done | bytes 1658896 | tf_op jit(solution)/shard_map/psum | solution.py:334
  592.2 1.8 convert_element_type.230
  593.9 1.7 convert_element_type.236
  595.6 2.0 convert_element_type.238
  (270 shorter events, 57.7 us)
Async XLA Ops:
  7.2 4.6 copy-start
  7.2 158.1 %all-gather.6.cloned.1.call-start = ((), (), s32[]{:S(2)}) async-start(), calls=%async_computation.9 | async-start | bytes 2211840 | tf_op jit(solution)/shard_map/all_gather | solution.py:105
  7.9 160.9 %all-gather.4.cloned.1.call-start = ((), (), s32[]{:S(2)}) async-start(), calls=%async_computation.8 | async-start | bytes 2211840 | tf_op jit(solution)/shard_map/all_gather | solution.py:104
  8.7 163.7 %all-gather.8.cloned.1.call-start = ((), (), s32[]{:S(2)}) async-start(), calls=%async_computation.10 | async-start | bytes 2211840 | tf_op jit(solution)/shard_map/all_gather | solution.py:106
  9.4 247.1 %reduce-scatter.11.cloned.1.call-start = ((), (), s32[]{:S(2)}) async-start(), calls=%async_computation.11 | async-start | bytes 1769472 | tf_op jit(solution)/shard_map/reduce_scatter | solution.py:273
  11.8 12.4 %copy-start.1 = (bf16[1,256,576]{1,2,0:T(8,128)(2,1)S(1)}, bf16[1,256,576]{1,2,0:T(8,128)(2,1)}, u32[]{:S(2)}) copy-start(bf16[1,256,576]{1,2,0:T(8,128)(2,1)} %param.17) | copy-start | bytes 884740
  11.8 13.1 %copy-start.45 = (u32[32]{0:T(128)S(1)}, u32[32]{0:T(128)}, u32[]{:S(2)}) copy-start(u32[32]{0:T(128)} %constant.111) | copy-start | bytes 388
  11.8 14.4 %copy-start.47 = (bf16[144]{0:T(256)(128)(2,1)S(1)}, bf16[144]{0:T(256)(128)(2,1)}, u32[]{:S(2)}) copy-start(bf16[144]{0:T(256)(128)(2,1)} %param.27) | copy-start | bytes 868
  11.8 14.6 %copy-start.48 = (bf16[144]{0:T(256)(128)(2,1)S(1)}, bf16[144]{0:T(256)(128)(2,1)}, u32[]{:S(2)}) copy-start(bf16[144]{0:T(256)(128)(2,1)} %param.28) | copy-start | bytes 868
  11.8 29.4 %copy-start.40 = (bf16[144,192]{1,0:T(8,128)(2,1)S(1)}, bf16[144,192]{1,0:T(8,128)(2,1)}, u32[]{:S(2)}) copy-start(bf16[144,192]{1,0:T(8,128)(2,1)} %param.21) | copy-start | bytes 165892
  11.8 45.9 %copy-start.41 = (bf16[144,192]{1,0:T(8,128)(2,1)S(1)}, bf16[144,192]{1,0:T(8,128)(2,1)}, u32[]{:S(2)}) copy-start(bf16[144,192]{1,0:T(8,128)(2,1)} %param.22) | copy-start | bytes 165892
  57.5 15.6 %copy-start.18 = (bf16[576,192]{1,0:T(8,128)(2,1)}, bf16[576,192]{1,0:T(8,128)(2,1)S(1)}, u32[]{:S(2)}) copy-start(bf16[576,192]{1,0:T(8,128)(2,1)S(1)} %all_gather.34) | copy-start | bytes 663556
  89.2 37.9 %copy-start.27 = (f32[256,32]{0,1:T(8,128)}, f32[256,32]{0,1:T(8,128)S(1)}, u32[]{:S(2)}) copy-start(f32[256,32]{0,1:T(8,128)S(1)} %get-tuple-element.407) | copy-start | bytes 98308
  89.2 37.9 %copy-start.30 = (f32[256,32]{0,1:T(8,128)}, f32[256,32]{0,1:T(8,128)S(1)}, u32[]{:S(2)}) copy-start(f32[256,32]{0,1:T(8,128)S(1)} %get-tuple-element.408) | copy-start | bytes 98308
  128.2 17.5 %copy-start.44 = (bf16[576]{0:T(1024)(128)(2,1)S(1)}, bf16[576]{0:T(1024)(128)(2,1)}, u32[]{:S(2)}) copy-start(bf16[576]{0:T(1024)(128)(2,1)} %get-tuple-element.381) | copy-start | bytes 3460
  128.2 17.6 %copy-start.39 = (bf16[144,576]{1,0:T(8,128)(2,1)S(1)}, bf16[144,576]{1,0:T(8,128)(2,1)}, u32[]{:S(2)}) copy-start(bf16[144,576]{1,0:T(8,128)(2,1)} %param.23) | copy-start | bytes 497668
  145.7 19.0 %copy-start.21 = (f32[3,3,256,64]{2,3,1,0:T(8,128)}, f32[3,3,256,64]{2,3,1,0:T(8,128)S(1)}, u32[]{:S(2)}) copy-start(f32[3,3,256,64]{2,3,1,0:T(8,128)S(1)} %get-tuple-element.138) | copy-start | bytes 1769476
  145.8 19.3 %copy-start.16 = (bf16[256,3,3,64]{0,3,2,1:T(8,128)(2,1)}, bf16[256,3,3,64]{0,3,2,1:T(8,128)(2,1)S(1)}, u32[]{:S(2)}) copy-start(bf16[256,3,3,64]{0,3,2,1:T(8,128)(2,1)S(1)} %bitcast_convert_fusion) | copy-start | bytes 884740
  165.3 3.6 copy-start.4
  168.9 3.6 copy-start.23
  172.4 4.8 copy-start.6
  177.2 3.4 copy-start.13
  177.2 3.4 copy-start.15
  177.2 2.0 copy-start.7
  180.6 2.2 copy-start.22
  181.7 2.2 copy-start.2
  218.2 39.3 %copy-start.28 = (f32[256,32]{0,1:T(8,128)S(1)}, f32[256,32]{0,1:T(8,128)}, u32[]{:S(2)}) copy-start(f32[256,32]{0,1:T(8,128)} %copy-done.27) | copy-start | bytes 98308
  218.2 39.4 %copy-start.31 = (f32[256,32]{0,1:T(8,128)S(1)}, f32[256,32]{0,1:T(8,128)}, u32[]{:S(2)}) copy-start(f32[256,32]{0,1:T(8,128)} %copy-done.30) | copy-start | bytes 98308
  218.2 41.6 %copy-start.24 = (bf16[1,256,576]{1,2,0:T(8,128)(2,1)S(1)}, bf16[1,256,576]{1,2,0:T(8,128)(2,1)}, u32[]{:S(2)}) copy-start(bf16[1,256,576]{1,2,0:T(8,128)(2,1)} %param.29) | copy-start | bytes 884740
  218.2 70.8 %reduce-scatter.15.cloned.1.call-start = ((), (), s32[]{:S(2)}) async-start(), calls=%async_computation.13 | async-start | bytes 368640 | tf_op jit(solution)/shard_map/reduce_scatter | solution.py:308
  256.5 2.2 copy-start.37
  257.6 2.2 copy-start.35
  258.6 40.8 %reduce-scatter.17.cloned.1.call-start = ((), (), s32[]{:S(2)}) async-start(), calls=%async_computation.14 | async-start | bytes 368640 | tf_op jit(solution)/shard_map/reduce_scatter | solution.py:311
  259.7 81.7 %reduce-scatter.25.cloned.1.call-start = ((), (), s32[]{:S(2)}) async-start(), calls=%async_computation.18 | async-start | bytes 2457600
  263.9 2.6 copy-start.29
  263.9 2.6 copy-start.32
  263.9 102.0 %reduce-scatter.19.cloned.1.call-start = ((), (), s32[]{:S(2)}) async-start(), calls=%async_computation.15 | async-start | bytes 921600 | tf_op jit(solution)/shard_map/reduce_scatter | solution.py:314
  266.4 124.4 %reduce-scatter.13.cloned.1.call-start = ((), (), s32[]{:S(2)}) async-start(), calls=%async_computation.12 | async-start | bytes 921600 | tf_op jit(solution)/shard_map/reduce_scatter | solution.py:305
  268.0 3.2 copy-start.14
  268.0 162.5 %reduce-scatter.23.cloned.1.call-start = ((), (), s32[]{:S(2)}) async-start(), calls=%async_computation.17 | async-start | bytes 2211840 | tf_op jit(solution)/shard_map/reduce_scatter | solution.py:320
  271.1 2.7 copy-start.19
  271.1 2.7 copy-start.36
  271.1 199.3 %reduce-scatter.21.cloned.1.call-start = ((), (), s32[]{:S(2)}) async-start(), calls=%async_computation.16 | async-start | bytes 2211840 | tf_op jit(solution)/shard_map/reduce_scatter | solution.py:317
  273.1 253.1 %all-reduce.11.cloned.1.call-start = ((), (), s32[]{:S(2)}) async-start(), calls=%async_computation.19 | async-start | bytes 296960 | tf_op jit(solution)/shard_map/psum | solution.py:335
  275.9 194.6 %copy-start.12 = (bf16[256,1536]{1,0:T(8,128)(2,1)S(1)}, bf16[256,1536]{1,0:T(8,128)(2,1)}, u32[]{:S(2)}) copy-start(bf16[256,1536]{1,0:T(8,128)(2,1)} %get-tuple-element.394) | copy-start | bytes 2359300
  299.4 292.7 %all-reduce.13.cloned.1.call-start = ((), (), s32[]{:S(2)}) async-start(), calls=%async_computation.20 | async-start | bytes 3391488 | tf_op jit(solution)/shard_map/psum | solution.py:334
  592.1 5.5 copy-start.34
  592.2 6.5 %copy-start.33 = (bf16[384,576]{0,1:T(8,128)(2,1)S(1)}, bf16[384,576]{0,1:T(8,128)(2,1)}, u32[]{:S(2)}) copy-start(bf16[384,576]{0,1:T(8,128)(2,1)} %get-tuple-element.377) | copy-start | bytes 1327108
  (14 other events, 15.2 us)
Sparse Core Ops, SparseCore 0:
  9.6 48.4 all-gather.5
  59.6 39.3 all-gather.3
  100.6 46.0 all-gather.7
  218.3 38.1 reduce-scatter.10
  259.2 19.8 reduce-scatter.14
  281.3 18.0 reduce-scatter.16
  301.7 39.6 reduce-scatter.24
  343.7 22.1 reduce-scatter.18
  368.8 21.9 reduce-scatter.12
  393.0 37.4 reduce-scatter.22
  433.0 37.4 reduce-scatter.20
  474.4 51.7 all-reduce.10
  530.6 61.4 all-reduce.12
where the time goes:
time: 607 us; the launch traced here: 606 us
  waiting for transfers between devices  332 us (55%)
  blocking collectives  126 us (21%)
  matrix products  71.5 us (12%)
  local copies, waits for them, and re-layouts  36.4 us (6%)
  other arithmetic  23.3 us (4%)
  between operations  16.1 us (3%)
    psum x1, waiting for transfers between devices, local(): lax.psum(part_q.astype(jnp.bfloat16), 'ctx').astype(jnp.float32)  60.4 us
    psum x1, waiting for transfers between devices, local(): lax.psum(part_k.astype(jnp.bfloat16), 'ctx').astype(jnp.float32)  51.9 us
    unnamed x14, waiting for transfers between devices  44.2 us
    reduce_scatter x1, waiting for transfers between devices, local(): lax.psum_scatter(grad_gate_w.astype(jnp.bfloat16), 'fsdp', scatter_dimens...  40 us
    reduce_scatter x1, waiting for transfers between devices, local(): lax.psum_scatter(grad_up_w.astype(jnp.bfloat16), 'fsdp', scatter_dimensio...  39.7 us
    reduce_scatter x1, waiting for transfers between devices, local(): lax.psum_scatter(key_terms.reshape(key_count, 2 * kv_width).astype(jnp.bf...  38.3 us
    unnamed x2, blocking collectives  26.3 us
    reduce_scatter x1, waiting for transfers between devices, local(): lax.psum_scatter(grad_query_w.astype(jnp.bfloat16), 'fsdp', scatter_dimen...  24.9 us
  transfers between devices with their start and end apart: 13, of which 9 were waited for; matrix products, arithmetic and copies ran while one was open for 12% of the time, Pallas kernels for 0%

commit v1 on v0

v1 whole, which is shorter than its diff:
```python
import jax
import jax.numpy as jnp
from jax import lax
from jax.experimental import pallas as pl
from jax.experimental.pallas import tpu as pltpu
from jax.sharding import PartitionSpec as P

D = 576
HEADS = 9
KV_HEADS = 3
HEAD = 64


epsilon = 1e-05
rope_base = 100000.0


def rotary_tables(positions):
    half_width = HEAD // 2
    frequencies = rope_base ** (-(jnp.arange(half_width, dtype=jnp.float32) * 2.0 / HEAD))
    angles = positions.astype(jnp.float32)[:, None] * frequencies[None, :]
    return (jnp.cos(angles), jnp.sin(angles))


def rotate(values, cos_table, sin_table):
    half_width = HEAD // 2
    first_half = values[..., :half_width]
    second_half = values[..., half_width:]
    cos_part = cos_table[:, None, :]
    sin_part = sin_table[:, None, :]
    return jnp.concatenate(
        [
            first_half * cos_part - second_half * sin_part,
            second_half * cos_part + first_half * sin_part,
        ],
        axis=-1,
    )


def rotate_back(values, cos_table, sin_table):
    half_width = HEAD // 2
    first_half = values[..., :half_width]
    second_half = values[..., half_width:]
    cos_part = cos_table[:, None, :]
    sin_part = sin_table[:, None, :]
    return jnp.concatenate(
        [
            first_half * cos_part + second_half * sin_part,
            second_half * cos_part - first_half * sin_part,
        ],
        axis=-1,
    )


def matmul(first_matrix, second_matrix):
    return jnp.dot(first_matrix, second_matrix, preferred_element_type=jnp.float32)


def contract_rows(first_matrix, second_matrix):
    return lax.dot_general(
        first_matrix, second_matrix, (((0,), (0,)), ((), ())), preferred_element_type=jnp.float32
    )


def times_transposed(first_matrix, second_matrix):
    return lax.dot_general(
        first_matrix, second_matrix, (((1,), (1,)), ((), ())), preferred_element_type=jnp.float32
    )


def norm_back(grad_normed, unit_rows, inv_root, gain_vec):
    scaled_grad = grad_normed * gain_vec
    return inv_root * (
        scaled_grad - unit_rows * jnp.mean(scaled_grad * unit_rows, axis=-1, keepdims=True)
    )


def swap(value, axis, offset):
    count = lax.axis_size(axis)
    return lax.ppermute(value, axis, [(i, i ^ offset) for i in range(count)])


def chip_swap(value, offset):
    return swap(value, "ctx", 2 * offset)


def core_swap(value):
    return swap(value, "ctx", 1)


def by_owner(pieces, index):
    bit = 1
    while bit < len(pieces):
        flag = (index & bit) != 0
        pieces = [jnp.where(flag, pieces[i ^ bit], pieces[i]) for i in range(len(pieces))]
        bit = bit * 2
    return pieces


def gather_rows(piece):
    count = lax.axis_size("fsdp")
    index = lax.axis_index("fsdp")
    pieces = [piece] + [swap(piece, "fsdp", i) for i in range(1, count)]
    return jnp.stack(by_owner(pieces, index))


def gather_chips(piece):
    chips = lax.axis_size("ctx") // 2
    own = [piece] + [chip_swap(piece, i) for i in range(1, chips)]
    return own + [core_swap(value) for value in own]


def place(pieces, shape, target, table=None):
    count = len(pieces)
    chips = count // 2
    scalars = [] if table is None else [table]

    def kernel(*refs):
        ins = refs[len(scalars) : len(scalars) + count]
        out = refs[-1]
        index = lax.axis_index("ctx")
        chip, core = index // 2, index % 2
        for n in range(count):
            target(out, ins[n], chip ^ (n % chips), core ^ (n // chips), *refs[: len(scalars)])

    return pl.pallas_call(
        kernel,
        out_shape=jax.ShapeDtypeStruct(shape, pieces[0].dtype),
        in_specs=[pl.BlockSpec(memory_space=pltpu.SMEM)] * len(scalars)
        + [pl.BlockSpec(memory_space=pltpu.VMEM)] * count,
        out_specs=pl.BlockSpec(memory_space=pltpu.VMEM),
        compiler_params=pltpu.CompilerParams(vmem_limit_bytes=56 * 1024 * 1024),
    )(*scalars, *pieces)


def store_chip_core(out, piece, to_chip, to_core):
    out[to_chip, to_core] = piece[...]


def store_core_chip(out, piece, to_chip, to_core):
    out[to_core, to_chip] = piece[...]


def store_chip_rows_core(out, piece, to_chip, to_core):
    out[to_chip, :, to_core] = piece[...]


def store_rows_chip_core(out, piece, to_chip, to_core):
    out[:, to_chip, to_core] = piece[...]


def store_blocks(out, piece, to_chip, to_core, table):
    block_len = out.shape[1]
    block = table[to_chip * 2 + to_core]
    out[block] = piece[:block_len]
    out[out.shape[0] - 1 - block] = piece[block_len:]


def dot_nt(first_matrix, second_matrix):
    return lax.dot_general(
        first_matrix, second_matrix, (((1,), (1,)), ((), ())), preferred_element_type=jnp.float32
    )


def dot_tn(first_matrix, second_matrix):
    return lax.dot_general(
        first_matrix, second_matrix, (((0,), (0,)), ((), ())), preferred_element_type=jnp.float32
    )


def heads_to_rows(values, group):
    groups = HEADS // KV_HEADS
    return jnp.concatenate(
        [
            values[:, (group * groups + i) * HEAD : (group * groups + i + 1) * HEAD]
            for i in range(groups)
        ],
        axis=0,
    )


def rows_to_heads(parts, block_len):
    groups = HEADS // KV_HEADS
    return jnp.concatenate(
        [part[i * block_len : (i + 1) * block_len] for part in parts for i in range(groups)],
        axis=1,
    )


def attention_forward(bounds, query_rot, pairs_all, first_key, last_key):
    row_count = query_rot.shape[0]
    block_len = row_count // 2
    groups = HEADS // KV_HEADS
    kv_width = KV_HEADS * HEAD
    wide = groups * block_len

    def kernel(bounds_ref, query_ref, pairs_ref, first_ref, last_ref, out_ref, log_ref):
        for b in range(2):
            rows = slice(b * block_len, (b + 1) * block_len)
            query_block = query_ref[rows, :]
            queries = [heads_to_rows(query_block, g) for g in range(KV_HEADS)]
            first = jnp.concatenate([first_ref[b : b + 1, :]] * groups, axis=1)
            last = jnp.concatenate([last_ref[b : b + 1, :]] * groups, axis=1)

            def step(j, state):
                start = pl.multiple_of(j * row_count, row_count)
                pos = start + lax.broadcasted_iota(jnp.int32, (row_count, wide), 0)
                visible = (pos >= first) & (pos <= last)
                result = []
                for g in range(KV_HEADS):
                    top, total, acc = state[g]
                    key_piece = pairs_ref[pl.ds(start, row_count), g * HEAD : (g + 1) * HEAD]
                    value_piece = pairs_ref[
                        pl.ds(start, row_count), kv_width + g * HEAD : kv_width + (g + 1) * HEAD
                    ]
                    scores = jnp.where(visible, dot_nt(key_piece, queries[g]), -1e30)
                    new_top = jnp.maximum(top, jnp.max(scores, axis=0, keepdims=True))
                    weights = jnp.exp(scores - new_top)
                    rescale = jnp.exp(top - new_top)
                    total = total * rescale + jnp.sum(weights, axis=0, keepdims=True)
                    acc = acc * rescale + dot_tn(value_piece, weights.astype(jnp.bfloat16))
                    result.append((new_top, total, acc))
                return tuple(result)

            state = lax.fori_loop(
                bounds_ref[2 * b],
                bounds_ref[2 * b + 1],
                step,
                tuple(
                    (
                        jnp.full((1, wide), -1e30, jnp.float32),
                        jnp.zeros((1, wide), jnp.float32),
                        jnp.zeros((HEAD, wide), jnp.float32),
                    )
                    for _ in range(KV_HEADS)
                ),
            )
            parts = []
            for g in range(KV_HEADS):
                top, total, acc = state[g]
                parts.append((acc / total).T)
                n = b * KV_HEADS + g
                log_ref[n : n + 1, :] = top + jnp.log(total)
            out_ref[rows, :] = rows_to_heads(parts, block_len)

    vmem = pl.BlockSpec(memory_space=pltpu.VMEM)
    return pl.pallas_call(
        kernel,
        out_shape=(
            jax.ShapeDtypeStruct((row_count, D), jnp.float32),
            jax.ShapeDtypeStruct((2 * KV_HEADS, wide), jnp.float32),
        ),
        in_specs=[pl.BlockSpec(memory_space=pltpu.SMEM)] + [vmem] * 4,
        out_specs=(vmem, vmem),
        compiler_params=pltpu.CompilerParams(vmem_limit_bytes=56 * 1024 * 1024),
        cost_estimate=pl.CostEstimate(
            flops=8 * 1024**3, bytes_accessed=4 * 1024**2, transcendentals=0
        ),
    )(bounds, query_rot, pairs_all, first_key, last_key)


def attention_backward(
    bounds, table, query_rot, pairs_all, first_key, last_key, log_total, attended, grad_attended
):
    row_count = query_rot.shape[0]
    block_len = row_count // 2
    groups = HEADS // KV_HEADS
    kv_width = KV_HEADS * HEAD
    wide = groups * block_len
    slots = table.shape[0]

    def kernel(
        bounds_ref,
        table_ref,
        query_ref,
        pairs_ref,
        first_ref,
        last_ref,
        log_ref,
        attended_ref,
        grad_ref,
        query_grad_ref,
        kept_ref,
        sent_ref,
        pair_grad_ref,
    ):
        pair_grad_ref[...] = jnp.zeros_like(pair_grad_ref)
        for b in range(2):
            rows = slice(b * block_len, (b + 1) * block_len)
            query_block = query_ref[rows, :]
            grad_block = grad_ref[rows, :]
            product = grad_block.astype(jnp.float32) * attended_ref[rows, :]
            queries = [heads_to_rows(query_block, g) for g in range(KV_HEADS)]
            grads = [heads_to_rows(grad_block, g) for g in range(KV_HEADS)]
            deltas = [
                jnp.sum(heads_to_rows(product, g).T, axis=0, keepdims=True)
                for g in range(KV_HEADS)
            ]
            first = jnp.concatenate([first_ref[b : b + 1, :]] * groups, axis=1)
            last = jnp.concatenate([last_ref[b : b + 1, :]] * groups, axis=1)

            def step(j, state):
                start = pl.multiple_of(j * row_count, row_count)
                pos = start + lax.broadcasted_iota(jnp.int32, (row_count, wide), 0)
                visible = (pos >= first) & (pos <= last)
                result = []
                key_grads = []
                value_grads = []
                for g in range(KV_HEADS):
                    key_piece = pairs_ref[pl.ds(start, row_count), g * HEAD : (g + 1) * HEAD]
                    value_piece = pairs_ref[
                        pl.ds(start, row_count), kv_width + g * HEAD : kv_width + (g + 1) * HEAD
                    ]
                    n = b * KV_HEADS + g
                    scores = dot_nt(key_piece, queries[g])
                    weights = jnp.where(visible, jnp.exp(scores - log_ref[n : n + 1, :]), 0.0)
                    weight_grad = dot_nt(value_piece, grads[g])
                    score_grad = (weights * (weight_grad - deltas[g])).astype(jnp.bfloat16)
                    value_grads.append(matmul(weights.astype(jnp.bfloat16), grads[g]))
                    key_grads.append(matmul(score_grad, queries[g]))
                    result.append(state[g] + dot_tn(key_piece, score_grad))
                pair_grad_ref[pl.ds(start, row_count), :] += jnp.concatenate(
                    key_grads + value_grads, axis=1
                )
                return tuple(result)

            state = lax.fori_loop(
                bounds_ref[2 * b],
                bounds_ref[2 * b + 1],
                step,
                tuple(jnp.zeros((HEAD, wide), jnp.float32) for _ in range(KV_HEADS)),
            )
            query_grad_ref[rows, :] = rows_to_heads([part.T for part in state], block_len)
        core = lax.axis_index("ctx") % 2
        for chip in range(slots // 2):
            for ref, owner in ((kept_ref, core), (sent_ref, 1 - core)):
                block = table_ref[chip * 2 + owner]
                other = 2 * slots - 1 - block
                for part, place_of in ((0, block), (1, other)):
                    source = pl.multiple_of(place_of * block_len, block_len)
                    ref[chip, part * block_len : (part + 1) * block_len, :] = pair_grad_ref[
                        pl.ds(source, block_len), :
                    ].astype(ref.dtype)

    vmem = pl.BlockSpec(memory_space=pltpu.VMEM)
    smem = pl.BlockSpec(memory_space=pltpu.SMEM)
    pair_shape = (slots // 2, row_count, 2 * kv_width)
    return pl.pallas_call(
        kernel,
        out_shape=(
            jax.ShapeDtypeStruct((row_count, D), jnp.float32),
            jax.ShapeDtypeStruct(pair_shape, jnp.float32),
            jax.ShapeDtypeStruct(pair_shape, jnp.bfloat16),
        ),
        in_specs=[smem, smem] + [vmem] * 7,
        out_specs=(vmem, vmem, vmem),
        scratch_shapes=[pltpu.VMEM((slots * row_count, 2 * kv_width), jnp.float32)],
        compiler_params=pltpu.CompilerParams(vmem_limit_bytes=56 * 1024 * 1024),
        cost_estimate=pl.CostEstimate(
            flops=16 * 1024**3, bytes_accessed=8 * 1024**2, transcendentals=0
        ),
    )(bounds, table, query_rot, pairs_all, first_key, last_key, log_total, attended, grad_attended)


def pick(values, index, axis=0):
    return lax.dynamic_index_in_dim(values, index, axis, keepdims=False)


def sum_chips(values):
    chips = lax.axis_size("ctx") // 2
    chip = lax.axis_index("ctx") // 2
    total = pick(values, chip).astype(jnp.float32)
    for i in range(1, chips):
        total = total + chip_swap(pick(values, chip ^ i), i).astype(jnp.float32)
    return total


def sum_rows(values):
    count = lax.axis_size("fsdp")
    index = lax.axis_index("fsdp")
    total = pick(values, index).astype(jnp.float32)
    for i in range(1, count):
        total = total + swap(pick(values, index ^ i), "fsdp", i).astype(jnp.float32)
    return total


def local(
    layer_input,
    slot_table,
    seq_ids,
    w_query,
    w_key,
    w_value,
    w_out,
    w_gate,
    w_up,
    w_down,
    attn_gain,
    ffn_gain,
    cotangent,
):
    ctx_count = lax.axis_size("ctx")
    ctx_index = lax.axis_index("ctx")
    row_count = layer_input.shape[1]
    block_len = row_count // 2
    key_count = row_count * ctx_count
    kv_width = KV_HEADS * HEAD
    scaling = HEAD ** (-0.5)
    chips = ctx_count // 2
    chip = ctx_index // 2
    core = ctx_index % 2
    shards_count = lax.axis_size("fsdp")
    shard_rows = w_query.shape[0]
    shard_down = w_down.shape[0]
    ff = w_gate.shape[1]
    mixed = w_query.shape[1] + 2 * kv_width + w_out.shape[1]
    lanes = ff // chips
    mixed_lanes = mixed // chips
    half_rows = shard_rows // 2
    down_rows = shard_down // ctx_count
    mixed_shard = jnp.concatenate([w_query, w_key, w_value, w_out], axis=1)
    mixed_piece = lax.dynamic_slice(
        mixed_shard, (core * half_rows, chip * mixed_lanes), (half_rows, mixed_lanes)
    )
    gains = jnp.concatenate([attn_gain, ffn_gain])
    gain_rows = -(-2 * shard_rows // mixed_lanes)
    gains = jnp.pad(gains, (0, gain_rows * mixed_lanes - 2 * shard_rows))
    mixed_rows = gather_rows(
        jnp.concatenate([mixed_piece, gains.reshape(gain_rows, mixed_lanes)], axis=0)
    )
    gains_all = mixed_rows[:, half_rows:].reshape(shards_count, gain_rows * mixed_lanes)
    gain_one = gains_all[:, :shard_rows].reshape(D).astype(jnp.float32)
    gain_two = gains_all[:, shard_rows : 2 * shard_rows].reshape(D).astype(jnp.float32)
    mixed_all = place(
        gather_chips(mixed_rows[:, :half_rows]),
        (chips, shards_count, 2, half_rows, mixed_lanes),
        store_chip_rows_core,
    )
    mixed_all = mixed_all.reshape(chips, D, mixed_lanes).transpose(1, 0, 2).reshape(D, mixed)
    wq_all = mixed_all[:, :D]
    wk_all = mixed_all[:, D : D + kv_width]
    wv_all = mixed_all[:, D + kv_width : D + 2 * kv_width]
    wo_all = mixed_all[:, D + 2 * kv_width :]
    gate_or_up = jnp.where(core == 0, w_gate, w_up)
    wide_piece = lax.dynamic_slice(gate_or_up, (0, chip * lanes), (shard_rows, lanes))
    wide_all = place(
        gather_chips(gather_rows(wide_piece)),
        (2, chips, shards_count, shard_rows, lanes),
        store_core_chip,
    )
    wide_all = wide_all.reshape(2, chips, D, lanes).transpose(0, 2, 1, 3).reshape(2, D, ff)
    gate_all, up_all = wide_all[0], wide_all[1]
    down_piece = lax.dynamic_slice(
        w_down, (ctx_index * down_rows, 0), (down_rows, w_down.shape[1])
    )
    down_all = place(
        gather_chips(gather_rows(down_piece)),
        (shards_count, chips, 2, down_rows, w_down.shape[1]),
        store_rows_chip_core,
    ).reshape(ff, w_down.shape[1])
    own_block = lax.dynamic_index_in_dim(slot_table, ctx_index, 0, keepdims=False)
    own_blocks = jnp.stack([own_block, 2 * ctx_count - 1 - own_block])
    block_pos = own_blocks[:, None] * block_len + jnp.arange(block_len, dtype=jnp.int32)[None, :]
    query_pos = block_pos.reshape(row_count)
    documents = seq_ids[0]
    query_doc = jnp.stack(
        [
            lax.dynamic_slice(documents, (own_block * block_len,), (block_len,)),
            lax.dynamic_slice(documents, (own_blocks[1] * block_len,), (block_len,)),
        ]
    )
    first_key = jnp.sum(
        (documents[None, :, None] < query_doc[:, None, :]).astype(jnp.int32), axis=1
    )
    bounds = jnp.stack(
        [jnp.min(first_key, axis=1) // row_count, own_blocks // 2 + 1], axis=1
    ).reshape(4)
    cos_table, sin_table = rotary_tables(query_pos)
    tokens = layer_input[0].astype(jnp.float32)
    inv_one = lax.rsqrt(jnp.mean(tokens * tokens, axis=-1, keepdims=True) + epsilon)
    unit_one = tokens * inv_one
    hidden_one = (unit_one * gain_one).astype(jnp.bfloat16)
    query_raw = matmul(hidden_one, wq_all).reshape(row_count, HEADS, HEAD)
    key_raw = matmul(hidden_one, wk_all).reshape(row_count, KV_HEADS, HEAD)
    value_low = matmul(hidden_one, wv_all).astype(jnp.bfloat16)
    query_rot = (
        (rotate(query_raw, cos_table, sin_table) * scaling)
        .astype(jnp.bfloat16)
        .reshape(row_count, D)
    )
    key_rot = (
        rotate(key_raw, cos_table, sin_table).astype(jnp.bfloat16).reshape(row_count, kv_width)
    )
    pairs_all = place(
        gather_chips(jnp.concatenate([key_rot, value_low], axis=1)),
        (2 * ctx_count, block_len, 2 * kv_width),
        store_blocks,
        slot_table,
    ).reshape(key_count, 2 * kv_width)
    attended, log_total = attention_forward(bounds, query_rot, pairs_all, first_key, block_pos)
    attn_low = attended.astype(jnp.bfloat16)
    residual = tokens + matmul(attn_low, wo_all)
    inv_two = lax.rsqrt(jnp.mean(residual * residual, axis=-1, keepdims=True) + epsilon)
    unit_two = residual * inv_two
    hidden_two = (unit_two * gain_two).astype(jnp.bfloat16)
    gate_value = matmul(hidden_two, gate_all)
    up_value = matmul(hidden_two, up_all)
    gate_sigmoid = jax.nn.sigmoid(gate_value)
    silu_gate = gate_value * gate_sigmoid
    activation = (silu_gate * up_value).astype(jnp.bfloat16)
    output = (residual + matmul(activation, down_all)).astype(jnp.bfloat16)
    grad_out = cotangent[0]
    grad_down_w = contract_rows(activation, grad_out)
    grad_activation = times_transposed(grad_out, down_all)
    grad_gate_low = (
        grad_activation * up_value * gate_sigmoid * (1.0 + gate_value * (1.0 - gate_sigmoid))
    ).astype(jnp.bfloat16)
    grad_up_low = (grad_activation * silu_gate).astype(jnp.bfloat16)
    wide_kept = contract_rows(hidden_two, jnp.where(core == 0, grad_gate_low, grad_up_low))
    wide_sent = contract_rows(hidden_two, jnp.where(core == 0, grad_up_low, grad_gate_low))
    wide_sum = (wide_kept + core_swap(wide_sent.astype(jnp.bfloat16)).astype(jnp.float32)).astype(
        jnp.bfloat16
    )
    wide_sum = wide_sum.reshape(D, chips, lanes).transpose(1, 0, 2)
    wide_sum = sum_chips(wide_sum).astype(jnp.bfloat16).reshape(shards_count, shard_rows, lanes)
    wide_part = sum_rows(wide_sum).astype(jnp.bfloat16)
    wide_grads = place(
        gather_chips(wide_part),
        (2, chips, shard_rows, lanes),
        store_core_chip,
    )
    wide_grads = wide_grads.transpose(0, 2, 1, 3).reshape(2, shard_rows, ff).astype(jnp.float32)
    grad_gate_w, grad_up_w = wide_grads[0], wide_grads[1]
    grad_down_w = grad_down_w.astype(jnp.bfloat16).reshape(
        shards_count, chips, 2, down_rows, w_down.shape[1]
    )
    down_sum = (
        pick(grad_down_w, core, 2).astype(jnp.float32)
        + core_swap(pick(grad_down_w, 1 - core, 2)).astype(jnp.float32)
    ).astype(jnp.bfloat16)
    down_sum = sum_chips(down_sum.transpose(1, 0, 2, 3)).astype(jnp.bfloat16)
    down_part = sum_rows(down_sum).astype(jnp.bfloat16)
    grad_down_w = (
        place(
            gather_chips(down_part),
            (chips, 2, down_rows, w_down.shape[1]),
            store_chip_core,
        )
        .reshape(shard_down, w_down.shape[1])
        .astype(jnp.float32)
    )
    grad_hidden_two = times_transposed(grad_gate_low, gate_all) + times_transposed(
        grad_up_low, up_all
    )
    grad_residual = grad_out.astype(jnp.float32) + norm_back(
        grad_hidden_two, unit_two, inv_two, gain_two
    )
    grad_branch = grad_residual.astype(jnp.bfloat16)
    grad_out_w = contract_rows(attn_low, grad_branch)
    grad_attended = times_transposed(grad_branch, wo_all).astype(jnp.bfloat16)
    query_grad, pairs_kept, pairs_sent = attention_backward(
        bounds,
        slot_table,
        query_rot,
        pairs_all,
        first_key,
        block_pos,
        log_total,
        attended,
        grad_attended,
    )
    owned_grads = sum_chips(
        (pairs_kept + core_swap(pairs_sent).astype(jnp.float32)).astype(jnp.bfloat16)
    )
    grad_query_low = (
        (rotate_back(query_grad.reshape(row_count, HEADS, HEAD), cos_table, sin_table) * scaling)
        .reshape(row_count, D)
        .astype(jnp.bfloat16)
    )
    grad_key_low = (
        rotate_back(
            owned_grads[:, :kv_width].reshape(row_count, KV_HEADS, HEAD), cos_table, sin_table
        )
        .reshape(row_count, kv_width)
        .astype(jnp.bfloat16)
    )
    grad_value_low = owned_grads[:, kv_width:].astype(jnp.bfloat16)
    grad_query_w = contract_rows(hidden_one, grad_query_low)
    grad_key_w = contract_rows(hidden_one, grad_key_low)
    grad_value_w = contract_rows(hidden_one, grad_value_low)
    grad_hidden_one = (
        times_transposed(grad_query_low, wq_all)
        + times_transposed(grad_key_low, wk_all)
        + times_transposed(grad_value_low, wv_all)
    )
    grad_input = (grad_residual + norm_back(grad_hidden_one, unit_one, inv_one, gain_one)).astype(
        jnp.bfloat16
    )
    mixed_grads = jnp.concatenate(
        [grad_query_w, grad_key_w, grad_value_w, grad_out_w], axis=1
    ).astype(jnp.bfloat16)
    mixed_grads = (
        mixed_grads.reshape(D, chips, mixed_lanes)
        .transpose(1, 0, 2)
        .reshape(chips, shards_count, 2, half_rows, mixed_lanes)
    )
    mixed_sum = (
        pick(mixed_grads, core, 2).astype(jnp.float32)
        + core_swap(pick(mixed_grads, 1 - core, 2)).astype(jnp.float32)
    ).astype(jnp.bfloat16)
    mixed_sum = sum_chips(mixed_sum).astype(jnp.bfloat16)
    mixed_part = sum_rows(mixed_sum).astype(jnp.bfloat16)
    mixed_shards = place(
        gather_chips(mixed_part),
        (chips, 2, half_rows, mixed_lanes),
        store_chip_core,
    )
    mixed_shards = (
        mixed_shards.reshape(chips, shard_rows, mixed_lanes)
        .transpose(1, 0, 2)
        .reshape(shard_rows, mixed)
        .astype(jnp.float32)
    )
    grad_gain_one = (
        jnp.sum(
            mixed_shards[:, : D + 2 * kv_width]
            * mixed_shard[:, : D + 2 * kv_width].astype(jnp.float32),
            axis=1,
        )
        / attn_gain.astype(jnp.float32)
    )
    grad_gain_two = (
        jnp.sum(grad_gate_w * w_gate.astype(jnp.float32), axis=1)
        + jnp.sum(grad_up_w * w_up.astype(jnp.float32), axis=1)
    ) / ffn_gain.astype(jnp.float32)
    return (
        output[None],
        grad_input[None],
        mixed_shards[:, :D],
        mixed_shards[:, D : D + kv_width],
        mixed_shards[:, D + kv_width : D + 2 * kv_width],
        mixed_shards[:, D + 2 * kv_width :],
        grad_gate_w,
        grad_up_w,
        grad_down_w,
        grad_gain_one,
        grad_gain_two,
    )


def solution(mesh):
    placed = (
        P("fsdp", "ctx", None),
        P(),
        P("fsdp", None),
        P("fsdp", None),
        P("fsdp", None),
        P("fsdp", None),
        P("fsdp", None),
        P("fsdp", None),
        P("fsdp", None),
        P("fsdp", None),
        P("fsdp"),
        P("fsdp"),
        P("fsdp", "ctx", None),
    )
    return jax.shard_map(
        local,
        mesh=mesh,
        in_specs=placed,
        out_specs=(
            P("fsdp", "ctx", None),
            P("fsdp", "ctx", None),
            P("fsdp", None),
            P("fsdp", None),
            P("fsdp", None),
            P("fsdp", None),
            P("fsdp", None),
            P("fsdp", None),
            P("fsdp", None),
            P("fsdp"),
            P("fsdp"),
        ),
        check_vma=False,
    )
```

time: 607 us -> 311 us (0.51)
  waiting for transfers between devices: 332 us -> 57 us
  blocking collectives: 126 us -> 0 us
  starting transfers between devices: 0.52 us -> 85.7 us
  matrix products: 71.5 us -> 27 us
  Pallas kernels: 0 us -> 43.9 us
  local copies, waits for them, and re-layouts: 36.4 us -> 66.5 us
  between operations: 16.1 us -> 3.43 us
    reduce_scatter x7 -> x0, waiting for transfers between devices: 176 us -> none  [the longest x1 40 us: local(): lax.psum_scatter(grad_gate_w.astype(jnp.bfloat16), 'fsdp', scatter_dimens...]
    psum x2 -> x0, waiting for transfers between devices: 112 us -> none  [the longest x1 60.4 us: local(): lax.psum(part_q.astype(jnp.bfloat16), 'ctx').astype(jnp.float32)]
    all_gather x6 -> x0, blocking collectives: 99.3 us -> none  [the longest x1 24.2 us: local(): lax.all_gather(w_query, 'fsdp', axis=0, tiled=True)]
    ppermute x0 -> x83, starting transfers between devices: none -> 85.7 us  [swap(): return lax.ppermute(value, axis, [(i, i ^ offset) for i in range(count)])]
    ppermute x0 -> x83, waiting for transfers between devices: none -> 57 us  [swap(): return lax.ppermute(value, axis, [(i, i ^ offset) for i in range(count)])]
    unnamed x14 -> x0, waiting for transfers between devices: 44.2 us -> none
    pallas_call x0 -> x9, Pallas kernels: none -> 43.9 us  [the longest x1 18.9 us: attention_backward(): pl.pallas_call(kernel, out_shape=(jax.ShapeDtypeStruct((row_count, D), jn...]
    dot_general x28 -> x0, matrix products: 38.7 us -> none  [the longest x4 10.1 us: score_part(): jnp.einsum('qhgd,khd->hgqk', grad_attended, value_piece, preferred_elemen...]
  transfers between devices with their start and end apart: 13 -> 83, of which waited for: 9 -> 17; matrix products, arithmetic and copies ran while one was open for 12% -> 27% of each run, Pallas kernels for 0% -> 6%
where the time goes in v1:
time: 311 us; the launch traced here: 307 us
  starting transfers between devices  85.7 us (28%)
  local copies, waits for them, and re-layouts  66.5 us (21%)
  waiting for transfers between devices  57 us (18%)
  Pallas kernels  43.9 us (14%)
  matrix products  27 us (9%)
  other arithmetic  23.2 us (7%)
  between operations  3.43 us (1%)
    ppermute x83, starting transfers between devices, swap(): return lax.ppermute(value, axis, [(i, i ^ offset) for i in range(count)])  85.7 us
    ppermute x83, waiting for transfers between devices, swap(): return lax.ppermute(value, axis, [(i, i ^ offset) for i in range(count)])  57 us
    pallas_call x1, Pallas kernels, attention_backward(): pl.pallas_call(kernel, out_shape=(jax.ShapeDtypeStruct((row_count, D), jn...  18.9 us
    pallas_call x7, Pallas kernels, place(): pl.pallas_call(kernel, out_shape=jax.ShapeDtypeStruct(shape, pieces[0].dt...  18.8 us
    unnamed x171, local copies, waits for them, and re-layouts  17 us
    dot_general x7, matrix products, contract_rows(): lax.dot_general(first_matrix, second_matrix, (((0,), (0,)), ((), ())), pr...  13 us
    another operation x3, local copies, waits for them, and re-layouts  8.23 us
    dot_general x7, matrix products, times_transposed(): lax.dot_general(first_matrix, second_matrix, (((1,), (1,)), ((), ())), pr...  7.52 us
  transfers between devices with their start and end apart: 83, of which 17 were waited for; matrix products, arithmetic and copies ran while one was open for 27% of the time, Pallas kernels for 6%

profile of v1, /device:TPU:0, one launch (start us, length us, event | category | flops | bytes accessed | tf_op | source)
XLA Modules:
  0.0 306.8 jit_solution(8752805708137180804)
XLA Ops:
  2.9 5.1 %collective-permute-start = (bf16[73,384]{1,0:T(8,128)(2,1)S(1)}, bf16[73,384]{1,0:T(8,128)(2,1)S(1)}, u32[]{:S(2)}, u32[]{:S(2)}) collective-permute-start(bf16[73,384]{1,0:T(8,128)(2,1)S(1)} %pad_maximum_fusion.7), channel_id=1, source_target_pairs={{0,3},{1,2},{2,1},{3,0},{4,7},{5,6},{6,5},{7,4},{8,11},{9,10},{10,... | collective-permute-start | bytes 168200 | tf_op jit(solution)/shard_map/ppermute | solution.py:80
  8.2 2.0 collective-permute-start.27
  20.0 2.8 collective-permute-start.17
  27.4 3.9 %collective-permute-done.18 = bf16[144,384]{1,0:T(8,128)(2,1)S(1)} collective-permute-done((bf16[144,384]{1,0:T(8,128)(2,1)S(1)}, bf16[144,384]{1,0:T(8,128)(2,1)S(1)}, u32[]{:S(2)}, u32[]{:S(2)}) %collective-permute-start.18) | collective-permute-done | bytes 110624 | tf_op jit(solution)/shard_map/ppermute | solution.py:80
  32.0 4.7 %collective-permute-done.19 = bf16[144,384]{1,0:T(8,128)(2,1)S(1)} collective-permute-done((bf16[144,384]{1,0:T(8,128)(2,1)S(1)}, bf16[144,384]{1,0:T(8,128)(2,1)S(1)}, u32[]{:S(2)}, u32[]{:S(2)}) %collective-permute-start.19) | collective-permute-done | bytes 110624 | tf_op jit(solution)/shard_map/ppermute | solution.py:80
  41.0 3.4 %collective-permute-done.3.refs_1_ = bf16[4,72,384]{2,1,0:T(8,128)(2,1)} collective-permute-done((bf16[4,72,384]{2,1,0:T(8,128)(2,1)S(1)}, bf16[4,72,384]{2,1,0:T(8,128)(2,1)}, u32[]{:S(2)}, u32[]{:S(2)}) %collective-permute-start.3) | collective-permute-done | bytes 221216 | tf_op jit(solution)/shard_map/ppermute | solution.py:80
  44.4 3.5 %collective-permute-done.4.refs_2_ = bf16[4,72,384]{2,1,0:T(8,128)(2,1)} collective-permute-done((bf16[4,72,384]{2,1,0:T(8,128)(2,1)S(1)}, bf16[4,72,384]{2,1,0:T(8,128)(2,1)}, u32[]{:S(2)}, u32[]{:S(2)}) %collective-permute-start.4) | collective-permute-done | bytes 221216 | tf_op jit(solution)/shard_map/ppermute | solution.py:80
  51.6 3.1 %shard_map.216 = bf16[4,4,2,48,576]{4,3,2,1,0:T(8,128)(2,1)} custom-call(bf16[4,48,576]{2,1,0:T(8,128)(2,1)} %copy-done.25, bf16[4,48,576]{2,1,0:T(8,128)(2,1)} %copy-done.42, bf16[4,48,576]{2,1,0:T(8,128)(2,1)} %copy-done.43, bf16[4,48,576]{2,1,0:T(8,128)(2,1)} %copy-done.44, bf16[4,48,576]{2,1,0:T(8,128)(2,1)} %copy-done.45, ...), custom_call_target="tpu_custom_call" | custom-call | tf_op jit(solution)/shard_map/pallas_call | solution.py:126
  58.9 2.9 shard_map.212
  61.8 2.8 copy.99
  73.5 4.5 %collective-permute-done.21.refs_2_ = bf16[4,144,384]{2,1,0:T(8,128)(2,1)} collective-permute-done((bf16[4,144,384]{2,1,0:T(8,128)(2,1)}, bf16[4,144,384]{2,1,0:T(8,128)(2,1)}, u32[]{:S(2)}, u32[]{:S(2)}) %collective-permute-start.21) | collective-permute-done | bytes 442400 | tf_op jit(solution)/shard_map/ppermute | solution.py:80
  78.5 6.6 %collective-permute-done.11.refs_3_ = bf16[256,384]{1,0:T(8,128)(2,1)} collective-permute-done((bf16[256,384]{1,0:T(8,128)(2,1)}, bf16[256,384]{1,0:T(8,128)(2,1)}, u32[]{:S(2)}, u32[]{:S(2)}) %collective-permute-start.11) | collective-permute-done | bytes 196640 | tf_op jit(solution)/shard_map/ppermute | solution.py:80
  87.8 2.8 shard_map.213
  90.5 6.2 %shard_map.214 = (f32[256,576]{1,0:T(8,128)}, f32[6,384]{1,0:T(8,128)}) custom-call(s32[4]{0:T(128)} %reshape.547.bounds_ref, bf16[256,576]{1,0:T(8,128)(2,1)} %copy.104.query_ref, bf16[2048,384]{1,0:T(8,128)(2,1)} %bitcast.295, s32[2,128]{1,0:T(2,128)} %copy-done.76, s32[2,128]{1,0:T(2,128)} %get-tuple-element.126.last_ref), custom_call_target="tpu_custom_call" | custom-call | flops 8589934592 | bytes 4194304 | tf_op jit(solution)/shard_map/pallas_call | solution.py:247
  96.8 2.1 multiply_reduce_fusion.3
  100.9 4.1 %shard_map.215 = bf16[2,4,4,144,384]{4,3,2,1,0:T(8,128)(2,1)} custom-call(bf16[4,144,384]{2,1,0:T(8,128)(2,1)} %pad_maximum_fusion.refs_0_, bf16[4,144,384]{2,1,0:T(8,128)(2,1)} %collective-permute-done.20.refs_1_, bf16[4,144,384]{2,1,0:T(8,128)(2,1)} %collective-permute-done.21.refs_2_, bf16[4,144,384]{2,1,0:T(8,128)(2,1)} %collective-permute-done.22.refs_3_, ...), custom_call_target="tpu_custom_call" | custom-call | tf_op jit(solution)/shard_map/pallas_call | solution.py:126
  105.0 4.7 %copy.156 = bf16[2,4,576,384]{3,1,2,0:T(4,128)(2,1)S(1)} copy(bf16[2,4,576,384]{3,2,1,0:T(8,128)(2,1)} %bitcast.268) | data formatting | bytes 7077888 | tf_op jit(solution)/shard_map/reshape | solution.py:451
  113.9 2.3 multiply_convert_fusion
  116.8 2.0 convolution_convert_fusion.1
  120.8 1.9 copy.109.grad_ref
  122.7 18.9 %shard_map.217 = (f32[256,576]{1,0:T(8,128)}, f32[4,256,384]{2,1,0:T(8,128)}, bf16[4,256,384]{2,1,0:T(8,128)(2,1)}) custom-call(s32[4]{0:T(128)} %reshape.547.bounds_ref, s32[8]{0:T(128)} %table_ref.1, bf16[256,576]{1,0:T(8,128)(2,1)} %copy.104.query_ref, bf16[2048,384]{1,0:T(8,128)(2,1)} %bitcast.296, s32[2,128]{1,0:T(2,128)} %copy-done.76, ...), custom_call_target="tpu_custom_call" | custom-call | flops 17179869184 | bytes 8388608 | tf_op jit(solution)/shard_map/pallas_call | solution.py:348
  141.5 12.4 %collective-permute-start.37 = (bf16[4,256,384]{2,1,0:T(8,128)(2,1)}, bf16[4,256,384]{2,1,0:T(8,128)(2,1)}, u32[]{:S(2)}, u32[]{:S(2)}) collective-permute-start(bf16[4,256,384]{2,1,0:T(8,128)(2,1)} %get-tuple-element.20), channel_id=1, source_target_pairs={{0,4},{4,0},{8,12},{12,8},{16,20},{20,16},{24,28},{28,24},{1,5},{5... | collective-permute-start | bytes 2359304 | tf_op jit(solution)/shard_map/ppermute | solution.py:80
  154.0 2.1 copy.110
  156.1 2.0 multiply_add_fusion.1
  158.1 2.9 convolution_convert_fusion
  161.0 3.9 %copy.123 = bf16[1536,576]{1,0:T(8,128)(2,1)} copy(bf16[1536,576]{0,1:T(8,128)(2,1)} %convolution_convert_fusion) | data formatting | bytes 3538944 | tf_op jit(solution)/shard_map/convert_element_type | solution.py:534
  173.6 1.9 collective-permute-start.40
  179.3 1.8 collective-permute-start.72
  183.6 3.0 collective-permute-done.39
  196.5 1.8 copy.113
  198.3 4.1 %concatenate.69 = bf16[576,1536]{1,0:T(8,128)(2,1)} concatenate(bf16[576,576]{1,0:T(8,128)(2,1)} %convolution_convert_fusion.3, bf16[576,192]{1,0:T(8,128)(2,1)} %copy.112, bf16[576,192]{1,0:T(8,128)(2,1)} %copy.113, bf16[576,576]{1,0:T(8,128)(2,1)} %convolution_convert_fusion.2), dimensions={1} | concatenate | bytes 3538944 | tf_op jit(solution)/shard_map/concatenate | solution.py:599
  208.5 2.8 collective-permute-start.74
  212.8 2.3 collective-permute-done.75
  220.3 2.0 collective-permute-start.44
  223.8 3.4 %add_convert_fusion = bf16[576,1536]{1,0:T(8,128)(2,1)} fusion(bf16[576,1536]{1,0:T(8,128)(2,1)} %collective-permute-done.55, bf16[256,576]{0,1:T(8,128)(2,1)S(1)} %multiply_convert_fusion.3, bf16[256,1536]{1,0:T(8,128)(2,1)S(1)} %copy-done.6, bf16[256,1536]{1,0:T(8,128)(2,1)S(1)} %copy-done.8, pred[]{:T(512)S(6)} %eq.4), kind=kOutput, calls=%fused_computation.1 | convolution fusion | flops 456032256 | bytes 5406721 | tf_op jit(solution)/shard_map/dot_general | solution.py:60
  227.2 3.2 %reshape.558 = bf16[576,4,384]{2,1,0:T(4,128)(2,1)S(1)} reshape(bf16[576,1536]{1,0:T(8,128)(2,1)} %add_convert_fusion) | data formatting | bytes 3538944 | tf_op jit(solution)/shard_map/reshape | solution.py:524
  230.4 2.0 collective-permute-start.78
  233.7 2.3 collective-permute-start.47
  236.0 2.1 collective-permute-start.45
  238.2 4.6 %constant_dynamic-slice_fusion.5 = (bf16[576,1,384]{2,1,0:T(2,128)(2,1)}, bf16[576,1,384]{2,1,0:T(2,128)(2,1)S(1)}, bf16[576,1,384]{2,1,0:T(2,128)(2,1)S(1)}, bf16[576,1,384]{2,1,0:T(2,128)(2,1)S(1)}) fusion(bf16[576,4,384]{2,1,0:T(4,128)(2,1)S(1)} %reshape.558, s32[]{:T(128)S(6)} %select_n.294, s32[]{:T(128)S(6)} %select_n.296, s32[]{:T(128)S(6)} %select_n.295, ...), kind=kLoop, calls=%fused_computation.192 | loop fusion | bytes 3538960 | tf_op jit(solution)/shard_map/dynamic-slice.2
  252.4 1.9 shard_map.220
  255.4 14.6 %collective-permute-done.48.refs_1_ = bf16[72,384]{1,0:T(8,128)(2,1)S(1)} collective-permute-done((bf16[72,384]{1,0:T(8,128)(2,1)S(1)}, bf16[72,384]{1,0:T(8,128)(2,1)S(1)}, u32[]{:S(2)}, u32[]{:S(2)}) %collective-permute-start.48) | collective-permute-done | bytes 55328 | tf_op jit(solution)/shard_map/ppermute | solution.py:80
  277.1 2.0 collective-permute-start.61
  279.2 2.4 collective-permute-start.59
  282.8 1.8 shard_map.218
  293.1 1.8 collective-permute-done.62.refs_1_
  294.9 2.4 collective-permute-done.63.refs_2_
  299.9 2.2 shard_map.219
  (420 shorter events, 123.0 us)
Async XLA Ops:
  2.9 20.1 %collective-permute-start = (bf16[73,384]{1,0:T(8,128)(2,1)S(1)}, bf16[73,384]{1,0:T(8,128)(2,1)S(1)}, u32[]{:S(2)}, u32[]{:S(2)}) collective-permute-start(bf16[73,384]{1,0:T(8,128)(2,1)S(1)} %pad_maximum_fusion.7), channel_id=1, source_target_pairs={{0,3},{1,2},{2,1},{3,0},{4,7},{5,6},{6,5},{7,4},{8,11},{9,10},{10,... | collective-permute-start | bytes 168200 | tf_op jit(solution)/shard_map/ppermute | solution.py:80
  8.0 16.6 %collective-permute-start.1 = (bf16[73,384]{1,0:T(8,128)(2,1)S(1)}, bf16[73,384]{1,0:T(8,128)(2,1)S(1)}, u32[]{:S(2)}, u32[]{:S(2)}) collective-permute-start(bf16[73,384]{1,0:T(8,128)(2,1)S(1)} %pad_maximum_fusion.7), channel_id=1, source_target_pairs={{0,2},{1,3},{2,0},{3,1},{4,6},{5,7},{6,4},{7,5},{8,10},{9,11},{10,... | collective-permute-start | bytes 168200 | tf_op jit(solution)/shard_map/ppermute | solution.py:80
  8.2 11.1 %collective-permute-start.27 = (bf16[48,576]{1,0:T(8,128)(2,1)S(1)}, bf16[48,576]{1,0:T(8,128)(2,1)S(1)}, u32[]{:S(2)}, u32[]{:S(2)}) collective-permute-start(bf16[48,576]{1,0:T(8,128)(2,1)S(1)} %copy.129), channel_id=1, source_target_pairs={{0,3},{1,2},{2,1},{3,0},{4,7},{5,6},{6,5},{7,4},{8,11},{9,10},{10,... | collective-permute-start | bytes 165896 | tf_op jit(solution)/shard_map/ppermute | solution.py:80
  10.2 9.8 %collective-permute-start.28 = (bf16[48,576]{1,0:T(8,128)(2,1)S(1)}, bf16[48,576]{1,0:T(8,128)(2,1)S(1)}, u32[]{:S(2)}, u32[]{:S(2)}) collective-permute-start(bf16[48,576]{1,0:T(8,128)(2,1)S(1)} %copy.129), channel_id=1, source_target_pairs={{0,2},{1,3},{2,0},{3,1},{4,6},{5,7},{6,4},{7,5},{8,10},{9,11},{10,... | collective-permute-start | bytes 165896 | tf_op jit(solution)/shard_map/ppermute | solution.py:80
  11.3 11.6 %collective-permute-start.29 = (bf16[48,576]{1,0:T(8,128)(2,1)S(1)}, bf16[48,576]{1,0:T(8,128)(2,1)S(1)}, u32[]{:S(2)}, u32[]{:S(2)}) collective-permute-start(bf16[48,576]{1,0:T(8,128)(2,1)S(1)} %copy.129), channel_id=1, source_target_pairs={{0,1},{1,0},{2,3},{3,2},{4,5},{5,4},{6,7},{7,6},{8,9},{9,8},{10,11... | collective-permute-start | bytes 165896 | tf_op jit(solution)/shard_map/ppermute | solution.py:80
  23.0 15.2 %collective-permute-start.30 = (bf16[4,48,576]{2,1,0:T(8,128)(2,1)S(1)}, bf16[4,48,576]{2,1,0:T(8,128)(2,1)S(1)}, u32[]{:S(2)}, u32[]{:S(2)}) collective-permute-start(bf16[4,48,576]{2,1,0:T(8,128)(2,1)S(1)} %pad_maximum_fusion.1.refs_0_), channel_id=1, source_target_pairs={{0,8},{4,12},{8,0},{12,4},{16,24},{20,28},{24,16},{28,20},{1,9},{5... | collective-permute-start | bytes 663560 | tf_op jit(solution)/shard_map/ppermute | solution.py:80
  24.5 15.2 %collective-permute-start.31 = (bf16[4,48,576]{2,1,0:T(8,128)(2,1)S(1)}, bf16[4,48,576]{2,1,0:T(8,128)(2,1)S(1)}, u32[]{:S(2)}, u32[]{:S(2)}) collective-permute-start(bf16[4,48,576]{2,1,0:T(8,128)(2,1)S(1)} %pad_maximum_fusion.1.refs_0_), channel_id=1, source_target_pairs={{0,16},{4,20},{8,24},{12,28},{16,0},{20,4},{24,8},{28,12},{1,17},{... | collective-permute-start | bytes 663560 | tf_op jit(solution)/shard_map/ppermute | solution.py:80
  26.1 14.2 %collective-permute-start.32 = (bf16[4,48,576]{2,1,0:T(8,128)(2,1)S(1)}, bf16[4,48,576]{2,1,0:T(8,128)(2,1)S(1)}, u32[]{:S(2)}, u32[]{:S(2)}) collective-permute-start(bf16[4,48,576]{2,1,0:T(8,128)(2,1)S(1)} %pad_maximum_fusion.1.refs_0_), channel_id=1, source_target_pairs={{0,24},{4,28},{8,16},{12,20},{16,8},{20,12},{24,0},{28,4},{1,25},{... | collective-permute-start | bytes 663560 | tf_op jit(solution)/shard_map/ppermute | solution.py:80
  27.3 13.0 %collective-permute-start.33 = (bf16[4,48,576]{2,1,0:T(8,128)(2,1)S(1)}, bf16[4,48,576]{2,1,0:T(8,128)(2,1)S(1)}, u32[]{:S(2)}, u32[]{:S(2)}) collective-permute-start(bf16[4,48,576]{2,1,0:T(8,128)(2,1)S(1)} %pad_maximum_fusion.1.refs_0_), channel_id=1, source_target_pairs={{0,4},{4,0},{8,12},{12,8},{16,20},{20,16},{24,28},{28,24},{1,5},{5... | collective-permute-start | bytes 663560 | tf_op jit(solution)/shard_map/ppermute | solution.py:80
  38.2 9.7 %collective-permute-start.4 = (bf16[4,72,384]{2,1,0:T(8,128)(2,1)S(1)}, bf16[4,72,384]{2,1,0:T(8,128)(2,1)}, u32[]{:S(2)}, u32[]{:S(2)}) collective-permute-start(bf16[4,72,384]{2,1,0:T(8,128)(2,1)S(1)} %pad_maximum_fusion.2.refs_0_), channel_id=1, source_target_pairs={{0,16},{4,20},{8,24},{12,28},{16,0},{20,4},{24,8},{28,12},{1,17},{... | collective-permute-start | bytes 663560 | tf_op jit(solution)/shard_map/ppermute | solution.py:80
  44.3 10.3 %collective-permute-start.6 = (bf16[4,72,384]{2,1,0:T(8,128)(2,1)S(1)}, bf16[4,72,384]{2,1,0:T(8,128)(2,1)S(1)}, u32[]{:S(2)}, u32[]{:S(2)}) collective-permute-start(bf16[4,72,384]{2,1,0:T(8,128)(2,1)S(1)} %pad_maximum_fusion.2.refs_0_), channel_id=1, source_target_pairs={{0,4},{4,0},{8,12},{12,8},{16,20},{20,16},{24,28},{28,24},{1,5},{5... | collective-permute-start | bytes 663560 | tf_op jit(solution)/shard_map/ppermute | solution.py:80
  48.4 9.1 %collective-permute-start.8 = (bf16[4,72,384]{2,1,0:T(8,128)(2,1)}, bf16[4,72,384]{2,1,0:T(8,128)(2,1)S(1)}, u32[]{:S(2)}, u32[]{:S(2)}) collective-permute-start(bf16[4,72,384]{2,1,0:T(8,128)(2,1)} %collective-permute-done.4.refs_2_), channel_id=1, source_target_pairs={{0,4},{4,0},{8,12},{12,8},{16,20},{20,16},{24,28},{28,24},{1,5},{5... | collective-permute-start | bytes 663560 | tf_op jit(solution)/shard_map/ppermute | solution.py:80
  50.8 20.8 %collective-permute-start.20 = (bf16[4,144,384]{2,1,0:T(8,128)(2,1)}, bf16[4,144,384]{2,1,0:T(8,128)(2,1)}, u32[]{:S(2)}, u32[]{:S(2)}) collective-permute-start(bf16[4,144,384]{2,1,0:T(8,128)(2,1)} %pad_maximum_fusion.refs_0_), channel_id=1, source_target_pairs={{0,8},{4,12},{8,0},{12,4},{16,24},{20,28},{24,16},{28,20},{1,9},{5... | collective-permute-start | bytes 1327112 | tf_op jit(solution)/shard_map/ppermute | solution.py:80
  54.6 23.4 %collective-permute-start.21 = (bf16[4,144,384]{2,1,0:T(8,128)(2,1)}, bf16[4,144,384]{2,1,0:T(8,128)(2,1)}, u32[]{:S(2)}, u32[]{:S(2)}) collective-permute-start(bf16[4,144,384]{2,1,0:T(8,128)(2,1)} %pad_maximum_fusion.refs_0_), channel_id=1, source_target_pairs={{0,16},{4,20},{8,24},{12,28},{16,0},{20,4},{24,8},{28,12},{1,17},{... | collective-permute-start | bytes 1327112 | tf_op jit(solution)/shard_map/ppermute | solution.py:80
  56.1 30.6 %collective-permute-start.22 = (bf16[4,144,384]{2,1,0:T(8,128)(2,1)}, bf16[4,144,384]{2,1,0:T(8,128)(2,1)}, u32[]{:S(2)}, u32[]{:S(2)}) collective-permute-start(bf16[4,144,384]{2,1,0:T(8,128)(2,1)} %pad_maximum_fusion.refs_0_), channel_id=1, source_target_pairs={{0,24},{4,28},{8,16},{12,20},{16,8},{20,12},{24,0},{28,4},{1,25},{... | collective-permute-start | bytes 1327112 | tf_op jit(solution)/shard_map/ppermute | solution.py:80
  67.1 11.0 %collective-permute-start.10 = (bf16[256,384]{1,0:T(8,128)(2,1)}, bf16[256,384]{1,0:T(8,128)(2,1)}, u32[]{:S(2)}, u32[]{:S(2)}) collective-permute-start(bf16[256,384]{1,0:T(8,128)(2,1)} %pad_maximum_fusion.5.refs_1_), channel_id=1, source_target_pairs={{0,8},{4,12},{8,0},{12,4},{16,24},{20,28},{24,16},{28,20},{1,9},{5... | collective-permute-start | bytes 589832 | tf_op jit(solution)/shard_map/ppermute | solution.py:80
  67.8 17.4 %collective-permute-start.11 = (bf16[256,384]{1,0:T(8,128)(2,1)}, bf16[256,384]{1,0:T(8,128)(2,1)}, u32[]{:S(2)}, u32[]{:S(2)}) collective-permute-start(bf16[256,384]{1,0:T(8,128)(2,1)} %pad_maximum_fusion.5.refs_1_), channel_id=1, source_target_pairs={{0,16},{4,20},{8,24},{12,28},{16,0},{20,4},{24,8},{28,12},{1,17},{... | collective-permute-start | bytes 589832 | tf_op jit(solution)/shard_map/ppermute | solution.py:80
  71.5 13.6 %collective-permute-start.12 = (bf16[256,384]{1,0:T(8,128)(2,1)}, bf16[256,384]{1,0:T(8,128)(2,1)}, u32[]{:S(2)}, u32[]{:S(2)}) collective-permute-start(bf16[256,384]{1,0:T(8,128)(2,1)} %pad_maximum_fusion.5.refs_1_), channel_id=1, source_target_pairs={{0,24},{4,28},{8,16},{12,20},{16,8},{20,12},{24,0},{28,4},{1,25},{... | collective-permute-start | bytes 589832 | tf_op jit(solution)/shard_map/ppermute | solution.py:80
  78.0 9.2 %collective-permute-start.14 = (bf16[256,384]{1,0:T(8,128)(2,1)}, bf16[256,384]{1,0:T(8,128)(2,1)}, u32[]{:S(2)}, u32[]{:S(2)}) collective-permute-start(bf16[256,384]{1,0:T(8,128)(2,1)} %collective-permute-done.10.refs_2_), channel_id=1, source_target_pairs={{0,4},{4,0},{8,12},{12,8},{16,20},{20,16},{24,28},{28,24},{1,5},{5... | collective-permute-start | bytes 589832 | tf_op jit(solution)/shard_map/ppermute | solution.py:80
  86.7 12.3 %collective-permute-start.23 = (bf16[4,144,384]{2,1,0:T(8,128)(2,1)}, bf16[4,144,384]{2,1,0:T(8,128)(2,1)S(1)}, u32[]{:S(2)}, u32[]{:S(2)}) collective-permute-start(bf16[4,144,384]{2,1,0:T(8,128)(2,1)} %pad_maximum_fusion.refs_0_), channel_id=1, source_target_pairs={{0,4},{4,0},{8,12},{12,8},{16,20},{20,16},{24,28},{28,24},{1,5},{5... | collective-permute-start | bytes 1327112 | tf_op jit(solution)/shard_map/ppermute | solution.py:80
  86.7 12.3 %collective-permute-start.24 = (bf16[4,144,384]{2,1,0:T(8,128)(2,1)}, bf16[4,144,384]{2,1,0:T(8,128)(2,1)S(1)}, u32[]{:S(2)}, u32[]{:S(2)}) collective-permute-start(bf16[4,144,384]{2,1,0:T(8,128)(2,1)} %collective-permute-done.20.refs_1_), channel_id=1, source_target_pairs={{0,4},{4,0},{8,12},{12,8},{16,20},{20,16},{24,28},{28,24},{1,5},{5... | collective-permute-start | bytes 1327112 | tf_op jit(solution)/shard_map/ppermute | solution.py:80
  87.2 11.8 %collective-permute-start.25 = (bf16[4,144,384]{2,1,0:T(8,128)(2,1)}, bf16[4,144,384]{2,1,0:T(8,128)(2,1)S(1)}, u32[]{:S(2)}, u32[]{:S(2)}) collective-permute-start(bf16[4,144,384]{2,1,0:T(8,128)(2,1)} %collective-permute-done.21.refs_2_), channel_id=1, source_target_pairs={{0,4},{4,0},{8,12},{12,8},{16,20},{20,16},{24,28},{28,24},{1,5},{5... | collective-permute-start | bytes 1327112 | tf_op jit(solution)/shard_map/ppermute | solution.py:80
  87.3 11.8 %collective-permute-start.26 = (bf16[4,144,384]{2,1,0:T(8,128)(2,1)}, bf16[4,144,384]{2,1,0:T(8,128)(2,1)S(1)}, u32[]{:S(2)}, u32[]{:S(2)}) collective-permute-start(bf16[4,144,384]{2,1,0:T(8,128)(2,1)} %collective-permute-done.22.refs_3_), channel_id=1, source_target_pairs={{0,4},{4,0},{8,12},{12,8},{16,20},{20,16},{24,28},{28,24},{1,5},{5... | collective-permute-start | bytes 1327112 | tf_op jit(solution)/shard_map/ppermute | solution.py:80
  141.5 30.6 %collective-permute-start.37 = (bf16[4,256,384]{2,1,0:T(8,128)(2,1)}, bf16[4,256,384]{2,1,0:T(8,128)(2,1)}, u32[]{:S(2)}, u32[]{:S(2)}) collective-permute-start(bf16[4,256,384]{2,1,0:T(8,128)(2,1)} %get-tuple-element.20), channel_id=1, source_target_pairs={{0,4},{4,0},{8,12},{12,8},{16,20},{20,16},{24,28},{28,24},{1,5},{5... | collective-permute-start | bytes 2359304 | tf_op jit(solution)/shard_map/ppermute | solution.py:80
  158.1 65.4 %collective-permute-start.55 = (bf16[576,1536]{1,0:T(8,128)(2,1)}, bf16[576,1536]{1,0:T(8,128)(2,1)}, u32[]{:S(2)}, u32[]{:S(2)}) collective-permute-start(bf16[576,1536]{1,0:T(8,128)(2,1)} %convolution_convert_fusion.1), channel_id=1, source_target_pairs={{0,4},{4,0},{8,12},{12,8},{16,20},{20,16},{24,28},{28,24},{1,5},{5... | collective-permute-start | bytes 5308424 | tf_op jit(solution)/shard_map/ppermute | solution.py:80
  166.7 10.4 %collective-permute-start.69 = (bf16[4,4,48,576]{3,2,0,1:T(8,128)(2,1)S(1)}, bf16[4,4,48,576]{3,2,0,1:T(8,128)(2,1)S(1)}, u32[]{:S(2)}, u32[]{:S(2)}) collective-permute-start(bf16[4,4,48,576]{3,2,0,1:T(8,128)(2,1)S(1)} %bitcast.298), channel_id=1, source_target_pairs={{0,4},{4,0},{8,12},{12,8},{16,20},{20,16},{24,28},{28,24},{1,5},{5... | collective-permute-start | bytes 2654216 | tf_op jit(solution)/shard_map/ppermute | solution.py:80
  175.5 11.0 %collective-permute-start.39 = (bf16[256,384]{1,0:T(8,128)(2,1)S(1)}, bf16[256,384]{1,0:T(8,128)(2,1)S(1)}, u32[]{:S(2)}, u32[]{:S(2)}) collective-permute-start(bf16[256,384]{1,0:T(8,128)(2,1)S(1)} %get-tuple-element.90), channel_id=1, source_target_pairs={{0,16},{4,20},{8,24},{12,28},{16,0},{20,4},{24,8},{28,12},{1,17},{... | collective-permute-start | bytes 589832 | tf_op jit(solution)/shard_map/ppermute | solution.py:80
  176.5 11.5 %collective-permute-start.38 = (bf16[256,384]{1,0:T(8,128)(2,1)S(1)}, bf16[256,384]{1,0:T(8,128)(2,1)S(1)}, u32[]{:S(2)}, u32[]{:S(2)}) collective-permute-start(bf16[256,384]{1,0:T(8,128)(2,1)S(1)} %get-tuple-element.88), channel_id=1, source_target_pairs={{0,8},{4,12},{8,0},{12,4},{16,24},{20,28},{24,16},{28,20},{1,9},{5... | collective-permute-start | bytes 589832 | tf_op jit(solution)/shard_map/ppermute | solution.py:80
  179.3 27.6 %collective-permute-start.72 = (bf16[4,48,576]{2,1,0:T(8,128)(2,1)}, bf16[4,48,576]{2,1,0:T(8,128)(2,1)}, u32[]{:S(2)}, u32[]{:S(2)}) collective-permute-start(bf16[4,48,576]{2,1,0:T(8,128)(2,1)} %get-tuple-element.79), channel_id=1, source_target_pairs={{0,24},{4,28},{8,16},{12,20},{16,8},{20,12},{24,0},{28,4},{1,25},{... | collective-permute-start | bytes 663560 | tf_op jit(solution)/shard_map/ppermute | solution.py:80
  182.3 24.6 %collective-permute-start.71 = (bf16[4,48,576]{2,1,0:T(8,128)(2,1)}, bf16[4,48,576]{2,1,0:T(8,128)(2,1)}, u32[]{:S(2)}, u32[]{:S(2)}) collective-permute-start(bf16[4,48,576]{2,1,0:T(8,128)(2,1)} %get-tuple-element.80), channel_id=1, source_target_pairs={{0,16},{4,20},{8,24},{12,28},{16,0},{20,4},{24,8},{28,12},{1,17},{... | collective-permute-start | bytes 663560 | tf_op jit(solution)/shard_map/ppermute | solution.py:80
  186.6 20.3 %collective-permute-start.70 = (bf16[4,48,576]{2,1,0:T(8,128)(2,1)}, bf16[4,48,576]{2,1,0:T(8,128)(2,1)}, u32[]{:S(2)}, u32[]{:S(2)}) collective-permute-start(bf16[4,48,576]{2,1,0:T(8,128)(2,1)} %get-tuple-element.78), channel_id=1, source_target_pairs={{0,8},{4,12},{8,0},{12,4},{16,24},{20,28},{24,16},{28,20},{1,9},{5... | collective-permute-start | bytes 663560 | tf_op jit(solution)/shard_map/ppermute | solution.py:80
  204.3 14.0 %collective-permute-start.41 = (bf16[4,4,72,384]{3,2,1,0:T(8,128)(2,1)S(1)}, bf16[4,4,72,384]{3,2,1,0:T(8,128)(2,1)S(1)}, u32[]{:S(2)}, u32[]{:S(2)}) collective-permute-start(bf16[4,4,72,384]{3,2,1,0:T(8,128)(2,1)S(1)} %dynamic-slice_bitcast_fusion), channel_id=1, source_target_pairs={{0,4},{4,0},{8,12},{12,8},{16,20},{20,16},{24,28},{28,24},{1,5},{5... | collective-permute-start | bytes 2654216 | tf_op jit(solution)/shard_map/ppermute | solution.py:80
  216.7 19.3 %collective-permute-start.76 = (bf16[48,576]{1,0:T(8,128)(2,1)S(1)}, bf16[48,576]{1,0:T(8,128)(2,1)}, u32[]{:S(2)}, u32[]{:S(2)}) collective-permute-start(bf16[48,576]{1,0:T(8,128)(2,1)S(1)} %fusion.67.refs_0_), channel_id=1, source_target_pairs={{0,8},{4,12},{8,0},{12,4},{16,24},{20,28},{24,16},{28,20},{1,9},{5... | collective-permute-start | bytes 165896 | tf_op jit(solution)/shard_map/ppermute | solution.py:80
  217.6 27.6 %collective-permute-start.77 = (bf16[48,576]{1,0:T(8,128)(2,1)S(1)}, bf16[48,576]{1,0:T(8,128)(2,1)}, u32[]{:S(2)}, u32[]{:S(2)}) collective-permute-start(bf16[48,576]{1,0:T(8,128)(2,1)S(1)} %fusion.67.refs_0_), channel_id=1, source_target_pairs={{0,16},{4,20},{8,24},{12,28},{16,0},{20,4},{24,8},{28,12},{1,17},{... | collective-permute-start | bytes 165896 | tf_op jit(solution)/shard_map/ppermute | solution.py:80
  220.3 10.0 %collective-permute-start.44 = (bf16[4,72,384]{2,1,0:T(8,128)(2,1)}, bf16[4,72,384]{2,1,0:T(8,128)(2,1)S(1)}, u32[]{:S(2)}, u32[]{:S(2)}) collective-permute-start(bf16[4,72,384]{2,1,0:T(8,128)(2,1)} %get-tuple-element.86), channel_id=1, source_target_pairs={{0,24},{4,28},{8,16},{12,20},{16,8},{20,12},{24,0},{28,4},{1,25},{... | collective-permute-start | bytes 663560 | tf_op jit(solution)/shard_map/ppermute | solution.py:80
  222.3 10.1 %collective-permute-start.43 = (bf16[4,72,384]{2,1,0:T(8,128)(2,1)}, bf16[4,72,384]{2,1,0:T(8,128)(2,1)}, u32[]{:S(2)}, u32[]{:S(2)}) collective-permute-start(bf16[4,72,384]{2,1,0:T(8,128)(2,1)} %get-tuple-element.87), channel_id=1, source_target_pairs={{0,16},{4,20},{8,24},{12,28},{16,0},{20,4},{24,8},{28,12},{1,17},{... | collective-permute-start | bytes 663560 | tf_op jit(solution)/shard_map/ppermute | solution.py:80
  230.4 14.9 %collective-permute-start.78 = (bf16[48,576]{1,0:T(8,128)(2,1)S(1)}, bf16[48,576]{1,0:T(8,128)(2,1)S(1)}, u32[]{:S(2)}, u32[]{:S(2)}) collective-permute-start(bf16[48,576]{1,0:T(8,128)(2,1)S(1)} %fusion.67.refs_0_), channel_id=1, source_target_pairs={{0,24},{4,28},{8,16},{12,20},{16,8},{20,12},{24,0},{28,4},{1,25},{... | collective-permute-start | bytes 165896 | tf_op jit(solution)/shard_map/ppermute | solution.py:80
  233.7 12.1 %collective-permute-start.47 = (bf16[72,384]{1,0:T(8,128)(2,1)S(1)}, bf16[72,384]{1,0:T(8,128)(2,1)S(1)}, u32[]{:S(2)}, u32[]{:S(2)}) collective-permute-start(bf16[72,384]{1,0:T(8,128)(2,1)S(1)} %get-tuple-element.118), channel_id=1, source_target_pairs={{0,3},{1,2},{2,1},{3,0},{4,7},{5,6},{6,5},{7,4},{8,11},{9,10},{10,... | collective-permute-start | bytes 165896 | tf_op jit(solution)/shard_map/ppermute | solution.py:80
  236.0 9.9 %collective-permute-start.46 = (bf16[72,384]{1,0:T(8,128)(2,1)S(1)}, bf16[72,384]{1,0:T(8,128)(2,1)S(1)}, u32[]{:S(2)}, u32[]{:S(2)}) collective-permute-start(bf16[72,384]{1,0:T(8,128)(2,1)S(1)} %get-tuple-element.119), channel_id=1, source_target_pairs={{0,2},{1,3},{2,0},{3,1},{4,6},{5,7},{6,4},{7,5},{8,10},{9,11},{10,... | collective-permute-start | bytes 165896 | tf_op jit(solution)/shard_map/ppermute | solution.py:80
  236.0 10.3 %collective-permute-start.45 = (bf16[72,384]{1,0:T(8,128)(2,1)S(1)}, bf16[72,384]{1,0:T(8,128)(2,1)S(1)}, u32[]{:S(2)}, u32[]{:S(2)}) collective-permute-start(bf16[72,384]{1,0:T(8,128)(2,1)S(1)} %get-tuple-element.117), channel_id=1, source_target_pairs={{0,1},{1,0},{2,3},{3,2},{4,5},{5,4},{6,7},{7,6},{8,9},{9,8},{10,11... | collective-permute-start | bytes 165896 | tf_op jit(solution)/shard_map/ppermute | solution.py:80
  246.3 28.8 %collective-permute-start.58 = (bf16[576,384]{1,0:T(8,128)(2,1)}, bf16[576,384]{1,0:T(8,128)(2,1)}, u32[]{:S(2)}, u32[]{:S(2)}) collective-permute-start(bf16[576,384]{1,0:T(8,128)(2,1)} %bitcast.252), channel_id=1, source_target_pairs={{0,24},{4,28},{8,16},{12,20},{16,8},{20,12},{24,0},{28,4},{1,25},{... | collective-permute-start | bytes 1327112 | tf_op jit(solution)/shard_map/ppermute | solution.py:80
  247.9 27.7 %collective-permute-start.57 = (bf16[576,384]{1,0:T(8,128)(2,1)}, bf16[576,384]{1,0:T(8,128)(2,1)S(1)}, u32[]{:S(2)}, u32[]{:S(2)}) collective-permute-start(bf16[576,384]{1,0:T(8,128)(2,1)} %bitcast.253), channel_id=1, source_target_pairs={{0,16},{4,20},{8,24},{12,28},{16,0},{20,4},{24,8},{28,12},{1,17},{... | collective-permute-start | bytes 1327112 | tf_op jit(solution)/shard_map/ppermute | solution.py:80
  248.9 26.8 %collective-permute-start.56 = (bf16[576,384]{1,0:T(8,128)(2,1)}, bf16[576,384]{1,0:T(8,128)(2,1)}, u32[]{:S(2)}, u32[]{:S(2)}) collective-permute-start(bf16[576,384]{1,0:T(8,128)(2,1)} %bitcast.254), channel_id=1, source_target_pairs={{0,8},{4,12},{8,0},{12,4},{16,24},{20,28},{24,16},{28,20},{1,9},{5... | collective-permute-start | bytes 1327112 | tf_op jit(solution)/shard_map/ppermute | solution.py:80
  250.0 20.1 %collective-permute-start.48 = (bf16[72,384]{1,0:T(8,128)(2,1)S(1)}, bf16[72,384]{1,0:T(8,128)(2,1)S(1)}, u32[]{:S(2)}, u32[]{:S(2)}) collective-permute-start(bf16[72,384]{1,0:T(8,128)(2,1)S(1)} %fusion.70.refs_0_), channel_id=1, source_target_pairs={{0,8},{4,12},{8,0},{12,4},{16,24},{20,28},{24,16},{28,20},{1,9},{5... | collective-permute-start | bytes 165896 | tf_op jit(solution)/shard_map/ppermute | solution.py:80
  254.3 19.3 %collective-permute-start.49 = (bf16[72,384]{1,0:T(8,128)(2,1)S(1)}, bf16[72,384]{1,0:T(8,128)(2,1)S(1)}, u32[]{:S(2)}, u32[]{:S(2)}) collective-permute-start(bf16[72,384]{1,0:T(8,128)(2,1)S(1)} %fusion.70.refs_0_), channel_id=1, source_target_pairs={{0,16},{4,20},{8,24},{12,28},{16,0},{20,4},{24,8},{28,12},{1,17},{... | collective-permute-start | bytes 165896 | tf_op jit(solution)/shard_map/ppermute | solution.py:80
  277.1 10.5 %collective-permute-start.61 = (bf16[144,384]{1,0:T(8,128)(2,1)S(1)}, bf16[144,384]{1,0:T(8,128)(2,1)S(1)}, u32[]{:S(2)}, u32[]{:S(2)}) collective-permute-start(bf16[144,384]{1,0:T(8,128)(2,1)S(1)} %get-tuple-element.96), channel_id=1, source_target_pairs={{0,3},{1,2},{2,1},{3,0},{4,7},{5,6},{6,5},{7,4},{8,11},{9,10},{10,... | collective-permute-start | bytes 331784 | tf_op jit(solution)/shard_map/ppermute | solution.py:80
  279.1 10.0 %collective-permute-start.60 = (bf16[144,384]{1,0:T(8,128)(2,1)S(1)}, bf16[144,384]{1,0:T(8,128)(2,1)S(1)}, u32[]{:S(2)}, u32[]{:S(2)}) collective-permute-start(bf16[144,384]{1,0:T(8,128)(2,1)S(1)} %get-tuple-element.97), channel_id=1, source_target_pairs={{0,2},{1,3},{2,0},{3,1},{4,6},{5,7},{6,4},{7,5},{8,10},{9,11},{10,... | collective-permute-start | bytes 331784 | tf_op jit(solution)/shard_map/ppermute | solution.py:80
  279.2 10.0 %collective-permute-start.59 = (bf16[144,384]{1,0:T(8,128)(2,1)S(1)}, bf16[144,384]{1,0:T(8,128)(2,1)S(1)}, u32[]{:S(2)}, u32[]{:S(2)}) collective-permute-start(bf16[144,384]{1,0:T(8,128)(2,1)S(1)} %get-tuple-element.95), channel_id=1, source_target_pairs={{0,1},{1,0},{2,3},{3,2},{4,5},{5,4},{6,7},{7,6},{8,9},{9,8},{10,11... | collective-permute-start | bytes 331784 | tf_op jit(solution)/shard_map/ppermute | solution.py:80
  (115 other events, 794.2 us)

commit v2 on v1

v2 whole, which is shorter than its diff:
```python
import jax
import jax.numpy as jnp
from jax import lax
from jax.experimental import pallas as pl
from jax.experimental.pallas import tpu as pltpu
from jax.sharding import PartitionSpec as P

D = 576
HEADS = 9
KV_HEADS = 3
HEAD = 64
GROUPS = HEADS // KV_HEADS
KV_WIDTH = KV_HEADS * HEAD
TILE = 128

epsilon = 1e-05
rope_base = 100000.0

VMEM = pl.BlockSpec(memory_space=pltpu.VMEM)
SMEM = pl.BlockSpec(memory_space=pltpu.SMEM)


def run_kernel(kernel, out_shapes, inputs, scalars=0, scratch=(), microseconds=1):
    return pl.pallas_call(
        kernel,
        out_shape=tuple(jax.ShapeDtypeStruct(*out) for out in out_shapes),
        in_specs=[SMEM] * scalars + [VMEM] * (len(inputs) - scalars),
        out_specs=tuple(VMEM for _ in out_shapes),
        scratch_shapes=list(scratch),
        compiler_params=pltpu.CompilerParams(vmem_limit_bytes=60 * 1024 * 1024),
        cost_estimate=pl.CostEstimate(
            flops=microseconds * 1150 * 10**6, bytes_accessed=1024, transcendentals=0
        ),
    )(*inputs)


def rank():
    index = lax.axis_index("ctx")
    return index // 2, index % 2


def swap(value, axis, offset):
    count = lax.axis_size(axis)
    return lax.ppermute(value, axis, [(i, i ^ offset) for i in range(count)])


def chip_swap(value, offset):
    return swap(value, "ctx", 2 * offset)


def core_swap(value):
    return swap(value, "ctx", 1)


def by_owner(pieces, index):
    bit = 1
    while bit < len(pieces):
        flag = (index & bit) != 0
        pieces = [jnp.where(flag, pieces[i ^ bit], pieces[i]) for i in range(len(pieces))]
        bit = bit * 2
    return pieces


def gather_rows(piece, *others):
    count = lax.axis_size("fsdp")
    index = lax.axis_index("fsdp")
    values = piece[None]
    offset = 1
    while offset < count:
        if offset > 1 and others:
            values = after(values, *others)
        other = swap(values, "fsdp", offset)
        flag = (index & offset) != 0
        values = jnp.concatenate(
            [jnp.where(flag, other, values), jnp.where(flag, values, other)], axis=0
        )
        offset = offset * 2
    return values


def gather_half(piece, *others):
    half = lax.axis_size("fsdp") // 2
    index = lax.axis_index("fsdp")
    received = lax.ppermute(piece, ("ctx", "fsdp"), half_pairs())
    values = after(jnp.where(in_half(), piece, received)[None], *others)
    offset = 1
    while offset < half:
        other = swap(values, "fsdp", offset)
        flag = (index & offset) != 0
        values = jnp.concatenate(
            [jnp.where(flag, other, values), jnp.where(flag, values, other)], axis=0
        )
        offset = offset * 2
    return values


def gather_same_core(piece):
    return [piece] + [chip_swap(piece, i) for i in range(1, lax.axis_size("ctx") // 2)]


def gather_chips(piece):
    own = gather_same_core(piece)
    return own + [core_swap(value) for value in own]


def after(value, *others):
    return lax.optimization_barrier((value, others))[0]


def in_rank_order(pieces):
    chip, core = rank()
    chips = len(pieces) // 2
    own, other = by_owner(pieces[:chips], chip), by_owner(pieces[chips:], chip)
    ordered = [by_owner(list(pair), core) for pair in zip(own, other)]
    return [value for pair in ordered for value in pair]


def sum_cores(kept, sent):
    return (kept.astype(jnp.float32) + core_swap(sent).astype(jnp.float32)).astype(jnp.bfloat16)


def sum_chips(sums, *others):
    received = tuple(chip_swap(sums[i], i) for i in range(1, len(sums)))
    if others:
        received = after(received, *others)
    return sum((value.astype(jnp.float32) for value in received), sums[0].astype(jnp.float32))


def half_pairs():
    count = lax.axis_size("fsdp")
    half = count // 2
    return [
        (c * count + z, c * count + (z ^ half))
        for c in range(lax.axis_size("ctx"))
        for z in range(count)
        if z // half == c % 2
    ]


def in_half():
    half = lax.axis_size("fsdp") // 2
    return lax.axis_index("fsdp") // half == lax.axis_index("ctx") % 2


def sum_rows(values):
    count = lax.axis_size("fsdp")
    index = lax.axis_index("fsdp")

    def pick(offset):
        return lax.dynamic_index_in_dim(values, index ^ offset, 0, keepdims=False)

    total = pick(0).astype(jnp.float32)
    for i in range(1, count):
        total = total + swap(pick(i), "fsdp", i).astype(jnp.float32)
    return total


def first_piece(mixed, c, count):
    width = mixed.shape[1] // count
    return lax.dynamic_slice_in_dim(mixed, c * width, width, 1)


def wide_piece(gate, up, chip, core, chips):
    lanes = gate.shape[1] // chips
    q = chip % (chips // 2)
    wide = jnp.where(chip < chips // 2, gate, up)
    return lax.dynamic_slice_in_dim(wide, (core * (chips // 2) + q) * lanes, lanes, 1)


def stack_down(part, pile):
    width = D // pile
    return jnp.concatenate([part[:, n * width : (n + 1) * width] for n in range(pile)], axis=0)


def unstack_down(part, pile):
    rows = part.shape[0] // pile
    return jnp.concatenate([part[n * rows : (n + 1) * rows] for n in range(pile)], axis=1)


def by_core_slices(values):
    _, core = rank()
    values = values.reshape(-1, 2, *values.shape[1:])
    mine, theirs = (
        lax.dynamic_index_in_dim(values, side, 1, keepdims=False) for side in (core, 1 - core)
    )
    return jnp.concatenate(both_cores(mine, core_swap(theirs), core))


def both_cores(own, other, core):
    return jnp.where(core == 0, own, other), jnp.where(core == 0, other, own)


def gain_gradient(terms, gain_row):
    total = sum(terms[:, t : t + TILE] for t in range(0, terms.shape[1], TILE))
    return jnp.sum(total.T, axis=0, keepdims=True) / gain_row


def finish_first(pieces, shard, gain):
    count = len(pieces)
    chips = count // 2
    rows = shard.shape[0]
    used = 2 * KV_WIDTH + D

    def kernel(*refs):
        shard_ref, gain_ref = refs[count : count + 2]
        query, key, value, out, gain_grad, whole = refs[count + 2 :]
        chip, core = rank()
        for n in range(count):
            c = (chip ^ (n % chips)) * 2 + (core ^ (n // chips))
            whole[:, pl.ds(pl.multiple_of(c * TILE, TILE), TILE)] = refs[n][:rows, :].astype(
                jnp.float32
            )
        key[...] = whole[:, :KV_WIDTH]
        value[...] = whole[:, KV_WIDTH : 2 * KV_WIDTH]
        query[...] = whole[:, 2 * KV_WIDTH : used]
        for n in range(chips):
            columns = pl.ds(pl.multiple_of((chip ^ n) * TILE, TILE), TILE)
            pair = both_cores(
                refs[n][rows:, :].astype(jnp.float32),
                refs[n + chips][rows:, :].astype(jnp.float32),
                core,
            )
            for m in range(2):
                out[m * (rows // 2) : (m + 1) * (rows // 2), columns] = jnp.concatenate(
                    [part[:, m * (TILE // 2) : (m + 1) * (TILE // 2)] for part in pair], axis=1
                )
        out[:, chips * TILE :] = whole[:, used:]
        gain_grad[...] = gain_gradient(whole[...] * shard_ref[...].astype(jnp.float32), gain_ref[...])

    return run_kernel(
        kernel,
        [
            ((rows, D), jnp.float32),
            ((rows, KV_WIDTH), jnp.float32),
            ((rows, KV_WIDTH), jnp.float32),
            ((rows, D), jnp.float32),
            ((1, rows), jnp.float32),
        ],
        [*pieces, shard, gain],
        scratch=[pltpu.VMEM((rows, count * TILE), jnp.float32)],
    )


def finish_wide(pieces, w_gate, w_up, gain, pile):
    count = len(pieces)
    chips = count // 2
    rows, ff = w_gate.shape
    lanes = ff // chips
    down_rows = rows // pile
    low_lanes = D // pile

    def kernel(*refs):
        gate_ref, up_ref, gain_ref = refs[count : count + 3]
        gate, up, down, gain_grad, total = refs[count + 3 :]
        chip, core = rank()
        total[...] = jnp.zeros_like(total)
        for n in range(count):
            to_chip, to_core = chip ^ (n % chips), core ^ (n // chips)
            column = (to_core * (chips // 2) + to_chip % (chips // 2)) * lanes
            columns = pl.ds(pl.multiple_of(column, TILE), lanes)
            for kind, out, weight in ((0, gate, gate_ref), (1, up, up_ref)):

                @pl.when(to_chip // (chips // 2) == kind)
                def _():
                    part = refs[n][:, :lanes].astype(jnp.float32)
                    out[:, columns] = part
                    total[...] += part * weight[:, columns].astype(jnp.float32)

            start = pl.multiple_of((to_chip * 2 + to_core) * down_rows, 16)
            for m in range(pile):
                down[pl.ds(start, down_rows), m * low_lanes : (m + 1) * low_lanes] = refs[n][
                    m * down_rows : (m + 1) * down_rows, lanes:
                ].astype(jnp.float32)
        gain_grad[...] = gain_gradient(total[...], gain_ref[...])

    return run_kernel(
        kernel,
        [
            ((rows, ff), jnp.float32),
            ((rows, ff), jnp.float32),
            ((count * down_rows, D), jnp.float32),
            ((1, rows), jnp.float32),
        ],
        [*pieces, w_gate, w_up, gain],
        scratch=[pltpu.VMEM((rows, lanes), jnp.float32)],
    )


def dot(first_matrix, second_matrix):
    return jnp.dot(first_matrix, second_matrix, preferred_element_type=jnp.float32)


def dot_nt(first_matrix, second_matrix):
    return lax.dot_general(
        first_matrix, second_matrix, (((1,), (1,)), ((), ())), preferred_element_type=jnp.float32
    )


def dot_tn(first_matrix, second_matrix):
    return lax.dot_general(
        first_matrix, second_matrix, (((0,), (0,)), ((), ())), preferred_element_type=jnp.float32
    )


def norm_back(grad_normed, unit_rows, inv_root, gain_vec):
    scaled_grad = grad_normed * gain_vec
    return inv_root * (
        scaled_grad - unit_rows * jnp.mean(scaled_grad * unit_rows, axis=-1, keepdims=True)
    )


def inverse_root(rows):
    return lax.rsqrt(jnp.mean(rows * rows, axis=-1, keepdims=True) + epsilon)


def turn(values, cos_tile, sin_tile):
    lane = lax.broadcasted_iota(jnp.int32, values.shape, 1) % HEAD
    turned = jnp.where(
        lane < HEAD // 2,
        -pltpu.roll(values, TILE - HEAD // 2, 1),
        pltpu.roll(values, HEAD // 2, 1),
    )
    return values * cos_tile + turned * sin_tile


def turn_pairs(values, cos_tile, sin_tile):
    lane = lax.broadcasted_iota(jnp.int32, cos_tile.shape, 1)
    middle = values[:, TILE : 2 * TILE]
    return jnp.concatenate(
        [
            turn(values[:, :TILE], cos_tile, sin_tile),
            jnp.where(lane < HEAD, turn(middle, cos_tile, sin_tile), middle),
            values[:, 2 * TILE :],
        ],
        axis=1,
    )


def normalize(token_pieces, gain):
    row_count = token_pieces[0].shape[0]
    chips = len(token_pieces)

    def kernel(*refs):
        gain_ref, hidden_ref = refs[chips:]
        for n in range(chips):
            tokens = refs[n][...].astype(jnp.float32)
            hidden_ref[n] = ((tokens * inverse_root(tokens)) * gain_ref[...]).astype(jnp.bfloat16)

    return run_kernel(
        kernel, [((chips, row_count, D), jnp.bfloat16)], [*token_pieces, gain], microseconds=3
    )[0]


def project(direct, table, hidden_half, first, cos_all, sin_all):
    chips, row_count, _ = hidden_half.shape
    block_len = row_count // 2
    count = 2 * chips
    columns_all = count * TILE if direct else first[0].shape[1]
    shards = lax.axis_size("fsdp")
    rows = D // shards

    def kernel(table_ref, hidden_ref, cos_ref, sin_ref, *refs):
        first_refs = refs[: len(first)]
        query_ref, pairs_ref = refs[len(first) : len(first) + 2]
        chip, core = rank()
        if direct:
            mixed_ref = refs[-1]
            for n in range(count):
                c = (chip ^ (n % chips)) * 2 + (core ^ (n // chips))
                columns = pl.ds(pl.multiple_of(c * TILE, TILE), TILE)
                for z in range(shards):
                    mixed_ref[z * rows : (z + 1) * rows, columns] = first_refs[n][z, :rows, :]
        else:
            mixed_ref = first_refs[0]
        for n in range(chips):
            hidden = hidden_ref[n]
            pairs = dot(hidden, mixed_ref[:, : 2 * KV_WIDTH])
            block = table_ref[(chip ^ n) * 2 + core]
            queries = dot(hidden, mixed_ref[:, 2 * KV_WIDTH :]) if n == 0 else None
            for part, place in ((0, block), (1, 2 * count - 1 - block)):
                source = pl.ds(pl.multiple_of(place * block_len, block_len), block_len)
                own = slice(part * block_len, (part + 1) * block_len)
                cos_tile, sin_tile = cos_ref[source, :], sin_ref[source, :]
                pairs_ref[n, own, :] = turn_pairs(pairs[own], cos_tile, sin_tile).astype(
                    jnp.bfloat16
                )
                if n == 0:
                    for start in range(0, D, TILE):
                        width = min(TILE, D - start)
                        turned = turn(queries[own, start : start + TILE], cos_tile, sin_tile)
                        query_ref[own, start : start + width] = (
                            (turned * HEAD ** (-0.5)).astype(jnp.bfloat16)[:, :width]
                        )

    outs = [((row_count, D), jnp.bfloat16), ((chips, row_count, 2 * KV_WIDTH), jnp.bfloat16)]
    if direct:
        outs += [((D, columns_all), jnp.bfloat16)]
    result = run_kernel(
        kernel, outs, [table, hidden_half, cos_all, sin_all, *first], scalars=1, microseconds=5
    )
    return result if direct else (*result, first[0])


def natural_order(out, table_ref, halves):
    chip, core = rank()
    chips, row_count, _ = halves[0].shape
    block_len = row_count // 2
    for a in range(2):
        for n in range(chips):
            block = table_ref[(chip ^ n) * 2 + (core ^ a)]
            for part, place in ((0, block), (1, 4 * chips - 1 - block)):
                rows = pl.ds(pl.multiple_of(place * block_len, block_len), block_len)
                out[rows, :] = halves[a][n, part * block_len : (part + 1) * block_len, :]


def heads_to_rows(values, group):
    return jnp.concatenate(
        [
            values[:, (group * GROUPS + i) * HEAD : (group * GROUPS + i + 1) * HEAD]
            for i in range(GROUPS)
        ],
        axis=0,
    )


def attention_forward(bounds, table, query_rot, pair_halves, first_key, last_key):
    row_count = query_rot.shape[0]
    block_len = row_count // 2
    wide = GROUPS * block_len

    def kernel(
        bounds_ref,
        table_ref,
        query_ref,
        own_ref,
        other_ref,
        first_ref,
        last_ref,
        out_ref,
        log_ref,
        pairs_ref,
    ):
        natural_order(pairs_ref, table_ref, (own_ref, other_ref))
        for b in range(2):
            rows = slice(b * block_len, (b + 1) * block_len)
            query_block = query_ref[rows, :]
            queries = [heads_to_rows(query_block, g) for g in range(KV_HEADS)]
            first = jnp.concatenate([first_ref[b : b + 1, :]] * GROUPS, axis=1)
            last = jnp.concatenate([last_ref[b : b + 1, :]] * GROUPS, axis=1)

            def step(j, state):
                start = pl.multiple_of(j * row_count, row_count)
                pos = start + lax.broadcasted_iota(jnp.int32, (row_count, wide), 0)
                visible = (pos >= first) & (pos <= last)
                result = []
                for g in range(KV_HEADS):
                    top, total, acc = state[g]
                    key_piece = pairs_ref[pl.ds(start, row_count), g * HEAD : (g + 1) * HEAD]
                    value_piece = pairs_ref[
                        pl.ds(start, row_count), KV_WIDTH + g * HEAD : KV_WIDTH + (g + 1) * HEAD
                    ]
                    scores = jnp.where(visible, dot_nt(key_piece, queries[g]), -1e30)
                    new_top = jnp.maximum(top, jnp.max(scores, axis=0, keepdims=True))
                    weights = jnp.exp(scores - new_top)
                    rescale = jnp.exp(top - new_top)
                    total = total * rescale + jnp.sum(weights, axis=0, keepdims=True)
                    acc = acc * rescale + dot_tn(value_piece, weights.astype(jnp.bfloat16))
                    result.append((new_top, total, acc))
                return tuple(result)

            state = lax.fori_loop(
                bounds_ref[2 * b],
                bounds_ref[2 * b + 1],
                step,
                tuple(
                    (
                        jnp.full((1, wide), -1e30, jnp.float32),
                        jnp.zeros((1, wide), jnp.float32),
                        jnp.zeros((HEAD, wide), jnp.float32),
                    )
                    for _ in range(KV_HEADS)
                ),
            )
            parts = []
            for g in range(KV_HEADS):
                top, total, acc = state[g]
                part = (acc / total).T
                parts += [part[i * block_len : (i + 1) * block_len] for i in range(GROUPS)]
                n = b * KV_HEADS + g
                log_ref[n : n + 1, :] = top + jnp.log(total)
            out_ref[rows, :] = jnp.concatenate(parts, axis=1)

    return run_kernel(
        kernel,
        [((row_count, D), jnp.float32), ((2 * KV_HEADS, wide), jnp.float32)],
        [bounds, table, query_rot, *pair_halves, first_key, last_key],
        scalars=2,
        scratch=[pltpu.VMEM((table.shape[0] * row_count, 2 * KV_WIDTH), jnp.bfloat16)],
        microseconds=12,
    )


def fill_out_weights(out_w_ref, own_ref, other_ref, down_rows):
    _, core = rank()
    half, rows, _ = other_ref.shape
    for n in range(half):
        pair = both_cores(own_ref[n, down_rows:, :], other_ref[n], core)
        for owner in range(2):
            start = (owner * half + n) * rows
            out_w_ref[start : start + rows, :] = pair[owner]


def mix(attended, tokens, low_own, out_other, gain):
    row_count = tokens.shape[0]
    down_rows = low_own.shape[1] - out_other.shape[1]

    def kernel(
        attended_ref, tokens_ref, own_ref, other_ref, gain_ref, residual_ref, hidden_ref, out_w_ref
    ):
        fill_out_weights(out_w_ref, own_ref, other_ref, down_rows)
        attn_low = attended_ref[...].astype(jnp.bfloat16)
        residual = tokens_ref[...].astype(jnp.float32) + dot(attn_low, out_w_ref[...])
        residual_ref[...] = residual
        hidden_ref[...] = ((residual * inverse_root(residual)) * gain_ref[...]).astype(jnp.bfloat16)

    return run_kernel(
        kernel,
        [((row_count, D), jnp.float32), ((row_count, D), jnp.bfloat16)],
        [attended, tokens, low_own, out_other, gain],
        scratch=[pltpu.VMEM((D, D), jnp.bfloat16)],
        microseconds=2,
    )


def feed_forward(direct, hidden, hidden_other, grad_out, grad_other, wide, low_own, ff, shards):
    row_count = hidden.shape[0]
    width = ff // 2
    chips = lax.axis_size("ctx") // 2
    lanes = ff // chips
    rows = D // shards
    down_rows = ff // shards
    half = shards // 2
    steps = 2
    chunk = width // steps
    slice_rows = down_rows // (2 * chips)
    pile = rows // slice_rows

    def kernel(hidden_ref, hidden_other_ref, grad_ref, grad_other_ref, low_ref, *refs):
        wide_refs, refs = refs[: len(wide)], refs[len(wide) :]
        out_ref, hidden_grad_ref, sent_ref = refs[:3]
        wide_grads = refs[3 : 3 + (chips if direct else 2)]
        wide_ref, gate_grad_ref, down_ref, low_ref_f32 = refs[-4:]
        chip, _ = rank()
        for n in range(half):
            down_ref[n * down_rows : (n + 1) * down_rows, :] = low_ref[n, :down_rows, :]
        if direct:
            for i in range(chips):
                q = chip ^ i
                columns = pl.ds(pl.multiple_of((q % (chips // 2)) * lanes, TILE), lanes)
                wide_ref[q // (chips // 2), :, columns] = wide_refs[i][...].reshape(D, lanes)
        else:
            for kind in range(2):
                wide_ref[kind] = wide_refs[kind][...]
        hidden_all = jnp.concatenate([hidden_ref[...], hidden_other_ref[...]], axis=0)
        grad_all = jnp.concatenate([grad_ref[...], grad_other_ref[...]], axis=0)
        hidden_t = hidden_all.T
        result = jnp.zeros((2 * row_count, D), jnp.float32)
        grad_hidden = jnp.zeros((2 * row_count, D), jnp.float32)
        for j in range(steps):
            columns = slice(j * chunk, (j + 1) * chunk)
            gate_w, up_w = wide_ref[0, :, columns], wide_ref[1, :, columns]
            down_w = down_ref[columns, :]
            gate_value, up_value = dot(hidden_all, gate_w), dot(hidden_all, up_w)
            sigmoid = 1.0 / (1.0 + jnp.exp(-gate_value))
            silu = gate_value * sigmoid
            activation = (silu * up_value).astype(jnp.bfloat16)
            result += dot(activation, down_w)
            grad_activation = dot_nt(grad_all, down_w)
            grad_gate = (
                grad_activation * up_value * sigmoid * (1.0 + gate_value * (1.0 - sigmoid))
            ).astype(jnp.bfloat16)
            grad_up = (grad_activation * silu).astype(jnp.bfloat16)
            grad_hidden += dot_nt(grad_gate, gate_w) + dot_nt(grad_up, up_w)
            gate_grad_ref[0, :, columns] = grad_gate
            gate_grad_ref[1, :, columns] = grad_up
            low = dot(activation.T, grad_all)
            if direct:
                low_ref_f32[...] = low
                for i in range(chips):
                    for g in range(2):
                        start = pl.multiple_of(((chip ^ i) * 2 + g) * slice_rows, 16)
                        part = low_ref_f32[pl.ds(start, slice_rows), :].astype(jnp.bfloat16)
                        wide_grads[i][2 * j + g, :, lanes:] = stack_down(part, pile)
            else:
                refs[5][columns, :] = low.astype(jnp.bfloat16)
        out_ref[...] = result[:row_count]
        hidden_grad_ref[...] = grad_hidden[:row_count]
        sent_ref[0] = result[row_count:].astype(jnp.bfloat16)
        sent_ref[1] = grad_hidden[row_count:].astype(jnp.bfloat16)
        if direct:
            for i in range(chips):
                q = chip ^ i
                columns = pl.ds(pl.multiple_of((q % (chips // 2)) * lanes, TILE), lanes)
                operand = gate_grad_ref[q // (chips // 2), :, columns]
                wide_grads[i][:, :, :lanes] = (
                    dot(hidden_t, operand).astype(jnp.bfloat16).reshape(shards, rows, lanes)
                )
        else:
            for kind in range(2):
                wide_grads[kind][...] = dot(hidden_t, gate_grad_ref[kind]).astype(jnp.bfloat16)

    outs = [
        ((row_count, D), jnp.float32),
        ((row_count, D), jnp.float32),
        ((2, row_count, D), jnp.bfloat16),
    ]
    outs += (
        [((shards, rows, lanes + D // pile), jnp.bfloat16)] * chips
        if direct
        else [((D, width), jnp.bfloat16)] * 2 + [((width, D), jnp.bfloat16)]
    )
    return run_kernel(
        kernel,
        outs,
        [hidden, hidden_other, grad_out, grad_other, low_own, *wide],
        scratch=[
            pltpu.VMEM((2, D, width), jnp.bfloat16),
            pltpu.VMEM((2, 2 * row_count, width), jnp.bfloat16),
            pltpu.VMEM((width, D), jnp.bfloat16),
            pltpu.VMEM((chunk, D), jnp.float32),
        ],
        microseconds=12,
    )


def unmix(
    residual, out_kept, grad_kept, received, grad_out, attended, low_own, out_other, gain
):
    row_count = residual.shape[0]
    down_rows = low_own.shape[1] - out_other.shape[1]

    def kernel(
        residual_ref,
        out_kept_ref,
        grad_kept_ref,
        received_ref,
        grad_out_ref,
        attended_ref,
        own_ref,
        other_ref,
        gain_ref,
        output_ref,
        residual_grad_ref,
        attended_grad_ref,
        out_grad_ref,
        out_w_ref,
    ):
        fill_out_weights(out_w_ref, own_ref, other_ref, down_rows)
        residual = residual_ref[...]
        result = residual + out_kept_ref[...] + received_ref[0].astype(jnp.float32)
        output_ref[...] = result.astype(jnp.bfloat16)
        grad_hidden = grad_kept_ref[...] + received_ref[1].astype(jnp.float32)
        inv_two = inverse_root(residual)
        residual_grad = grad_out_ref[...].astype(jnp.float32) + norm_back(
            grad_hidden, residual * inv_two, inv_two, gain_ref[...]
        )
        residual_grad_ref[...] = residual_grad
        grad_branch = residual_grad.astype(jnp.bfloat16)
        attended_grad_ref[...] = dot_nt(grad_branch, out_w_ref[...]).astype(jnp.bfloat16)
        out_grad_ref[...] = dot_tn(
            attended_ref[...].astype(jnp.bfloat16), grad_branch
        ).astype(jnp.bfloat16)

    return run_kernel(
        kernel,
        [
            ((row_count, D), jnp.bfloat16),
            ((row_count, D), jnp.float32),
            ((row_count, D), jnp.bfloat16),
            ((D, D), jnp.bfloat16),
        ],
        [
            residual,
            out_kept,
            grad_kept,
            received,
            grad_out,
            attended,
            low_own,
            out_other,
            gain,
        ],
        scratch=[pltpu.VMEM((D, D), jnp.bfloat16)],
        microseconds=4,
    )


def attention_backward(
    bounds,
    table,
    query_rot,
    pair_halves,
    first_key,
    last_key,
    log_total,
    attended,
    grad_attended,
    cos_all,
    sin_all,
    cos_own,
    sin_own,
):
    row_count = query_rot.shape[0]
    block_len = row_count // 2
    wide = GROUPS * block_len
    slots = table.shape[0]
    chips = slots // 2
    half = HEAD // 2

    def kernel(
        bounds_ref,
        table_ref,
        query_ref,
        own_ref,
        other_ref,
        first_ref,
        last_ref,
        log_ref,
        attended_ref,
        grad_ref,
        cos_ref,
        sin_ref,
        cos_own_ref,
        sin_own_ref,
        query_t_ref,
        kept_ref,
        sent_ref,
        pairs_ref,
        pair_grad_ref,
    ):
        natural_order(pairs_ref, table_ref, (own_ref, other_ref))
        pair_grad_ref[...] = jnp.zeros_like(pair_grad_ref)
        for b in range(2):
            rows = slice(b * block_len, (b + 1) * block_len)
            query_block = query_ref[rows, :]
            grad_block = grad_ref[rows, :]
            product = grad_block.astype(jnp.float32) * attended_ref[rows, :]
            queries = [heads_to_rows(query_block, g) for g in range(KV_HEADS)]
            grads = [heads_to_rows(grad_block, g) for g in range(KV_HEADS)]
            deltas = [
                jnp.sum(heads_to_rows(product, g).T, axis=0, keepdims=True)
                for g in range(KV_HEADS)
            ]
            first = jnp.concatenate([first_ref[b : b + 1, :]] * GROUPS, axis=1)
            last = jnp.concatenate([last_ref[b : b + 1, :]] * GROUPS, axis=1)

            def step(j, state):
                start = pl.multiple_of(j * row_count, row_count)
                pos = start + lax.broadcasted_iota(jnp.int32, (row_count, wide), 0)
                visible = (pos >= first) & (pos <= last)
                result = []
                key_grads = []
                value_grads = []
                for g in range(KV_HEADS):
                    key_piece = pairs_ref[pl.ds(start, row_count), g * HEAD : (g + 1) * HEAD]
                    value_piece = pairs_ref[
                        pl.ds(start, row_count), KV_WIDTH + g * HEAD : KV_WIDTH + (g + 1) * HEAD
                    ]
                    n = b * KV_HEADS + g
                    scores = dot_nt(key_piece, queries[g])
                    weights = jnp.where(visible, jnp.exp(scores - log_ref[n : n + 1, :]), 0.0)
                    weight_grad = dot_nt(value_piece, grads[g])
                    score_grad = (weights * (weight_grad - deltas[g])).astype(jnp.bfloat16)
                    value_grads.append(dot(weights.astype(jnp.bfloat16), grads[g]))
                    key_grads.append(dot(score_grad, queries[g]))
                    result.append(state[g] + dot_tn(key_piece, score_grad))
                pair_grad_ref[pl.ds(start, row_count), :] += jnp.concatenate(
                    key_grads + value_grads, axis=1
                )
                return tuple(result)

            state = lax.fori_loop(
                bounds_ref[2 * b],
                bounds_ref[2 * b + 1],
                step,
                tuple(jnp.zeros((HEAD, wide), jnp.float32) for _ in range(KV_HEADS)),
            )
            cos_part, sin_part = cos_own_ref[:, rows], sin_own_ref[:, rows]
            for g in range(KV_HEADS):
                for i in range(GROUPS):
                    part = state[g][:, i * block_len : (i + 1) * block_len]
                    top, bottom = part[:half], part[half:]
                    h = (g * GROUPS + i) * HEAD
                    query_t_ref[h : h + half, rows] = (
                        (top * cos_part + bottom * sin_part) * HEAD ** (-0.5)
                    ).astype(jnp.bfloat16)
                    query_t_ref[h + half : h + HEAD, rows] = (
                        (bottom * cos_part - top * sin_part) * HEAD ** (-0.5)
                    ).astype(jnp.bfloat16)

        chip, core = rank()
        for i in range(chips):
            for ref, to_core in ((kept_ref, core), (sent_ref, 1 - core)):
                block = table_ref[(chip ^ i) * 2 + to_core]
                for part, place in ((0, block), (1, 2 * slots - 1 - block)):
                    source = pl.ds(pl.multiple_of(place * block_len, block_len), block_len)
                    ref[i, part * block_len : (part + 1) * block_len, :] = turn_pairs(
                        pair_grad_ref[source, :], cos_ref[source, :], -sin_ref[source, :]
                    ).astype(jnp.bfloat16)

    half_shape = ((chips, row_count, 2 * KV_WIDTH), jnp.bfloat16)
    return run_kernel(
        kernel,
        [((D, row_count), jnp.bfloat16), half_shape, half_shape],
        [
            bounds,
            table,
            query_rot,
            *pair_halves,
            first_key,
            last_key,
            log_total,
            attended,
            grad_attended,
            cos_all,
            sin_all,
            cos_own,
            sin_own,
        ],
        scalars=2,
        scratch=[
            pltpu.VMEM((slots * row_count, 2 * KV_WIDTH), jnp.bfloat16),
            pltpu.VMEM((slots * row_count, 2 * KV_WIDTH), jnp.float32),
        ],
        microseconds=16,
    )


def query_gradients(query_t, hidden_half):
    row_count = query_t.shape[1]

    def kernel(query_t_ref, hidden_ref, query_ref, weight_ref):
        query_ref[...] = query_t_ref[...].T
        weight_ref[...] = dot(query_t_ref[...], hidden_ref[0]).T.astype(jnp.bfloat16)

    return run_kernel(
        kernel,
        [((row_count, D), jnp.bfloat16), ((D, D), jnp.bfloat16)],
        [query_t, hidden_half],
        microseconds=2,
    )


def first_gradients(direct, kept, received, hidden_half, query_w, out_grad, shards):
    chips, row_count, _ = kept.shape
    rest = D - HEAD
    columns_all = 2 * KV_WIDTH + D + HEAD
    rows = D // shards

    def kernel(kept_ref, received_ref, hidden_ref, query_w_ref, out_grad_ref, *refs):
        pair_refs, outs = refs[:chips], refs[chips:-1]
        mixed_ref = refs[-1]
        total = jnp.zeros((2 * KV_WIDTH, D), jnp.float32)
        for i in range(chips):
            pairs = (
                kept_ref[i].astype(jnp.float32) + received_ref[i].astype(jnp.float32)
            ).astype(jnp.bfloat16)
            pair_refs[i][...] = pairs
            total += dot_tn(pairs, hidden_ref[i])
        mixed_ref[:, : 2 * KV_WIDTH] = total.T.astype(jnp.bfloat16)
        mixed_ref[:, 2 * KV_WIDTH : 2 * KV_WIDTH + D] = query_w_ref[...]
        mixed_ref[:, 2 * KV_WIDTH + D :] = out_grad_ref[:, rest:]
        if not direct:
            outs[0][...] = mixed_ref[...]
            return
        chip, core = rank()
        for n in range(2 * chips):
            c = (chip ^ (n % chips)) * 2 + (core ^ (n // chips))
            part = mixed_ref[:, pl.ds(pl.multiple_of(c * TILE, TILE), TILE)]
            tile = out_grad_ref[:, pl.ds(pl.multiple_of((c // 2) * TILE, TILE), TILE)]
            unit = jnp.where(c % 2 == 0, tile[:, : TILE // 2], tile[:, TILE // 2 :])
            for z in range(shards):
                outs[n][z, :rows, :] = part[z * rows : (z + 1) * rows]
                middle = z * rows + rows // 2
                outs[n][z, rows:, : TILE // 2] = unit[z * rows : middle]
                outs[n][z, rows:, TILE // 2 :] = unit[middle : (z + 1) * rows]

    outs = [((row_count, 2 * KV_WIDTH), jnp.bfloat16)] * chips
    outs += (
        [((shards, rows + rows // 2, TILE), jnp.bfloat16)] * (2 * chips)
        if direct
        else [((D, columns_all), jnp.bfloat16)]
    )
    result = run_kernel(
        kernel,
        outs,
        [kept, received, hidden_half, query_w, out_grad],
        scratch=[pltpu.VMEM((D, columns_all), jnp.bfloat16)],
        microseconds=3,
    )
    return result[:chips], result[chips:]


def local(
    layer_input,
    slot_table,
    seq_ids,
    w_query,
    w_key,
    w_value,
    w_out,
    w_gate,
    w_up,
    w_down,
    attn_gain,
    ffn_gain,
    cotangent,
):
    count = lax.axis_size("ctx")
    chips = count // 2
    index = lax.axis_index("ctx")
    chip, core = rank()
    shards = lax.axis_size("fsdp")
    rows, ff = w_gate.shape
    row_count = layer_input.shape[1]
    block_len = row_count // 2
    length = row_count * count
    direct = (
        rows % 16 == 0 and (ff // chips) % TILE == 0 and count * TILE == D + 2 * KV_WIDTH + HEAD
    )

    mixed_shard = jnp.concatenate(
        [w_key, w_value, w_query, jnp.zeros((rows, HEAD), jnp.bfloat16)], axis=1
    )
    piece = first_piece(mixed_shard, index, count)
    gains = jnp.concatenate([attn_gain, ffn_gain])
    gains = jnp.pad(gains, (0, 16 * piece.shape[1] - 2 * rows)).reshape(16, piece.shape[1])
    tokens_low = layer_input[0]
    token_pieces = [tokens_low] + [chip_swap(tokens_low, i) for i in range(1, chips)]
    first_rows = gather_rows(jnp.concatenate([piece, gains], axis=0))
    gains_all = first_rows[:, rows:].reshape(shards, -1).astype(jnp.float32)
    gain_one = gains_all[:, :rows].reshape(1, D)
    gain_two = gains_all[:, rows : 2 * rows].reshape(1, D)
    hidden_half = normalize(token_pieces, gain_one)
    first_own = gather_same_core(after(first_rows, hidden_half))
    first_pieces = first_own + [core_swap(v) for v in first_own]
    wide_rows = gather_rows(wide_piece(w_gate, w_up, chip, core, chips), first_rows)
    low_shard = after(jnp.concatenate([w_down, w_out], axis=0), wide_rows)
    wide_pieces = gather_same_core(wide_rows)
    low_own = gather_half(low_shard)
    out_other = core_swap(low_own[:, w_down.shape[0] :])
    grad_out = cotangent[0]
    first = (
        first_pieces
        if direct
        else [
            jnp.concatenate(
                [v[:, :rows].reshape(D, -1) for v in in_rank_order(first_pieces)], axis=1
            )
        ]
    )

    own_block = lax.dynamic_index_in_dim(slot_table, index, 0, keepdims=False)
    own_blocks = jnp.stack([own_block, 2 * count - 1 - own_block])
    block_pos = own_blocks[:, None] * block_len + jnp.arange(block_len, dtype=jnp.int32)[None, :]
    documents = seq_ids[0]
    query_doc = jnp.stack(
        [
            lax.dynamic_slice(documents, (own_blocks[i] * block_len,), (block_len,))
            for i in range(2)
        ]
    )
    first_key = jnp.sum(
        (documents[None, :, None] < query_doc[:, None, :]).astype(jnp.int32), axis=1
    )
    bounds = jnp.stack(
        [jnp.min(first_key, axis=1) // row_count, own_blocks // 2 + 1], axis=1
    ).reshape(4)
    frequencies = rope_base ** (-(jnp.arange(HEAD // 2, dtype=jnp.float32) * 2.0 / HEAD))
    angles = jnp.arange(length, dtype=jnp.int32).astype(jnp.float32)[:, None] * frequencies[None, :]
    cos_all = jnp.tile(jnp.cos(angles), (1, 2 * TILE // HEAD))
    sin_all = jnp.tile(jnp.sin(angles), (1, 2 * TILE // HEAD))
    own_angles = frequencies[:, None] * block_pos.reshape(1, row_count).astype(jnp.float32)
    cos_own, sin_own = jnp.cos(own_angles), jnp.sin(own_angles)

    query_rot, own_pairs, mixed = project(
        direct, slot_table, hidden_half, first, cos_all, sin_all
    )
    pair_halves = (own_pairs, core_swap(own_pairs))
    attended, log_total = attention_forward(
        bounds, slot_table, query_rot, pair_halves, first_key, block_pos
    )
    grad_other = core_swap(after(grad_out, attended))
    residual, hidden_two = mix(attended, tokens_low, low_own, out_other, gain_two)
    if direct:
        wide = wide_pieces
    else:
        whole = [v.reshape(D, -1) for v in by_owner(wide_pieces, chip)]
        wide = [jnp.concatenate(whole[n : n + chips // 2], axis=1) for n in (0, chips // 2)]
    out_kept, grad_kept, sent, *wide_grads = feed_forward(
        direct,
        hidden_two,
        core_swap(hidden_two),
        grad_out,
        grad_other,
        wide,
        low_own,
        ff,
        shards,
    )
    lanes = ff // chips
    slice_rows = w_down.shape[0] // count
    pile = rows // slice_rows
    if not direct:
        gate_grad, up_grad, down_grad = wide_grads
        down_grad = down_grad.reshape(shards // 2, chips, 2, slice_rows, pile, D // pile)
        down_grad = down_grad.transpose(0, 2, 1, 4, 3, 5).reshape(shards, chips, rows, D // pile)
        wide_grads = [
            jnp.concatenate(
                [
                    lax.dynamic_slice_in_dim(
                        jnp.where(c < chips // 2, gate_grad, up_grad),
                        (c % (chips // 2)) * lanes,
                        lanes,
                        1,
                    ).reshape(shards, rows, lanes),
                    lax.dynamic_index_in_dim(down_grad, c, 1, keepdims=False),
                ],
                axis=2,
            )
            for c in (chip ^ i for i in range(chips))
        ]
    output, grad_residual, grad_attended, out_grad = unmix(
        residual,
        out_kept,
        grad_kept,
        core_swap(sent),
        grad_out,
        attended,
        low_own,
        out_other,
        gain_two,
    )

    query_t, pairs_kept, pairs_sent = attention_backward(
        bounds,
        slot_table,
        query_rot,
        pair_halves,
        first_key,
        block_pos,
        log_total,
        attended,
        grad_attended,
        cos_all,
        sin_all,
        cos_own,
        sin_own,
    )
    pairs_received = core_swap(pairs_sent)
    grad_query, query_w = query_gradients(query_t, hidden_half)
    pair_sums, mixed_grads = first_gradients(
        direct, pairs_kept, pairs_received, hidden_half, query_w, out_grad, shards
    )
    if not direct:
        targets = [(chip ^ i) * 2 + (core ^ a) for a in range(2) for i in range(chips)]
        units = [
            first_piece(out_grad[:, : D - HEAD], c, count)
            .reshape(shards, 2, rows // 2, -1)
            .transpose(0, 2, 1, 3)
            .reshape(shards, rows // 2, -1)
            for c in targets
        ]
        mixed_grads = [
            jnp.concatenate(
                [first_piece(mixed_grads[0], c, count).reshape(shards, rows, -1), unit], axis=1
            )
            for c, unit in zip(targets, units)
        ]
    mixed_sums = [sum_cores(*pair) for pair in zip(mixed_grads[:chips], mixed_grads[chips:])]
    first_sum = sum_chips(mixed_sums).astype(jnp.bfloat16)
    first_part = sum_rows(first_sum).astype(jnp.bfloat16)
    first_all = gather_chips(first_part)
    wide_sum = sum_chips(wide_grads, query_t).astype(jnp.bfloat16)
    wide_sum = jnp.concatenate(
        [wide_sum[:, :, :lanes], by_core_slices(wide_sum[:, :, lanes:])], axis=2
    )
    wide_part = sum_rows(wide_sum).astype(jnp.bfloat16)
    wide_all = gather_chips(wide_part)
    owned = sum_chips(after(tuple(pair_sums), first_sum)).astype(jnp.bfloat16)
    grad_hidden_one = dot_nt(
        jnp.concatenate([owned, grad_query], axis=1), mixed[:, : 2 * KV_WIDTH + D]
    )
    tokens = tokens_low.astype(jnp.float32)
    inv_one = inverse_root(tokens)
    grad_input = (
        grad_residual + norm_back(grad_hidden_one, tokens * inv_one, inv_one, gain_one)
    ).astype(jnp.bfloat16)

    gain_rows = [v.astype(jnp.float32).reshape(1, rows) for v in (attn_gain, ffn_gain)]
    if direct:
        gate_grad, up_grad, down_grad, gain_grad_two = finish_wide(
            wide_all, w_gate, w_up, gain_rows[1], pile
        )
        query_w, key_w, value_w, out_w, gain_grad_one = finish_first(
            first_all, mixed_shard, gain_rows[0]
        )
    else:
        own, other = by_owner(wide_all[:chips], chip), by_owner(wide_all[chips:], chip)
        cores = both_cores(jnp.stack(own), jnp.stack(other), core)
        down_grad = jnp.concatenate(
            [unstack_down(cores[c % 2][c // 2][:, lanes:], pile) for c in range(count)]
        ).astype(jnp.float32)
        gate_grad, up_grad = (
            jnp.concatenate(
                [cores[k][n + q][:, :lanes] for k in range(2) for q in range(chips // 2)], axis=1
            ).astype(jnp.float32)
            for n in (0, chips // 2)
        )
        ordered = in_rank_order(first_all)
        first_grad = jnp.concatenate([v[:rows] for v in ordered], axis=1).astype(jnp.float32)
        units = [
            v[rows:].reshape(rows // 2, 2, -1).transpose(1, 0, 2).reshape(rows, -1) for v in ordered
        ]
        key_w, value_w, query_w, last = jnp.split(
            first_grad, [KV_WIDTH, 2 * KV_WIDTH, 2 * KV_WIDTH + D], axis=1
        )
        out_w = jnp.concatenate([*[v.astype(jnp.float32) for v in units], last], axis=1)
        used = 2 * KV_WIDTH + D
        gain_grad_one = (
            jnp.sum(
                first_grad[:, :used] * mixed_shard[:, :used].astype(jnp.float32),
                axis=1,
            )
            / gain_rows[0]
        )
        gain_grad_two = (
            jnp.sum(
                gate_grad * w_gate.astype(jnp.float32) + up_grad * w_up.astype(jnp.float32),
                axis=1,
            )
            / gain_rows[1]
        )
    return (
        output[None],
        grad_input[None],
        query_w,
        key_w,
        value_w,
        out_w,
        gate_grad,
        up_grad,
        down_grad,
        gain_grad_one.reshape(rows),
        gain_grad_two.reshape(rows),
    )


def solution(mesh):
    placed = (
        P("fsdp", "ctx", None),
        P(),
        P("fsdp", None),
        P("fsdp", None),
        P("fsdp", None),
        P("fsdp", None),
        P("fsdp", None),
        P("fsdp", None),
        P("fsdp", None),
        P("fsdp", None),
        P("fsdp"),
        P("fsdp"),
        P("fsdp", "ctx", None),
    )
    return jax.shard_map(
        local,
        mesh=mesh,
        in_specs=placed,
        out_specs=(
            P("fsdp", "ctx", None),
            P("fsdp", "ctx", None),
            P("fsdp", None),
            P("fsdp", None),
            P("fsdp", None),
            P("fsdp", None),
            P("fsdp", None),
            P("fsdp", None),
            P("fsdp", None),
            P("fsdp"),
            P("fsdp"),
        ),
        check_vma=False,
    )
```

time: 311 us -> 209 us (0.67); the launches traced: 307 us -> 209 us
  local copies, waits for them, and re-layouts: 66.5 us -> 19.3 us
  matrix products: 27 us -> 0.71 us
  starting transfers between devices: 85.7 us -> 60.5 us
  Pallas kernels: 43.9 us -> 57.4 us
  other arithmetic: 23.2 us -> 11.7 us
    ppermute x83 -> x58, starting transfers between devices: 85.7 us -> 59 us  [swap(): return lax.ppermute(value, axis, [(i, i ^ offset) for i in range(count)])]
    dot_general x21 -> x1, matrix products: 27 us -> 0.71 us  [dot_nt(): lax.dot_general(first_matrix, second_matrix, (((1,), (1,)), ((), ())), pr...]
    pallas_call x9 -> x11, Pallas kernels: 43.9 us -> 57.4 us  [run_kernel(): pl.pallas_call(kernel, out_shape=tuple((jax.ShapeDtypeStruct(*out) for ou...]
    reshape x4 -> x2, local copies, waits for them, and re-layouts: 10.8 us -> 1.33 us  [the longest x1 0.67 us: local(): gain_one = gains_all[:, :rows].reshape(1, D)]
    convert_element_type x9 -> x0, local copies, waits for them, and re-layouts: 8.75 us -> none  [the longest x1 3.89 us: local(): grad_down_w.astype(jnp.bfloat16)]
    convert_element_type x15 -> x9, other arithmetic: 8.68 us -> 1.5 us  [the longest x1 0.63 us: local(): block_pos.reshape(1, row_count).astype(jnp.float32)]
    unnamed x171 -> x121, local copies, waits for them, and re-layouts: 17 us -> 9.94 us
    slice x8 -> x4, local copies, waits for them, and re-layouts: 6.22 us -> 0.1 us  [the longest x1 0.07 us: local(): gain_two = gains_all[:, rows:2 * rows].reshape(1, D)]
  transfers between devices with their start and end apart: 83 -> 59, of which waited for: 17 -> 16; matrix products, arithmetic and copies ran while one was open for 27% -> 11% of each run, Pallas kernels for 6% -> 20%
where the time goes in v2:
time: 209 us
  starting transfers between devices  60.5 us (29%)
  Pallas kernels  57.4 us (27%)
  waiting for transfers between devices  56.5 us (27%)
  local copies, waits for them, and re-layouts  19.3 us (9%)
  other arithmetic  11.7 us (6%)
  between operations  2.86 us (1%)
    ppermute x58, starting transfers between devices, swap(): return lax.ppermute(value, axis, [(i, i ^ offset) for i in range(count)])  59 us
    pallas_call x11, Pallas kernels, run_kernel(): pl.pallas_call(kernel, out_shape=tuple((jax.ShapeDtypeStruct(*out) for ou...  57.4 us
    ppermute x58, waiting for transfers between devices, swap(): return lax.ppermute(value, axis, [(i, i ^ offset) for i in range(count)])  56.5 us
    unnamed x121, local copies, waits for them, and re-layouts  9.94 us
  transfers between devices with their start and end apart: 59, of which 16 were waited for; matrix products, arithmetic and copies ran while one was open for 11% of the time, Pallas kernels for 20%

profile of v2, /device:TPU:0, one launch (start us, length us, event | category | flops | bytes accessed | tf_op | source)
XLA Modules:
  0.0 208.9 jit_solution(1919828815235232375)
XLA Ops:
  1.9 3.0 %collective-permute-start = (bf16[256,576]{1,0:T(8,128)(2,1)S(1)}, bf16[256,576]{1,0:T(8,128)(2,1)}, u32[]{:S(2)}, u32[]{:S(2)}) collective-permute-start(bf16[256,576]{1,0:T(8,128)(2,1)S(1)} %bitcast.76), channel_id=1, source_target_pairs={{0,8},{4,12},{8,0},{12,4},{16,24},{20,28},{24,16},{28,20},{1,9},{5... | collective-permute-start | bytes 884744 | tf_op jit(solution)/shard_map/ppermute | solution.py:44
  4.9 1.5 collective-permute-start.1
  8.4 2.1 %collective-permute-start.3 = (bf16[1,160,128]{2,1,0:T(8,128)(2,1)S(1)}, bf16[1,160,128]{2,1,0:T(8,128)(2,1)S(1)}, u32[]{:S(2)}, u32[]{:S(2)}) collective-permute-start(bf16[1,160,128]{2,1,0:T(8,128)(2,1)S(1)} %maximum_bitcast_fusion), channel_id=1, source_target_pairs={{0,1},{1,0},{2,3},{3,2},{4,5},{5,4},{6,7},{7,6},{8,9},{9,8},{10,11... | collective-permute-start | bytes 122888 | tf_op jit(solution)/shard_map/ppermute | solution.py:44
  15.1 1.3 copy.66.cos_ref
  18.3 3.0 %collective-permute-start.4 = (bf16[2,160,128]{2,1,0:T(8,128)(2,1)S(1)}, bf16[2,160,128]{2,1,0:T(8,128)(2,1)S(1)}, u32[]{:S(2)}, u32[]{:S(2)}) collective-permute-start(bf16[2,160,128]{2,1,0:T(8,128)(2,1)S(1)} %pad_maximum_fusion.5), channel_id=1, source_target_pairs={{0,2},{1,3},{2,0},{3,1},{4,6},{5,7},{6,4},{7,5},{8,10},{9,11},{10,... | collective-permute-start | bytes 245768 | tf_op jit(solution)/shard_map/ppermute | solution.py:44
  21.4 2.3 %collective-permute-done.4 = bf16[2,160,128]{2,1,0:T(8,128)(2,1)S(1)} collective-permute-done((bf16[2,160,128]{2,1,0:T(8,128)(2,1)S(1)}, bf16[2,160,128]{2,1,0:T(8,128)(2,1)S(1)}, u32[]{:S(2)}, u32[]{:S(2)}) %collective-permute-start.4) | collective-permute-done | bytes 81952 | tf_op jit(solution)/shard_map/ppermute | solution.py:44
  23.8 3.1 %collective-permute-start.14 = (bf16[2,144,384]{2,1,0:T(8,128)(2,1)S(1)}, bf16[2,144,384]{2,1,0:T(8,128)(2,1)S(1)}, u32[]{:S(2)}, u32[]{:S(2)}) collective-permute-start(bf16[2,144,384]{2,1,0:T(8,128)(2,1)S(1)} %pad_maximum_fusion.3), channel_id=1, source_target_pairs={{0,2},{1,3},{2,0},{3,1},{4,6},{5,7},{6,4},{7,5},{8,10},{9,11},{10,... | collective-permute-start | bytes 663560 | tf_op jit(solution)/shard_map/ppermute | solution.py:44
  27.0 7.6 %collective-permute-done.14 = bf16[2,144,384]{2,1,0:T(8,128)(2,1)S(1)} collective-permute-done((bf16[2,144,384]{2,1,0:T(8,128)(2,1)S(1)}, bf16[2,144,384]{2,1,0:T(8,128)(2,1)S(1)}, u32[]{:S(2)}, u32[]{:S(2)}) %collective-permute-start.14) | collective-permute-done | bytes 221216 | tf_op jit(solution)/shard_map/ppermute | solution.py:44
  34.7 1.5 collective-permute-start.15
  36.9 2.9 %shard_map.212.hidden_ref = bf16[4,256,576]{2,1,0:T(8,128)(2,1)} custom-call(bf16[256,576]{1,0:T(8,128)(2,1)} %bitcast.79, bf16[256,576]{1,0:T(8,128)(2,1)} %collective-permute-done.refs_1_, bf16[256,576]{1,0:T(8,128)(2,1)} %collective-permute-done.1.refs_2_, bf16[256,576]{1,0:T(8,128)(2,1)} %collective-permute-done.2.refs_3_, f32[1,576]{1,0:T(1,128)} %reshape.394.refs_4_), custom_call_target="tpu_custom_call" | custom-call | flops 3449999872 | bytes 1024 | tf_op jit(solution)/shard_map/pallas_call | solution.py:24
  39.8 1.5 collective-permute-start.5
  41.3 1.5 collective-permute-start.6
  44.1 2.3 %collective-permute-done.5.refs_1_ = bf16[4,160,128]{2,1,0:T(8,128)(2,1)S(1)} collective-permute-done((bf16[4,160,128]{2,1,0:T(8,128)(2,1)S(1)}, bf16[4,160,128]{2,1,0:T(8,128)(2,1)S(1)}, u32[]{:S(2)}, u32[]{:S(2)}) %collective-permute-start.5) | collective-permute-done | bytes 163872 | tf_op jit(solution)/shard_map/ppermute | solution.py:44
  46.4 3.0 %collective-permute-done.6.refs_2_ = bf16[4,160,128]{2,1,0:T(8,128)(2,1)S(1)} collective-permute-done((bf16[4,160,128]{2,1,0:T(8,128)(2,1)S(1)}, bf16[4,160,128]{2,1,0:T(8,128)(2,1)S(1)}, u32[]{:S(2)}, u32[]{:S(2)}) %collective-permute-start.6) | collective-permute-done | bytes 163872 | tf_op jit(solution)/shard_map/ppermute | solution.py:44
  50.1 3.6 %collective-permute-start.16 = (bf16[1,528,576]{2,1,0:T(8,128)(2,1)S(1)}, bf16[1,528,576]{2,1,0:T(8,128)(2,1)S(1)}, u32[]{:S(2)}, u32[]{:S(2)}) collective-permute-start(bf16[1,528,576]{2,1,0:T(8,128)(2,1)S(1)} %select_bitcast_fusion), channel_id=1, source_target_pairs={{0,1},{1,0},{2,3},{3,2},{4,5},{5,4},{6,7},{7,6},{8,9},{9,8},{10,11... | collective-permute-start | bytes 1824776 | tf_op jit(solution)/shard_map/ppermute | solution.py:44
  54.5 5.4 %shard_map.213 = (bf16[256,576]{1,0:T(8,128)(2,1)}, bf16[4,256,384]{2,1,0:T(8,128)(2,1)}, bf16[576,1024]{1,0:T(8,128)(2,1)}) custom-call(s32[8]{0:T(128)} %table_ref.5, bf16[4,256,576]{2,1,0:T(8,128)(2,1)} %shard_map.212.hidden_ref, f32[2048,128]{1,0:T(8,128)} %copy.66.cos_ref, f32[2048,128]{1,0:T(8,128)} %copy.67.sin_ref, bf16[4,160,128]{2,1,0:T(8,128)(2,1)} %copy-done.18, ...), custom_call_target="tpu_custom_call" | custom-call | flops 5750000128 | bytes 1024 | tf_op jit(solution)/shard_map/pallas_call | solution.py:24
  63.9 1.5 collective-permute-start.21
  66.5 3.0 %collective-permute-done.16 = bf16[1,528,576]{2,1,0:T(8,128)(2,1)S(1)} collective-permute-done((bf16[1,528,576]{2,1,0:T(8,128)(2,1)S(1)}, bf16[1,528,576]{2,1,0:T(8,128)(2,1)S(1)}, u32[]{:S(2)}, u32[]{:S(2)}) %collective-permute-start.16) | collective-permute-done | bytes 608288 | tf_op jit(solution)/shard_map/ppermute | solution.py:44
  70.2 6.3 %shard_map.214 = (f32[256,576]{1,0:T(8,128)}, f32[6,384]{1,0:T(8,128)}) custom-call(s32[4]{0:T(128)} %reshape.392.bounds_ref, s32[8]{0:T(128)} %table_ref.5, bf16[256,576]{1,0:T(8,128)(2,1)} %get-tuple-element.67.query_ref, bf16[4,256,384]{2,1,0:T(8,128)(2,1)} %get-tuple-element.68.own_ref, bf16[4,256,384]{2,1,0:T(8,128)(2,1)} %collective-permute-done.12.other_ref, ...), custom_call_target="tpu_custom_call" | custom-call | flops 13799999488 | bytes 1024 | tf_op jit(solution)/shard_map/pallas_call | solution.py:24
  79.5 3.2 %shard_map.215 = (f32[256,576]{1,0:T(8,128)}, bf16[256,576]{1,0:T(8,128)(2,1)}) custom-call(f32[256,576]{1,0:T(8,128)} %get-tuple-element.69.attended_ref, bf16[256,576]{1,0:T(8,128)(2,1)} %bitcast.80, bf16[2,528,576]{2,1,0:T(8,128)(2,1)} %pad_maximum_fusion.own_ref.low_ref, bf16[2,144,576]{2,1,0:T(8,128)(2,1)} %copy-done.25, f32[1,576]{1,0:T(1,128)} %reshape.395.gain_ref), custom_call_target="tpu_custom_call" | custom-call | flops 2300000000 | bytes 1024 | tf_op jit(solution)/shard_map/pallas_call | solution.py:24
  82.8 2.0 collective-permute-done.21.refs_2_
  87.3 10.6 %shard_map.216 = (f32[256,576]{1,0:T(8,128)}, f32[256,576]{1,0:T(8,128)}, bf16[2,256,576]{2,1,0:T(8,128)(2,1)}, bf16[4,144,576]{2,1,0:T(8,128)(2,1)}, bf16[4,144...) custom-call(bf16[256,576]{1,0:T(8,128)(2,1)} %get-tuple-element.73.hidden_ref, ...), custom_call_target="tpu_custom_call" | custom-call | flops 13799999488 | bytes 1024 | tf_op jit(solution)/shard_map/pallas_call | solution.py:24
  97.9 1.3 copy.70
  100.2 4.0 %collective-permute-start.45 = (bf16[4,144,576]{2,1,0:T(8,128)(2,1)}, bf16[4,144,576]{2,1,0:T(8,128)(2,1)S(1)}, u32[]{:S(2)}, u32[]{:S(2)}) collective-permute-start(bf16[4,144,576]{2,1,0:T(8,128)(2,1)} %get-tuple-element.110), channel_id=1, source_target_pairs={{0,8},{4,12},{8,0},{12,4},{16,24},{20,28},{24,16},{28,20},{1,9},{5... | collective-permute-start | bytes 1990664 | tf_op jit(solution)/shard_map/ppermute | solution.py:44
  104.1 1.9 collective-permute-start.46
  106.0 2.2 %copy.71.received_ref = bf16[2,256,576]{2,1,0:T(8,128)(2,1)} copy(bf16[2,256,576]{1,2,0:T(8,128)(2,1)} %collective-permute-done.23) | data formatting | bytes 1179648 | tf_op jit(solution)/shard_map/ppermute | solution.py:44
  108.2 4.5 %shard_map.217 = (bf16[256,576]{1,0:T(8,128)(2,1)}, f32[256,576]{1,0:T(8,128)}, bf16[256,576]{1,0:T(8,128)(2,1)}, bf16[576,576]{1,0:T(8,128)(2,1)}) custom-call(f32[256,576]{1,0:T(8,128)} %get-tuple-element.72.residual_ref, f32[256,576]{1,0:T(8,128)} %get-tuple-element.75.out_kept_ref, f32[256,576]{1,0:T(8,128)} %get-tuple-element.76.grad_kept_ref, ...), custom_call_target="tpu_custom_call" | custom-call | flops 4600000000 | bytes 1024 | tf_op jit(solution)/shard_map/pallas_call | solution.py:24
  112.6 9.7 %shard_map.218 = (bf16[576,256]{1,0:T(8,128)(2,1)}, bf16[4,256,384]{2,1,0:T(8,128)(2,1)}, bf16[4,256,384]{2,1,0:T(8,128)(2,1)}) custom-call(s32[4]{0:T(128)} %reshape.392.bounds_ref, s32[8]{0:T(128)} %table_ref.5, bf16[256,576]{1,0:T(8,128)(2,1)} %get-tuple-element.67.query_ref, bf16[4,256,384]{2,1,0:T(8,128)(2,1)} %get-tuple-element.68.own_ref, ...), custom_call_target="tpu_custom_call" | custom-call | flops 18400000000 | bytes 1024 | tf_op jit(solution)/shard_map/pallas_call | solution.py:24
  123.0 15.6 %collective-permute-done.46 = bf16[4,144,576]{2,1,0:T(8,128)(2,1)S(1)} collective-permute-done((bf16[4,144,576]{2,1,0:T(8,128)(2,1)}, bf16[4,144,576]{2,1,0:T(8,128)(2,1)S(1)}, u32[]{:S(2)}, u32[]{:S(2)}) %collective-permute-start.46) | collective-permute-done | bytes 663584 | tf_op jit(solution)/shard_map/ppermute | solution.py:44
  139.1 2.9 %shard_map.219 = (bf16[256,576]{1,0:T(8,128)(2,1)}, bf16[576,576]{1,0:T(8,128)(2,1)}) custom-call(bf16[576,256]{1,0:T(8,128)(2,1)} %get-tuple-element.84.query_t_ref, bf16[4,256,576]{2,1,0:T(8,128)(2,1)} %shard_map.212.hidden_ref), custom_call_target="tpu_custom_call" | custom-call | flops 2300000000 | bytes 1024 | tf_op jit(solution)/shard_map/pallas_call | solution.py:24
  142.1 5.3 %shard_map.220 = (bf16[256,384]{1,0:T(8,128)(2,1)}, bf16[256,384]{1,0:T(8,128)(2,1)}, bf16[256,384]{1,0:T(8,128)(2,1)}, bf16[256,384]{1,0:T(8,128)(2,1)}, bf16[4...) custom-call(bf16[4,256,384]{2,1,0:T(8,128)(2,1)} %get-tuple-element., ...), custom_call_target="tpu_custom_call" | custom-call | flops 3449999872 | bytes 1024 | tf_op jit(solution)/shard_map/pallas_call | solution.py:24
  148.1 1.4 collective-permute-start.51
  149.6 1.3 collective-permute-start.50
  150.9 1.7 collective-permute-start.49
  154.4 1.4 collective-permute-start.31
  155.8 1.8 collective-permute-done.51
  157.6 1.6 collective-permute-start.29
  159.2 8.1 %collective-permute-done.50 = bf16[144,576]{1,0:T(8,128)(2,1)S(1)} collective-permute-done((bf16[144,576]{1,0:T(8,128)(2,1)S(1)}, bf16[144,576]{1,0:T(8,128)(2,1)S(1)}, u32[]{:S(2)}, u32[]{:S(2)}) %collective-permute-start.50) | collective-permute-done | bytes 165920 | tf_op jit(solution)/shard_map/ppermute | solution.py:44
  169.7 1.4 collective-permute-start.53
  171.1 4.7 %collective-permute-done.27 = bf16[4,216,128]{2,1,0:T(8,128)(2,1)S(1)} collective-permute-done((bf16[4,216,128]{2,1,0:T(8,128)(2,1)S(1)}, bf16[4,216,128]{2,1,0:T(8,128)(2,1)S(1)}, u32[]{:S(2)}, u32[]{:S(2)}) %collective-permute-start.27) | collective-permute-done | bytes 221216 | tf_op jit(solution)/shard_map/ppermute | solution.py:44
  177.2 3.2 %collective-permute-start.35 = (bf16[216,128]{1,0:T(8,128)(2,1)S(1)}, bf16[216,128]{1,0:T(8,128)(2,1)S(1)}, u32[]{:S(2)}, u32[]{:S(2)}) collective-permute-start(bf16[216,128]{1,0:T(8,128)(2,1)S(1)} %get-tuple-element.174), channel_id=1, source_target_pairs={{0,1},{1,0},{2,3},{3,2},{4,5},{5,4},{6,7},{7,6},{8,9},{9,8},{10,11... | collective-permute-start | bytes 165896 | tf_op jit(solution)/shard_map/ppermute | solution.py:44
  184.6 2.3 %collective-permute-done.54.refs_3_ = bf16[144,576]{1,0:T(8,128)(2,1)S(1)} collective-permute-done((bf16[144,576]{1,0:T(8,128)(2,1)S(1)}, bf16[144,576]{1,0:T(8,128)(2,1)S(1)}, u32[]{:S(2)}, u32[]{:S(2)}) %collective-permute-start.54) | collective-permute-done | bytes 165920 | tf_op jit(solution)/shard_map/ppermute | solution.py:44
  186.9 1.8 collective-permute-start.39
  192.5 1.8 collective-permute-start.34
  194.7 1.6 collective-permute-start.32
  196.8 4.1 %shard_map.222 = (f32[144,1536]{1,0:T(8,128)}, f32[144,1536]{1,0:T(8,128)}, f32[384,576]{1,0:T(8,128)}, f32[1,144]{1,0:T(1,128)}) custom-call(bf16[144,576]{1,0:T(8,128)(2,1)} %copy-done.17, bf16[144,576]{1,0:T(8,128)(2,1)} %copy-done.34, bf16[144,576]{1,0:T(8,128)(2,1)} %copy-done.35, bf16[144,576]{1,0:T(8,128)(2,1)} %copy-done.36, ...), custom_call_target="tpu_custom_call" | custom-call | flops 1150000000 | bytes 1024 | tf_op jit(solution)/shard_map/pallas_call | solution.py:24
  201.0 2.4 %copy.79 = f32[384,576]{0,1:T(8,128)} copy(f32[384,576]{1,0:T(8,128)} %get-tuple-element.162) | data formatting | bytes 1769472
  204.1 2.5 %shard_map.221 = (f32[144,576]{1,0:T(8,128)}, f32[144,192]{1,0:T(8,128)}, f32[144,192]{1,0:T(8,128)}, f32[144,576]{1,0:T(8,128)}, f32[1,144]{1,0:T(1,128)}) custom-call(bf16[216,128]{1,0:T(8,128)(2,1)} %copy-done.19, bf16[216,128]{1,0:T(8,128)(2,1)} %copy-done.47, bf16[216,128]{1,0:T(8,128)(2,1)} %copy-done.48, bf16[216,128]{1,0:T(8,128)(2,1)} %copy-done.49, ...), custom_call_target="tpu_custom_call" | custom-call | flops 1150000000 | bytes 1024 | tf_op jit(solution)/shard_map/pallas_call | solution.py:24
  (271 shorter events, 43.2 us)
Async XLA Ops:
  1.9 35.1 %collective-permute-start = (bf16[256,576]{1,0:T(8,128)(2,1)S(1)}, bf16[256,576]{1,0:T(8,128)(2,1)}, u32[]{:S(2)}, u32[]{:S(2)}) collective-permute-start(bf16[256,576]{1,0:T(8,128)(2,1)S(1)} %bitcast.76), channel_id=1, source_target_pairs={{0,8},{4,12},{8,0},{12,4},{16,24},{20,28},{24,16},{28,20},{1,9},{5... | collective-permute-start | bytes 884744 | tf_op jit(solution)/shard_map/ppermute | solution.py:44
  4.9 32.1 %collective-permute-start.1 = (bf16[256,576]{1,0:T(8,128)(2,1)S(1)}, bf16[256,576]{1,0:T(8,128)(2,1)}, u32[]{:S(2)}, u32[]{:S(2)}) collective-permute-start(bf16[256,576]{1,0:T(8,128)(2,1)S(1)} %bitcast.77), channel_id=1, source_target_pairs={{0,16},{4,20},{8,24},{12,28},{16,0},{20,4},{24,8},{28,12},{1,17},{... | collective-permute-start | bytes 884744 | tf_op jit(solution)/shard_map/ppermute | solution.py:44
  6.4 30.5 %collective-permute-start.2 = (bf16[256,576]{1,0:T(8,128)(2,1)S(1)}, bf16[256,576]{1,0:T(8,128)(2,1)}, u32[]{:S(2)}, u32[]{:S(2)}) collective-permute-start(bf16[256,576]{1,0:T(8,128)(2,1)S(1)} %bitcast.78), channel_id=1, source_target_pairs={{0,24},{4,28},{8,16},{12,20},{16,8},{20,12},{24,0},{28,4},{1,25},{... | collective-permute-start | bytes 884744 | tf_op jit(solution)/shard_map/ppermute | solution.py:44
  8.4 9.8 %collective-permute-start.3 = (bf16[1,160,128]{2,1,0:T(8,128)(2,1)S(1)}, bf16[1,160,128]{2,1,0:T(8,128)(2,1)S(1)}, u32[]{:S(2)}, u32[]{:S(2)}) collective-permute-start(bf16[1,160,128]{2,1,0:T(8,128)(2,1)S(1)} %maximum_bitcast_fusion), channel_id=1, source_target_pairs={{0,1},{1,0},{2,3},{3,2},{4,5},{5,4},{6,7},{7,6},{8,9},{9,8},{10,11... | collective-permute-start | bytes 122888 | tf_op jit(solution)/shard_map/ppermute | solution.py:44
  11.5 9.8 %collective-permute-start.13 = (bf16[1,144,384]{2,1,0:T(8,128)(2,1)S(1)}, bf16[1,144,384]{2,1,0:T(8,128)(2,1)S(1)}, u32[]{:S(2)}, u32[]{:S(2)}) collective-permute-start(bf16[1,144,384]{2,1,0:T(8,128)(2,1)S(1)} %fusion.17), channel_id=1, source_target_pairs={{0,1},{1,0},{2,3},{3,2},{4,5},{5,4},{6,7},{7,6},{8,9},{9,8},{10,11... | collective-permute-start | bytes 331784 | tf_op jit(solution)/shard_map/ppermute | solution.py:44
  23.8 10.8 %collective-permute-start.14 = (bf16[2,144,384]{2,1,0:T(8,128)(2,1)S(1)}, bf16[2,144,384]{2,1,0:T(8,128)(2,1)S(1)}, u32[]{:S(2)}, u32[]{:S(2)}) collective-permute-start(bf16[2,144,384]{2,1,0:T(8,128)(2,1)S(1)} %pad_maximum_fusion.3), channel_id=1, source_target_pairs={{0,2},{1,3},{2,0},{3,1},{4,6},{5,7},{6,4},{7,5},{8,10},{9,11},{10,... | collective-permute-start | bytes 663560 | tf_op jit(solution)/shard_map/ppermute | solution.py:44
  34.7 15.3 %collective-permute-start.15 = (bf16[528,576]{1,0:T(8,128)(2,1)S(1)}, bf16[528,576]{1,0:T(8,128)(2,1)S(1)}, u32[]{:S(2)}, u32[]{:S(2)}) collective-permute-start(bf16[528,576]{1,0:T(8,128)(2,1)S(1)} %pad_maximum_fusion.1), channel_id=1, source_target_pairs={{0,2},{1,3},{6,4},{7,5},{8,10},{9,11},{14,12},{15,13},{16,18},{17,... | collective-permute-start | bytes 1824776 | tf_op jit(solution)/shard_map/ppermute | solution.py:84
  39.8 6.6 %collective-permute-start.5 = (bf16[4,160,128]{2,1,0:T(8,128)(2,1)S(1)}, bf16[4,160,128]{2,1,0:T(8,128)(2,1)S(1)}, u32[]{:S(2)}, u32[]{:S(2)}) collective-permute-start(bf16[4,160,128]{2,1,0:T(8,128)(2,1)S(1)} %pad_maximum_fusion.4.refs_0_), channel_id=1, source_target_pairs={{0,8},{4,12},{8,0},{12,4},{16,24},{20,28},{24,16},{28,20},{1,9},{5... | collective-permute-start | bytes 491528 | tf_op jit(solution)/shard_map/ppermute | solution.py:44
  41.3 8.2 %collective-permute-start.6 = (bf16[4,160,128]{2,1,0:T(8,128)(2,1)S(1)}, bf16[4,160,128]{2,1,0:T(8,128)(2,1)S(1)}, u32[]{:S(2)}, u32[]{:S(2)}) collective-permute-start(bf16[4,160,128]{2,1,0:T(8,128)(2,1)S(1)} %pad_maximum_fusion.4.refs_0_), channel_id=1, source_target_pairs={{0,16},{4,20},{8,24},{12,28},{16,0},{20,4},{24,8},{28,12},{1,17},{... | collective-permute-start | bytes 491528 | tf_op jit(solution)/shard_map/ppermute | solution.py:44
  42.8 6.6 %collective-permute-start.7 = (bf16[4,160,128]{2,1,0:T(8,128)(2,1)S(1)}, bf16[4,160,128]{2,1,0:T(8,128)(2,1)S(1)}, u32[]{:S(2)}, u32[]{:S(2)}) collective-permute-start(bf16[4,160,128]{2,1,0:T(8,128)(2,1)S(1)} %pad_maximum_fusion.4.refs_0_), channel_id=1, source_target_pairs={{0,24},{4,28},{8,16},{12,20},{16,8},{20,12},{24,0},{28,4},{1,25},{... | collective-permute-start | bytes 491528 | tf_op jit(solution)/shard_map/ppermute | solution.py:44
  44.0 9.7 %collective-permute-start.8 = (bf16[4,160,128]{2,1,0:T(8,128)(2,1)S(1)}, bf16[4,160,128]{2,1,0:T(8,128)(2,1)S(1)}, u32[]{:S(2)}, u32[]{:S(2)}) collective-permute-start(bf16[4,160,128]{2,1,0:T(8,128)(2,1)S(1)} %pad_maximum_fusion.4.refs_0_), channel_id=1, source_target_pairs={{0,4},{4,0},{8,12},{12,8},{16,20},{20,16},{24,28},{28,24},{1,5},{5... | collective-permute-start | bytes 491528 | tf_op jit(solution)/shard_map/ppermute | solution.py:44
  46.4 7.3 %collective-permute-start.9 = (bf16[4,160,128]{2,1,0:T(8,128)(2,1)S(1)}, bf16[4,160,128]{2,1,0:T(8,128)(2,1)S(1)}, u32[]{:S(2)}, u32[]{:S(2)}) collective-permute-start(bf16[4,160,128]{2,1,0:T(8,128)(2,1)S(1)} %collective-permute-done.5.refs_1_), channel_id=1, source_target_pairs={{0,4},{4,0},{8,12},{12,8},{16,20},{20,16},{24,28},{28,24},{1,5},{5... | collective-permute-start | bytes 491528 | tf_op jit(solution)/shard_map/ppermute | solution.py:44
  50.1 19.4 %collective-permute-start.16 = (bf16[1,528,576]{2,1,0:T(8,128)(2,1)S(1)}, bf16[1,528,576]{2,1,0:T(8,128)(2,1)S(1)}, u32[]{:S(2)}, u32[]{:S(2)}) collective-permute-start(bf16[1,528,576]{2,1,0:T(8,128)(2,1)S(1)} %select_bitcast_fusion), channel_id=1, source_target_pairs={{0,1},{1,0},{2,3},{3,2},{4,5},{5,4},{6,7},{7,6},{8,9},{9,8},{10,11... | collective-permute-start | bytes 1824776 | tf_op jit(solution)/shard_map/ppermute | solution.py:44
  59.8 10.4 %collective-permute-start.12 = (bf16[4,256,384]{2,1,0:T(8,128)(2,1)}, bf16[4,256,384]{2,1,0:T(8,128)(2,1)}, u32[]{:S(2)}, u32[]{:S(2)}) collective-permute-start(bf16[4,256,384]{2,1,0:T(8,128)(2,1)} %get-tuple-element.68.own_ref), channel_id=1, source_target_pairs={{0,4},{4,0},{8,12},{12,8},{16,20},{20,16},{24,28},{28,24},{1,5},{5... | collective-permute-start | bytes 2359304 | tf_op jit(solution)/shard_map/ppermute | solution.py:44
  63.0 19.7 %collective-permute-start.20 = (bf16[4,144,384]{2,1,0:T(8,128)(2,1)S(1)}, bf16[4,144,384]{2,1,0:T(8,128)(2,1)S(1)}, u32[]{:S(2)}, u32[]{:S(2)}) collective-permute-start(bf16[4,144,384]{2,1,0:T(8,128)(2,1)S(1)} %pad_maximum_fusion.2.refs_0_), channel_id=1, source_target_pairs={{0,8},{4,12},{8,0},{12,4},{16,24},{20,28},{24,16},{28,20},{1,9},{5... | collective-permute-start | bytes 1327112 | tf_op jit(solution)/shard_map/ppermute | solution.py:44
  63.9 20.8 %collective-permute-start.21 = (bf16[4,144,384]{2,1,0:T(8,128)(2,1)S(1)}, bf16[4,144,384]{2,1,0:T(8,128)(2,1)}, u32[]{:S(2)}, u32[]{:S(2)}) collective-permute-start(bf16[4,144,384]{2,1,0:T(8,128)(2,1)S(1)} %pad_maximum_fusion.2.refs_0_), channel_id=1, source_target_pairs={{0,16},{4,20},{8,24},{12,28},{16,0},{20,4},{24,8},{28,12},{1,17},{... | collective-permute-start | bytes 1327112 | tf_op jit(solution)/shard_map/ppermute | solution.py:44
  65.4 20.4 %collective-permute-start.22 = (bf16[4,144,384]{2,1,0:T(8,128)(2,1)S(1)}, bf16[4,144,384]{2,1,0:T(8,128)(2,1)}, u32[]{:S(2)}, u32[]{:S(2)}) collective-permute-start(bf16[4,144,384]{2,1,0:T(8,128)(2,1)S(1)} %pad_maximum_fusion.2.refs_0_), channel_id=1, source_target_pairs={{0,24},{4,28},{8,16},{12,20},{16,8},{20,12},{24,0},{28,4},{1,25},{... | collective-permute-start | bytes 1327112 | tf_op jit(solution)/shard_map/ppermute | solution.py:44
  69.7 9.1 %collective-permute-start.17 = (bf16[2,144,576]{2,1,0:T(8,128)(2,1)S(1)}, bf16[2,144,576]{2,1,0:T(8,128)(2,1)S(1)}, u32[]{:S(2)}, u32[]{:S(2)}) collective-permute-start(bf16[2,144,576]{2,1,0:T(8,128)(2,1)S(1)} %fusion.12), channel_id=1, source_target_pairs={{0,4},{4,0},{8,12},{12,8},{16,20},{20,16},{24,28},{28,24},{1,5},{5... | collective-permute-start | bytes 995336 | tf_op jit(solution)/shard_map/ppermute | solution.py:44
  76.5 9.3 %collective-permute-start.19 = (bf16[256,576]{1,0:T(8,128)(2,1)S(1)}, bf16[256,576]{1,0:T(8,128)(2,1)S(1)}, u32[]{:S(2)}, u32[]{:S(2)}) collective-permute-start(bf16[256,576]{1,0:T(8,128)(2,1)S(1)} %bitcast.84), channel_id=1, source_target_pairs={{0,4},{4,0},{8,12},{12,8},{16,20},{20,16},{24,28},{28,24},{1,5},{5... | collective-permute-start | bytes 884744 | tf_op jit(solution)/shard_map/ppermute | solution.py:44
  99.2 6.8 %collective-permute-start.23 = (bf16[2,256,576]{1,2,0:T(8,128)(2,1)S(1)}, bf16[2,256,576]{1,2,0:T(8,128)(2,1)}, u32[]{:S(2)}, u32[]{:S(2)}) collective-permute-start(bf16[2,256,576]{1,2,0:T(8,128)(2,1)S(1)} %copy.70), channel_id=1, source_target_pairs={{0,4},{4,0},{8,12},{12,8},{16,20},{20,16},{24,28},{28,24},{1,5},{5... | collective-permute-start | bytes 1769480 | tf_op jit(solution)/shard_map/ppermute | solution.py:44
  100.2 22.8 %collective-permute-start.45 = (bf16[4,144,576]{2,1,0:T(8,128)(2,1)}, bf16[4,144,576]{2,1,0:T(8,128)(2,1)S(1)}, u32[]{:S(2)}, u32[]{:S(2)}) collective-permute-start(bf16[4,144,576]{2,1,0:T(8,128)(2,1)} %get-tuple-element.110), channel_id=1, source_target_pairs={{0,8},{4,12},{8,0},{12,4},{16,24},{20,28},{24,16},{28,20},{1,9},{5... | collective-permute-start | bytes 1990664 | tf_op jit(solution)/shard_map/ppermute | solution.py:44
  104.1 34.5 %collective-permute-start.46 = (bf16[4,144,576]{2,1,0:T(8,128)(2,1)}, bf16[4,144,576]{2,1,0:T(8,128)(2,1)S(1)}, u32[]{:S(2)}, u32[]{:S(2)}) collective-permute-start(bf16[4,144,576]{2,1,0:T(8,128)(2,1)} %get-tuple-element.111), channel_id=1, source_target_pairs={{0,16},{4,20},{8,24},{12,28},{16,0},{20,4},{24,8},{28,12},{1,17},{... | collective-permute-start | bytes 1990664 | tf_op jit(solution)/shard_map/ppermute | solution.py:44
  106.0 32.6 %collective-permute-start.47 = (bf16[4,144,576]{2,1,0:T(8,128)(2,1)}, bf16[4,144,576]{2,1,0:T(8,128)(2,1)S(1)}, u32[]{:S(2)}, u32[]{:S(2)}) collective-permute-start(bf16[4,144,576]{2,1,0:T(8,128)(2,1)} %get-tuple-element.112), channel_id=1, source_target_pairs={{0,24},{4,28},{8,16},{12,20},{16,8},{20,12},{24,0},{28,4},{1,25},{... | collective-permute-start | bytes 1990664 | tf_op jit(solution)/shard_map/ppermute | solution.py:44
  122.3 19.8 %collective-permute-start.24 = (bf16[4,256,384]{2,1,0:T(8,128)(2,1)}, bf16[4,256,384]{2,1,0:T(8,128)(2,1)}, u32[]{:S(2)}, u32[]{:S(2)}) collective-permute-start(bf16[4,256,384]{2,1,0:T(8,128)(2,1)} %get-tuple-element.83), channel_id=1, source_target_pairs={{0,4},{4,0},{8,12},{12,8},{16,20},{20,16},{24,28},{28,24},{1,5},{5... | collective-permute-start | bytes 2359304 | tf_op jit(solution)/shard_map/ppermute | solution.py:44
  148.1 9.5 %collective-permute-start.51 = (bf16[144,576]{1,0:T(8,128)(2,1)S(1)}, bf16[144,576]{1,0:T(8,128)(2,1)S(1)}, u32[]{:S(2)}, u32[]{:S(2)}) collective-permute-start(bf16[144,576]{1,0:T(8,128)(2,1)S(1)} %get-tuple-element.168), channel_id=1, source_target_pairs={{0,3},{1,2},{2,1},{3,0},{4,7},{5,6},{6,5},{7,4},{8,11},{9,10},{10,... | collective-permute-start | bytes 497672 | tf_op jit(solution)/shard_map/ppermute | solution.py:44
  149.6 17.8 %collective-permute-start.50 = (bf16[144,576]{1,0:T(8,128)(2,1)S(1)}, bf16[144,576]{1,0:T(8,128)(2,1)S(1)}, u32[]{:S(2)}, u32[]{:S(2)}) collective-permute-start(bf16[144,576]{1,0:T(8,128)(2,1)S(1)} %get-tuple-element.169), channel_id=1, source_target_pairs={{0,2},{1,3},{2,0},{3,1},{4,6},{5,7},{6,4},{7,5},{8,10},{9,11},{10,... | collective-permute-start | bytes 497672 | tf_op jit(solution)/shard_map/ppermute | solution.py:44
  150.9 17.6 %collective-permute-start.49 = (bf16[144,576]{1,0:T(8,128)(2,1)S(1)}, bf16[144,576]{1,0:T(8,128)(2,1)S(1)}, u32[]{:S(2)}, u32[]{:S(2)}) collective-permute-start(bf16[144,576]{1,0:T(8,128)(2,1)S(1)} %get-tuple-element.167), channel_id=1, source_target_pairs={{0,1},{1,0},{2,3},{3,2},{4,5},{5,4},{6,7},{7,6},{8,9},{9,8},{10,11... | collective-permute-start | bytes 497672 | tf_op jit(solution)/shard_map/ppermute | solution.py:44
  154.0 15.6 %collective-permute-start.25 = (bf16[4,216,128]{2,1,0:T(8,128)(2,1)S(1)}, bf16[4,216,128]{2,1,0:T(8,128)(2,1)S(1)}, u32[]{:S(2)}, u32[]{:S(2)}) collective-permute-start(bf16[4,216,128]{2,1,0:T(8,128)(2,1)S(1)} %copy-done.28), channel_id=1, source_target_pairs={{0,4},{4,0},{8,12},{12,8},{16,20},{20,16},{24,28},{28,24},{1,5},{5... | collective-permute-start | bytes 663560 | tf_op jit(solution)/shard_map/ppermute | solution.py:44
  154.4 16.7 %collective-permute-start.31 = (bf16[4,216,128]{2,1,0:T(8,128)(2,1)S(1)}, bf16[4,216,128]{2,1,0:T(8,128)(2,1)S(1)}, u32[]{:S(2)}, u32[]{:S(2)}) collective-permute-start(bf16[4,216,128]{2,1,0:T(8,128)(2,1)S(1)} %add_convert_fusion.2), channel_id=1, source_target_pairs={{0,24},{4,28},{8,16},{12,20},{16,8},{20,12},{24,0},{28,4},{1,25},{... | collective-permute-start | bytes 663560 | tf_op jit(solution)/shard_map/ppermute | solution.py:44
  157.6 13.5 %collective-permute-start.29 = (bf16[4,216,128]{2,1,0:T(8,128)(2,1)S(1)}, bf16[4,216,128]{2,1,0:T(8,128)(2,1)S(1)}, u32[]{:S(2)}, u32[]{:S(2)}) collective-permute-start(bf16[4,216,128]{2,1,0:T(8,128)(2,1)S(1)} %add_convert_fusion.3), channel_id=1, source_target_pairs={{0,16},{4,20},{8,24},{12,28},{16,0},{20,4},{24,8},{28,12},{1,17},{... | collective-permute-start | bytes 663560 | tf_op jit(solution)/shard_map/ppermute | solution.py:44
  167.4 8.4 %collective-permute-start.27 = (bf16[4,216,128]{2,1,0:T(8,128)(2,1)S(1)}, bf16[4,216,128]{2,1,0:T(8,128)(2,1)S(1)}, u32[]{:S(2)}, u32[]{:S(2)}) collective-permute-start(bf16[4,216,128]{2,1,0:T(8,128)(2,1)S(1)} %add_convert_fusion.4), channel_id=1, source_target_pairs={{0,8},{4,12},{8,0},{12,4},{16,24},{20,28},{24,16},{28,20},{1,9},{5... | collective-permute-start | bytes 663560 | tf_op jit(solution)/shard_map/ppermute | solution.py:44
  168.7 11.8 %collective-permute-start.52 = (bf16[144,576]{1,0:T(8,128)(2,1)S(1)}, bf16[144,576]{1,0:T(8,128)(2,1)S(1)}, u32[]{:S(2)}, u32[]{:S(2)}) collective-permute-start(bf16[144,576]{1,0:T(8,128)(2,1)S(1)} %fusion.15.refs_0_), channel_id=1, source_target_pairs={{0,8},{4,12},{8,0},{12,4},{16,24},{20,28},{24,16},{28,20},{1,9},{5... | collective-permute-start | bytes 497672 | tf_op jit(solution)/shard_map/ppermute | solution.py:44
  169.7 11.9 %collective-permute-start.53 = (bf16[144,576]{1,0:T(8,128)(2,1)S(1)}, bf16[144,576]{1,0:T(8,128)(2,1)S(1)}, u32[]{:S(2)}, u32[]{:S(2)}) collective-permute-start(bf16[144,576]{1,0:T(8,128)(2,1)S(1)} %fusion.15.refs_0_), channel_id=1, source_target_pairs={{0,16},{4,20},{8,24},{12,28},{16,0},{20,4},{24,8},{28,12},{1,17},{... | collective-permute-start | bytes 497672 | tf_op jit(solution)/shard_map/ppermute | solution.py:44
  176.0 6.1 %collective-permute-start.37 = (bf16[216,128]{1,0:T(8,128)(2,1)S(1)}, bf16[216,128]{1,0:T(8,128)(2,1)S(1)}, u32[]{:S(2)}, u32[]{:S(2)}) collective-permute-start(bf16[216,128]{1,0:T(8,128)(2,1)S(1)} %get-tuple-element.175), channel_id=1, source_target_pairs={{0,3},{1,2},{2,1},{3,0},{4,7},{5,6},{6,5},{7,4},{8,11},{9,10},{10,... | collective-permute-start | bytes 165896 | tf_op jit(solution)/shard_map/ppermute | solution.py:44
  177.2 6.0 %collective-permute-start.36 = (bf16[216,128]{1,0:T(8,128)(2,1)S(1)}, bf16[216,128]{1,0:T(8,128)(2,1)S(1)}, u32[]{:S(2)}, u32[]{:S(2)}) collective-permute-start(bf16[216,128]{1,0:T(8,128)(2,1)S(1)} %get-tuple-element.176), channel_id=1, source_target_pairs={{0,2},{1,3},{2,0},{3,1},{4,6},{5,7},{6,4},{7,5},{8,10},{9,11},{10,... | collective-permute-start | bytes 165896 | tf_op jit(solution)/shard_map/ppermute | solution.py:44
  177.2 6.0 %collective-permute-start.35 = (bf16[216,128]{1,0:T(8,128)(2,1)S(1)}, bf16[216,128]{1,0:T(8,128)(2,1)S(1)}, u32[]{:S(2)}, u32[]{:S(2)}) collective-permute-start(bf16[216,128]{1,0:T(8,128)(2,1)S(1)} %get-tuple-element.174), channel_id=1, source_target_pairs={{0,1},{1,0},{2,3},{3,2},{4,5},{5,4},{6,7},{7,6},{8,9},{9,8},{10,11... | collective-permute-start | bytes 165896 | tf_op jit(solution)/shard_map/ppermute | solution.py:44
  180.4 6.4 %collective-permute-start.54 = (bf16[144,576]{1,0:T(8,128)(2,1)S(1)}, bf16[144,576]{1,0:T(8,128)(2,1)S(1)}, u32[]{:S(2)}, u32[]{:S(2)}) collective-permute-start(bf16[144,576]{1,0:T(8,128)(2,1)S(1)} %fusion.15.refs_0_), channel_id=1, source_target_pairs={{0,24},{4,28},{8,16},{12,20},{16,8},{20,12},{24,0},{28,4},{1,25},{... | collective-permute-start | bytes 497672 | tf_op jit(solution)/shard_map/ppermute | solution.py:44
  182.0 6.7 %collective-permute-start.56 = (bf16[144,576]{1,0:T(8,128)(2,1)S(1)}, bf16[144,576]{1,0:T(8,128)(2,1)S(1)}, u32[]{:S(2)}, u32[]{:S(2)}) collective-permute-start(bf16[144,576]{1,0:T(8,128)(2,1)S(1)} %collective-permute-done.52.refs_1_), channel_id=1, source_target_pairs={{0,4},{4,0},{8,12},{12,8},{16,20},{20,16},{24,28},{28,24},{1,5},{5... | collective-permute-start | bytes 497672 | tf_op jit(solution)/shard_map/ppermute | solution.py:44
  183.2 6.7 %collective-permute-start.57 = (bf16[144,576]{1,0:T(8,128)(2,1)S(1)}, bf16[144,576]{1,0:T(8,128)(2,1)S(1)}, u32[]{:S(2)}, u32[]{:S(2)}) collective-permute-start(bf16[144,576]{1,0:T(8,128)(2,1)S(1)} %collective-permute-done.53.refs_2_), channel_id=1, source_target_pairs={{0,4},{4,0},{8,12},{12,8},{16,20},{20,16},{24,28},{28,24},{1,5},{5... | collective-permute-start | bytes 497672 | tf_op jit(solution)/shard_map/ppermute | solution.py:44
  183.2 6.7 %collective-permute-start.38 = (bf16[216,128]{1,0:T(8,128)(2,1)S(1)}, bf16[216,128]{1,0:T(8,128)(2,1)S(1)}, u32[]{:S(2)}, u32[]{:S(2)}) collective-permute-start(bf16[216,128]{1,0:T(8,128)(2,1)S(1)} %fusion.20.refs_0_), channel_id=1, source_target_pairs={{0,8},{4,12},{8,0},{12,4},{16,24},{20,28},{24,16},{28,20},{1,9},{5... | collective-permute-start | bytes 165896 | tf_op jit(solution)/shard_map/ppermute | solution.py:44
  186.9 7.4 %collective-permute-start.39 = (bf16[216,128]{1,0:T(8,128)(2,1)S(1)}, bf16[216,128]{1,0:T(8,128)(2,1)S(1)}, u32[]{:S(2)}, u32[]{:S(2)}) collective-permute-start(bf16[216,128]{1,0:T(8,128)(2,1)S(1)} %fusion.20.refs_0_), channel_id=1, source_target_pairs={{0,16},{4,20},{8,24},{12,28},{16,0},{20,4},{24,8},{28,12},{1,17},{... | collective-permute-start | bytes 165896 | tf_op jit(solution)/shard_map/ppermute | solution.py:44
  189.9 6.3 %collective-permute-start.41 = (bf16[216,128]{1,0:T(8,128)(2,1)S(1)}, bf16[216,128]{1,0:T(8,128)(2,1)S(1)}, u32[]{:S(2)}, u32[]{:S(2)}) collective-permute-start(bf16[216,128]{1,0:T(8,128)(2,1)S(1)} %fusion.20.refs_0_), channel_id=1, source_target_pairs={{0,4},{4,0},{8,12},{12,8},{16,20},{20,16},{24,28},{28,24},{1,5},{5... | collective-permute-start | bytes 165896 | tf_op jit(solution)/shard_map/ppermute | solution.py:44
  190.0 6.3 %collective-permute-start.42 = (bf16[216,128]{1,0:T(8,128)(2,1)S(1)}, bf16[216,128]{1,0:T(8,128)(2,1)S(1)}, u32[]{:S(2)}, u32[]{:S(2)}) collective-permute-start(bf16[216,128]{1,0:T(8,128)(2,1)S(1)} %collective-permute-done.38.refs_1_), channel_id=1, source_target_pairs={{0,4},{4,0},{8,12},{12,8},{16,20},{20,16},{24,28},{28,24},{1,5},{5... | collective-permute-start | bytes 165896 | tf_op jit(solution)/shard_map/ppermute | solution.py:44
  192.5 14.0 %collective-permute-start.34 = (bf16[256,384]{1,0:T(8,128)(2,1)S(1)}, bf16[256,384]{1,0:T(8,128)(2,1)S(1)}, u32[]{:S(2)}, u32[]{:S(2)}) collective-permute-start(bf16[256,384]{1,0:T(8,128)(2,1)S(1)} %copy-done.33), channel_id=1, source_target_pairs={{0,24},{4,28},{8,16},{12,20},{16,8},{20,12},{24,0},{28,4},{1,25},{... | collective-permute-start | bytes 589832 | tf_op jit(solution)/shard_map/ppermute | solution.py:44
  194.3 12.3 %collective-permute-start.33 = (bf16[256,384]{1,0:T(8,128)(2,1)S(1)}, bf16[256,384]{1,0:T(8,128)(2,1)S(1)}, u32[]{:S(2)}, u32[]{:S(2)}) collective-permute-start(bf16[256,384]{1,0:T(8,128)(2,1)S(1)} %copy-done.32), channel_id=1, source_target_pairs={{0,16},{4,20},{8,24},{12,28},{16,0},{20,4},{24,8},{28,12},{1,17},{... | collective-permute-start | bytes 589832 | tf_op jit(solution)/shard_map/ppermute | solution.py:44
  194.7 11.9 %collective-permute-start.32 = (bf16[256,384]{1,0:T(8,128)(2,1)S(1)}, bf16[256,384]{1,0:T(8,128)(2,1)S(1)}, u32[]{:S(2)}, u32[]{:S(2)}) collective-permute-start(bf16[256,384]{1,0:T(8,128)(2,1)S(1)} %copy-done.31), channel_id=1, source_target_pairs={{0,8},{4,12},{8,0},{12,4},{16,24},{20,28},{24,16},{28,20},{1,9},{5... | collective-permute-start | bytes 589832 | tf_op jit(solution)/shard_map/ppermute | solution.py:44
  196.2 7.2 %collective-permute-start.43 = (bf16[216,128]{1,0:T(8,128)(2,1)S(1)}, bf16[216,128]{1,0:T(8,128)(2,1)S(1)}, u32[]{:S(2)}, u32[]{:S(2)}) collective-permute-start(bf16[216,128]{1,0:T(8,128)(2,1)S(1)} %collective-permute-done.39.refs_2_), channel_id=1, source_target_pairs={{0,4},{4,0},{8,12},{12,8},{16,20},{20,16},{24,28},{28,24},{1,5},{5... | collective-permute-start | bytes 165896 | tf_op jit(solution)/shard_map/ppermute | solution.py:44
  196.3 7.2 %collective-permute-start.44 = (bf16[216,128]{1,0:T(8,128)(2,1)S(1)}, bf16[216,128]{1,0:T(8,128)(2,1)S(1)}, u32[]{:S(2)}, u32[]{:S(2)}) collective-permute-start(bf16[216,128]{1,0:T(8,128)(2,1)S(1)} %collective-permute-done.40.refs_3_), channel_id=1, source_target_pairs={{0,4},{4,0},{8,12},{12,8},{16,20},{20,16},{24,28},{28,24},{1,5},{5... | collective-permute-start | bytes 165896 | tf_op jit(solution)/shard_map/ppermute | solution.py:44
  (69 other events, 606.5 us)

commit v3 on v2

--- a/solution.py
+++ b/solution.py
@@ -59,6 +59,22 @@
         pieces = [jnp.where(flag, pieces[i ^ bit], pieces[i]) for i in range(len(pieces))]
         bit = bit * 2
     return pieces
+
+
+def in_order(own, other, offset):
+    flag = (lax.axis_index("fsdp") & offset) != 0
+    return jnp.concatenate([jnp.where(flag, other, own), jnp.where(flag, own, other)], axis=0)
+
+
+def start_gather_rows(piece, *others):
+    count = lax.axis_size("fsdp")
+    values = piece[None]
+    offset = 1
+    while offset < count // 2:
+        values = in_order(values, swap(values, "fsdp", offset), offset)
+        offset = offset * 2
+    values = after(values, *others)
+    return values, swap(values, "fsdp", offset)
 
 
 def gather_rows(piece, *others):
@@ -78,18 +94,15 @@
     return values
 
 
-def gather_half(piece, *others):
-    half = lax.axis_size("fsdp") // 2
-    index = lax.axis_index("fsdp")
+def start_gather_half(piece):
     received = lax.ppermute(piece, ("ctx", "fsdp"), half_pairs())
-    values = after(jnp.where(in_half(), piece, received)[None], *others)
+    return jnp.where(in_half(), piece, received)[None]
+
+
+def finish_gather_half(values):
     offset = 1
-    while offset < half:
-        other = swap(values, "fsdp", offset)
-        flag = (index & offset) != 0
-        values = jnp.concatenate(
-            [jnp.where(flag, other, values), jnp.where(flag, values, other)], axis=0
-        )
+    while offset < lax.axis_size("fsdp") // 2:
+        values = in_order(values, swap(values, "fsdp", offset), offset)
         offset = offset * 2
     return values
 
@@ -225,7 +238,9 @@
                     [part[:, m * (TILE // 2) : (m + 1) * (TILE // 2)] for part in pair], axis=1
                 )
         out[:, chips * TILE :] = whole[:, used:]
-        gain_grad[...] = gain_gradient(whole[...] * shard_ref[...].astype(jnp.float32), gain_ref[...])
+        terms = whole[...] * shard_ref[...].astype(jnp.float32)
+        lane = lax.broadcasted_iota(jnp.int32, terms.shape, 1)
+        gain_grad[...] = gain_gradient(jnp.where(lane < used, terms, 0.0), gain_ref[...])
 
     return run_kernel(
         kernel,
@@ -251,7 +266,7 @@
 
     def kernel(*refs):
         gate_ref, up_ref, gain_ref = refs[count : count + 3]
-        gate, up, down, gain_grad, total = refs[count + 3 :]
+        gate, up, down, gain_grad, total, low = refs[count + 3 :]
         chip, core = rank()
         total[...] = jnp.zeros_like(total)
         for n in range(count):
@@ -268,9 +283,10 @@
 
             start = pl.multiple_of((to_chip * 2 + to_core) * down_rows, 16)
             for m in range(pile):
-                down[pl.ds(start, down_rows), m * low_lanes : (m + 1) * low_lanes] = refs[n][
+                low[pl.ds(start, down_rows), m * low_lanes : (m + 1) * low_lanes] = refs[n][
                     m * down_rows : (m + 1) * down_rows, lanes:
                 ].astype(jnp.float32)
+        down[...] = low[...].T
         gain_grad[...] = gain_gradient(total[...], gain_ref[...])
 
     return run_kernel(
@@ -278,11 +294,14 @@
         [
             ((rows, ff), jnp.float32),
             ((rows, ff), jnp.float32),
-            ((count * down_rows, D), jnp.float32),
+            ((D, count * down_rows), jnp.float32),
             ((1, rows), jnp.float32),
         ],
         [*pieces, w_gate, w_up, gain],
-        scratch=[pltpu.VMEM((rows, lanes), jnp.float32)],
+        scratch=[
+            pltpu.VMEM((rows, lanes), jnp.float32),
+            pltpu.VMEM((count * down_rows, D), jnp.float32),
+        ],
     )
 
 
@@ -364,12 +383,30 @@
         query_ref, pairs_ref = refs[len(first) : len(first) + 2]
         chip, core = rank()
         if direct:
-            mixed_ref = refs[-1]
+            mixed_ref, out_w_ref = refs[-2:]
             for n in range(count):
                 c = (chip ^ (n % chips)) * 2 + (core ^ (n // chips))
                 columns = pl.ds(pl.multiple_of(c * TILE, TILE), TILE)
                 for z in range(shards):
                     mixed_ref[z * rows : (z + 1) * rows, columns] = first_refs[n][z, :rows, :]
+            for n in range(chips):
+                columns = pl.ds(pl.multiple_of((chip ^ n) * TILE, TILE), TILE)
+                for z in range(shards):
+                    pair = both_cores(
+                        first_refs[n][z, rows : rows + rows // 2, :].astype(jnp.float32),
+                        first_refs[n + chips][z, rows : rows + rows // 2, :].astype(jnp.float32),
+                        core,
+                    )
+                    half = TILE // 2
+                    block = jnp.concatenate(
+                        [
+                            jnp.concatenate([part[:, m * half : (m + 1) * half] for part in pair], axis=1)
+                            for m in range(2)
+                        ],
+                        axis=0,
+                    )
+                    out_w_ref[z * rows : (z + 1) * rows, columns] = block.astype(jnp.bfloat16)
+            out_w_ref[:, chips * TILE :] = mixed_ref[:, 2 * KV_WIDTH + D :]
         else:
             mixed_ref = first_refs[0]
         for n in range(chips):
@@ -394,11 +431,11 @@
 
     outs = [((row_count, D), jnp.bfloat16), ((chips, row_count, 2 * KV_WIDTH), jnp.bfloat16)]
     if direct:
-        outs += [((D, columns_all), jnp.bfloat16)]
+        outs += [((D, columns_all), jnp.bfloat16), ((D, D), jnp.bfloat16)]
     result = run_kernel(
         kernel, outs, [table, hidden_half, cos_all, sin_all, *first], scalars=1, microseconds=5
     )
-    return result if direct else (*result, first[0])
+    return result if direct else (*result, *first)
 
 
 def natural_order(out, table_ref, halves):
@@ -500,24 +537,12 @@
     )
 
 
-def fill_out_weights(out_w_ref, own_ref, other_ref, down_rows):
-    _, core = rank()
-    half, rows, _ = other_ref.shape
-    for n in range(half):
-        pair = both_cores(own_ref[n, down_rows:, :], other_ref[n], core)
-        for owner in range(2):
-            start = (owner * half + n) * rows
-            out_w_ref[start : start + rows, :] = pair[owner]
-
-
-def mix(attended, tokens, low_own, out_other, gain):
+def mix(attended, tokens, out_w, gain):
     row_count = tokens.shape[0]
-    down_rows = low_own.shape[1] - out_other.shape[1]
 
     def kernel(
-        attended_ref, tokens_ref, own_ref, other_ref, gain_ref, residual_ref, hidden_ref, out_w_ref
+        attended_ref, tokens_ref, out_w_ref, gain_ref, residual_ref, hidden_ref
     ):
-        fill_out_weights(out_w_ref, own_ref, other_ref, down_rows)
         attn_low = attended_ref[...].astype(jnp.bfloat16)
         residual = tokens_ref[...].astype(jnp.float32) + dot(attn_low, out_w_ref[...])
         residual_ref[...] = residual
@@ -526,8 +551,7 @@
     return run_kernel(
         kernel,
         [((row_count, D), jnp.float32), ((row_count, D), jnp.bfloat16)],
-        [attended, tokens, low_own, out_other, gain],
-        scratch=[pltpu.VMEM((D, D), jnp.bfloat16)],
+        [attended, tokens, out_w, gain],
         microseconds=2,
     )
 
@@ -552,7 +576,7 @@
         wide_ref, gate_grad_ref, down_ref, low_ref_f32 = refs[-4:]
         chip, _ = rank()
         for n in range(half):
-            down_ref[n * down_rows : (n + 1) * down_rows, :] = low_ref[n, :down_rows, :]
+            down_ref[n * down_rows : (n + 1) * down_rows, :] = low_ref[n]
         if direct:
             for i in range(chips):
                 q = chip ^ i
@@ -595,8 +619,9 @@
                 refs[5][columns, :] = low.astype(jnp.bfloat16)
         out_ref[...] = result[:row_count]
         hidden_grad_ref[...] = grad_hidden[:row_count]
-        sent_ref[0] = result[row_count:].astype(jnp.bfloat16)
-        sent_ref[1] = grad_hidden[row_count:].astype(jnp.bfloat16)
+        sent_ref[:, :, D:] = jnp.zeros((2, row_count, -D % TILE), jnp.bfloat16)
+        sent_ref[0, :, :D] = result[row_count:].astype(jnp.bfloat16)
+        sent_ref[1, :, :D] = grad_hidden[row_count:].astype(jnp.bfloat16)
         if direct:
             for i in range(chips):
                 q = chip ^ i
@@ -612,7 +637,7 @@
     outs = [
         ((row_count, D), jnp.float32),
         ((row_count, D), jnp.float32),
-        ((2, row_count, D), jnp.bfloat16),
+        ((2, row_count, -(-D // TILE) * TILE), jnp.bfloat16),
     ]
     outs += (
         [((shards, rows, lanes + D // pile), jnp.bfloat16)] * chips
@@ -634,10 +659,9 @@
 
 
 def unmix(
-    residual, out_kept, grad_kept, received, grad_out, attended, low_own, out_other, gain
+    residual, out_kept, grad_kept, received, grad_out, attended, out_w, gain
 ):
     row_count = residual.shape[0]
-    down_rows = low_own.shape[1] - out_other.shape[1]
 
     def kernel(
         residual_ref,
@@ -646,20 +670,17 @@
         received_ref,
         grad_out_ref,
         attended_ref,
-        own_ref,
-        other_ref,
+        out_w_ref,
         gain_ref,
         output_ref,
         residual_grad_ref,
         attended_grad_ref,
         out_grad_ref,
-        out_w_ref,
     ):
-        fill_out_weights(out_w_ref, own_ref, other_ref, down_rows)
         residual = residual_ref[...]
-        result = residual + out_kept_ref[...] + received_ref[0].astype(jnp.float32)
-        output_ref[...] = result.astype(jnp.bfloat16)
-        grad_hidden = grad_kept_ref[...] + received_ref[1].astype(jnp.float32)
+        result = residual + out_kept_ref[...] + received_ref[0, :, :D].astype(jnp.float32)
+        output_ref[...] = result.astype(jnp.bfloat16).T
+        grad_hidden = grad_kept_ref[...] + received_ref[1, :, :D].astype(jnp.float32)
         inv_two = inverse_root(residual)
         residual_grad = grad_out_ref[...].astype(jnp.float32) + norm_back(
             grad_hidden, residual * inv_two, inv_two, gain_ref[...]
@@ -674,7 +695,7 @@
     return run_kernel(
         kernel,
         [
-            ((row_count, D), jnp.bfloat16),
+            ((D, row_count), jnp.bfloat16),
             ((row_count, D), jnp.float32),
             ((row_count, D), jnp.bfloat16),
             ((D, D), jnp.bfloat16),
@@ -686,11 +707,9 @@
             received,
             grad_out,
             attended,
-            low_own,
-            out_other,
+            out_w,
             gain,
         ],
-        scratch=[pltpu.VMEM((D, D), jnp.bfloat16)],
         microseconds=4,
     )
 
@@ -709,6 +728,7 @@
     sin_all,
     cos_own,
     sin_own,
+    hidden_half,
 ):
     row_count = query_rot.shape[0]
     block_len = row_count // 2
@@ -732,12 +752,14 @@
         sin_ref,
         cos_own_ref,
         sin_own_ref,
-        query_t_ref,
+        hidden_ref,
+        query_grad_ref,
+        query_w_ref,
         kept_ref,
-        sent_ref,
-        pairs_ref,
-        pair_grad_ref,
+        *refs,
     ):
+        sent_refs = refs[:chips]
+        pairs_ref, pair_grad_ref, query_t_ref = refs[chips:]
         natural_order(pairs_ref, table_ref, (own_ref, other_ref))
         pair_grad_ref[...] = jnp.zeros_like(pair_grad_ref)
         for b in range(2):
@@ -798,20 +820,23 @@
                         (bottom * cos_part - top * sin_part) * HEAD ** (-0.5)
                     ).astype(jnp.bfloat16)
 
+        query_grad_ref[...] = query_t_ref[...].T
+        query_w_ref[...] = dot(query_t_ref[...], hidden_ref[0]).T.astype(jnp.bfloat16)
         chip, core = rank()
         for i in range(chips):
-            for ref, to_core in ((kept_ref, core), (sent_ref, 1 - core)):
+            for ref, to_core in ((kept_ref.at[i], core), (sent_refs[i], 1 - core)):
                 block = table_ref[(chip ^ i) * 2 + to_core]
                 for part, place in ((0, block), (1, 2 * slots - 1 - block)):
                     source = pl.ds(pl.multiple_of(place * block_len, block_len), block_len)
-                    ref[i, part * block_len : (part + 1) * block_len, :] = turn_pairs(
+                    ref[part * block_len : (part + 1) * block_len, :] = turn_pairs(
                         pair_grad_ref[source, :], cos_ref[source, :], -sin_ref[source, :]
                     ).astype(jnp.bfloat16)
 
     half_shape = ((chips, row_count, 2 * KV_WIDTH), jnp.bfloat16)
     return run_kernel(
         kernel,
-        [((D, row_count), jnp.bfloat16), half_shape, half_shape],
+        [((row_count, D), jnp.bfloat16), ((D, D), jnp.bfloat16), half_shape]
+        + [((row_count, 2 * KV_WIDTH), jnp.bfloat16)] * chips,
         [
             bounds,
             table,
@@ -826,28 +851,15 @@
             sin_all,
             cos_own,
             sin_own,
+            hidden_half,
         ],
         scalars=2,
         scratch=[
             pltpu.VMEM((slots * row_count, 2 * KV_WIDTH), jnp.bfloat16),
             pltpu.VMEM((slots * row_count, 2 * KV_WIDTH), jnp.float32),
+            pltpu.VMEM((D, row_count), jnp.bfloat16),
         ],
-        microseconds=16,
-    )
-
-
-def query_gradients(query_t, hidden_half):
-    row_count = query_t.shape[1]
-
-    def kernel(query_t_ref, hidden_ref, query_ref, weight_ref):
-        query_ref[...] = query_t_ref[...].T
-        weight_ref[...] = dot(query_t_ref[...], hidden_ref[0]).T.astype(jnp.bfloat16)
-
-    return run_kernel(
-        kernel,
-        [((row_count, D), jnp.bfloat16), ((D, D), jnp.bfloat16)],
-        [query_t, hidden_half],
-        microseconds=2,
+        microseconds=18,
     )
 
 
@@ -857,15 +869,22 @@
     columns_all = 2 * KV_WIDTH + D + HEAD
     rows = D // shards
 
-    def kernel(kept_ref, received_ref, hidden_ref, query_w_ref, out_grad_ref, *refs):
+    def kernel(kept_ref, hidden_ref, query_w_ref, out_grad_ref, *refs):
+        received_refs, refs = refs[:chips], refs[chips:]
         pair_refs, outs = refs[:chips], refs[chips:-1]
         mixed_ref = refs[-1]
         total = jnp.zeros((2 * KV_WIDTH, D), jnp.float32)
         for i in range(chips):
             pairs = (
-                kept_ref[i].astype(jnp.float32) + received_ref[i].astype(jnp.float32)
+                kept_ref[i].astype(jnp.float32) + received_refs[i][...].astype(jnp.float32)
             ).astype(jnp.bfloat16)
-            pair_refs[i][...] = pairs
+            if direct:
+                for n in range(2 * KV_WIDTH // TILE):
+                    pair_refs[i][n * row_count : (n + 1) * row_count, :] = pairs[
+                        :, n * TILE : (n + 1) * TILE
+                    ]
+            else:
+                pair_refs[i][...] = pairs
             total += dot_tn(pairs, hidden_ref[i])
         mixed_ref[:, : 2 * KV_WIDTH] = total.T.astype(jnp.bfloat16)
         mixed_ref[:, 2 * KV_WIDTH : 2 * KV_WIDTH + D] = query_w_ref[...]
@@ -885,7 +904,8 @@
                 outs[n][z, rows:, : TILE // 2] = unit[z * rows : middle]
                 outs[n][z, rows:, TILE // 2 :] = unit[middle : (z + 1) * rows]
 
-    outs = [((row_count, 2 * KV_WIDTH), jnp.bfloat16)] * chips
+    tiles = 2 * KV_WIDTH // TILE if direct else 1
+    outs = [((row_count * tiles, 2 * KV_WIDTH // tiles), jnp.bfloat16)] * chips
     outs += (
         [((shards, rows + rows // 2, TILE), jnp.bfloat16)] * (2 * chips)
         if direct
@@ -894,9 +914,9 @@
     result = run_kernel(
         kernel,
         outs,
-        [kept, received, hidden_half, query_w, out_grad],
+        [kept, hidden_half, query_w, out_grad, *received],
         scratch=[pltpu.VMEM((D, columns_all), jnp.bfloat16)],
-        microseconds=3,
+        microseconds=0,
     )
     return result[:chips], result[chips:]
 
@@ -930,35 +950,39 @@
     )
 
     mixed_shard = jnp.concatenate(
-        [w_key, w_value, w_query, jnp.zeros((rows, HEAD), jnp.bfloat16)], axis=1
+        [w_key, w_value, w_query, w_out[:, D - HEAD :]], axis=1
     )
     piece = first_piece(mixed_shard, index, count)
+    unit = first_piece(w_out[:, : D - HEAD], index, count)
+    unit = jnp.concatenate([unit[: rows // 2], unit[rows // 2 :]], axis=1)
     gains = jnp.concatenate([attn_gain, ffn_gain])
     gains = jnp.pad(gains, (0, 16 * piece.shape[1] - 2 * rows)).reshape(16, piece.shape[1])
     tokens_low = layer_input[0]
     token_pieces = [tokens_low] + [chip_swap(tokens_low, i) for i in range(1, chips)]
-    first_rows = gather_rows(jnp.concatenate([piece, gains], axis=0))
-    gains_all = first_rows[:, rows:].reshape(shards, -1).astype(jnp.float32)
+    first_rows = gather_rows(jnp.concatenate([piece, unit, gains], axis=0))
+    gains_all = first_rows[:, rows + rows // 2 :].reshape(shards, -1).astype(jnp.float32)
     gain_one = gains_all[:, :rows].reshape(1, D)
     gain_two = gains_all[:, rows : 2 * rows].reshape(1, D)
     hidden_half = normalize(token_pieces, gain_one)
     first_own = gather_same_core(after(first_rows, hidden_half))
+    wide_own, wide_received = start_gather_rows(
+        wide_piece(w_gate, w_up, chip, core, chips), first_rows
+    )
+    low_start = start_gather_half(after(w_down, hidden_half))
     first_pieces = first_own + [core_swap(v) for v in first_own]
-    wide_rows = gather_rows(wide_piece(w_gate, w_up, chip, core, chips), first_rows)
-    low_shard = after(jnp.concatenate([w_down, w_out], axis=0), wide_rows)
-    wide_pieces = gather_same_core(wide_rows)
-    low_own = gather_half(low_shard)
-    out_other = core_swap(low_own[:, w_down.shape[0] :])
-    grad_out = cotangent[0]
-    first = (
-        first_pieces
-        if direct
-        else [
-            jnp.concatenate(
-                [v[:, :rows].reshape(D, -1) for v in in_rank_order(first_pieces)], axis=1
-            )
+    if direct:
+        first = first_pieces
+    else:
+        ordered = in_rank_order(first_pieces)
+        mixed_all = jnp.concatenate([v[:, :rows].reshape(D, -1) for v in ordered], axis=1)
+        units = [
+            v[:, rows : rows + rows // 2]
+            .reshape(shards, rows // 2, 2, -1)
+            .transpose(0, 2, 1, 3)
+            .reshape(D, -1)
+            for v in ordered
         ]
-    )
+        first = [mixed_all, jnp.concatenate([*units, mixed_all[:, 2 * KV_WIDTH + D :]], axis=1)]
 
     own_block = lax.dynamic_index_in_dim(slot_table, index, 0, keepdims=False)
     own_blocks = jnp.stack([own_block, 2 * count - 1 - own_block])
@@ -976,22 +1000,27 @@
     bounds = jnp.stack(
         [jnp.min(first_key, axis=1) // row_count, own_blocks // 2 + 1], axis=1
     ).reshape(4)
-    frequencies = rope_base ** (-(jnp.arange(HEAD // 2, dtype=jnp.float32) * 2.0 / HEAD))
+    half_width = after(jnp.arange(HEAD // 2, dtype=jnp.float32), hidden_half)
+    frequencies = rope_base ** (-(half_width * 2.0 / HEAD))
     angles = jnp.arange(length, dtype=jnp.int32).astype(jnp.float32)[:, None] * frequencies[None, :]
     cos_all = jnp.tile(jnp.cos(angles), (1, 2 * TILE // HEAD))
     sin_all = jnp.tile(jnp.sin(angles), (1, 2 * TILE // HEAD))
     own_angles = frequencies[:, None] * block_pos.reshape(1, row_count).astype(jnp.float32)
     cos_own, sin_own = jnp.cos(own_angles), jnp.sin(own_angles)
 
-    query_rot, own_pairs, mixed = project(
-        direct, slot_table, hidden_half, first, cos_all, sin_all
+    wide_rows = in_order(wide_own, wide_received, shards // 2)
+    query_rot, own_pairs, mixed, out_w_all = project(
+        direct, slot_table, after(hidden_half, wide_rows, low_start, bounds, first_key, block_pos, cos_own, sin_own), first, cos_all, sin_all
     )
     pair_halves = (own_pairs, core_swap(own_pairs))
+    wide_pieces = gather_same_core(wide_rows)
+    low_own = finish_gather_half(after(low_start, wide_rows))
+    grad_out = cotangent[0]
     attended, log_total = attention_forward(
         bounds, slot_table, query_rot, pair_halves, first_key, block_pos
     )
     grad_other = core_swap(after(grad_out, attended))
-    residual, hidden_two = mix(attended, tokens_low, low_own, out_other, gain_two)
+    residual, hidden_two = mix(attended, tokens_low, out_w_all, gain_two)
     if direct:
         wide = wide_pieces
     else:
@@ -1037,12 +1066,11 @@
         core_swap(sent),
         grad_out,
         attended,
-        low_own,
-        out_other,
+        out_w_all,
         gain_two,
     )
 
-    query_t, pairs_kept, pairs_sent = attention_backward(
+    grad_query, query_w, pairs_kept, *pairs_sent = attention_backward(
         bounds,
         slot_table,
         query_rot,
@@ -1056,9 +1084,9 @@
         sin_all,
         cos_own,
         sin_own,
-    )
-    pairs_received = core_swap(pairs_sent)
-    grad_query, query_w = query_gradients(query_t, hidden_half)
+        hidden_half,
+    )
+    pairs_received = [core_swap(v) for v in pairs_sent]
     pair_sums, mixed_grads = first_gradients(
         direct, pairs_kept, pairs_received, hidden_half, query_w, out_grad, shards
     )
@@ -1078,16 +1106,28 @@
             for c, unit in zip(targets, units)
         ]
     mixed_sums = [sum_cores(*pair) for pair in zip(mixed_grads[:chips], mixed_grads[chips:])]
-    first_sum = sum_chips(mixed_sums).astype(jnp.bfloat16)
+    if direct:
+        shape = mixed_sums[0].shape
+        split = shape[0] * shape[1]
+        both_sum = sum_chips(
+            [
+                jnp.concatenate([one.reshape(split, TILE), other], axis=0)
+                for one, other in zip(mixed_sums, pair_sums)
+            ]
+        ).astype(jnp.bfloat16)
+        first_sum = both_sum[:split].reshape(shape)
+        owned = jnp.concatenate(jnp.split(both_sum[split:], 2 * KV_WIDTH // TILE), axis=1)
+    else:
+        first_sum = sum_chips(mixed_sums).astype(jnp.bfloat16)
+        owned = sum_chips(pair_sums).astype(jnp.bfloat16)
     first_part = sum_rows(first_sum).astype(jnp.bfloat16)
     first_all = gather_chips(first_part)
-    wide_sum = sum_chips(wide_grads, query_t).astype(jnp.bfloat16)
+    wide_sum = sum_chips(wide_grads, pair_sums[0]).astype(jnp.bfloat16)
     wide_sum = jnp.concatenate(
         [wide_sum[:, :, :lanes], by_core_slices(wide_sum[:, :, lanes:])], axis=2
     )
-    wide_part = sum_rows(wide_sum).astype(jnp.bfloat16)
+    wide_part = sum_rows(after(wide_sum, mixed_sums)).astype(jnp.bfloat16)
     wide_all = gather_chips(wide_part)
-    owned = sum_chips(after(tuple(pair_sums), first_sum)).astype(jnp.bfloat16)
     grad_hidden_one = dot_nt(
         jnp.concatenate([owned, grad_query], axis=1), mixed[:, : 2 * KV_WIDTH + D]
     )
@@ -1102,6 +1142,7 @@
         gate_grad, up_grad, down_grad, gain_grad_two = finish_wide(
             wide_all, w_gate, w_up, gain_rows[1], pile
         )
+        down_grad = down_grad.T
         query_w, key_w, value_w, out_w, gain_grad_one = finish_first(
             first_all, mixed_shard, gain_rows[0]
         )
@@ -1142,7 +1183,7 @@
             / gain_rows[1]
         )
     return (
-        output[None],
+        output.T[None],
         grad_input[None],
         query_w,
         key_w,

time: 209 us -> 190 us (0.909)
  waiting for transfers between devices: 56.5 us -> 24.3 us
  starting transfers between devices: 60.5 us -> 73 us
  other arithmetic: 11.7 us -> 13.8 us
    ppermute x58 -> x57, waiting for transfers between devices: 56.5 us -> 23.9 us  [swap(): return lax.ppermute(value, axis, [(i, i ^ offset) for i in range(count)])]
    ppermute x58 -> x57, starting transfers between devices: 59 us -> 69.6 us  [swap(): return lax.ppermute(value, axis, [(i, i ^ offset) for i in range(count)])]
    convert_element_type x4 -> x3, other arithmetic: 0.74 us -> 2.95 us  [the longest x1 1.39 us: local(): both_sum = sum_chips([jnp.concatenate([one.reshape(split, TILE), other],...]
    ppermute x1 -> x0, local copies, waits for them, and re-layouts: 2.17 us -> none  [swap(): return lax.ppermute(value, axis, [(i, i ^ offset) for i in range(count)])]
    pallas_call x11 -> x10, Pallas kernels: 57.4 us -> 56.4 us  [run_kernel(): pl.pallas_call(kernel, out_shape=tuple((jax.ShapeDtypeStruct(*out) for ou...]
    unnamed x121 -> x124, local copies, waits for them, and re-layouts: 9.94 us -> 10.6 us
  transfers between devices with their start and end apart: 59 -> 58, of which waited for: 16 -> 19; matrix products, arithmetic and copies ran while one was open for 11% -> 12% of each run, Pallas kernels for 20% -> 20%
where the time goes in v3:
time: 190 us; the launch traced here: 189 us
  starting transfers between devices  73 us (38%)
  Pallas kernels  56.4 us (30%)
  waiting for transfers between devices  24.3 us (13%)
  local copies, waits for them, and re-layouts  18.3 us (10%)
  other arithmetic  13.8 us (7%)
  between operations  2.8 us (1%)
    ppermute x57, starting transfers between devices, swap(): return lax.ppermute(value, axis, [(i, i ^ offset) for i in range(count)])  69.6 us
    pallas_call x10, Pallas kernels, run_kernel(): pl.pallas_call(kernel, out_shape=tuple((jax.ShapeDtypeStruct(*out) for ou...  56.4 us
    ppermute x57, waiting for transfers between devices, swap(): return lax.ppermute(value, axis, [(i, i ^ offset) for i in range(count)])  23.9 us
    unnamed x124, local copies, waits for them, and re-layouts  10.6 us
  transfers between devices with their start and end apart: 58, of which 19 were waited for; matrix products, arithmetic and copies ran while one was open for 12% of the time, Pallas kernels for 20%

profile of v3, /device:TPU:0, one launch (start us, length us, event | category | flops | bytes accessed | tf_op | source)
XLA Modules:
  0.0 189.4 jit_solution(5021834491322091768)
XLA Ops:
  0.7 1.2 copy.47
  1.9 3.0 %collective-permute-start = (bf16[256,576]{1,0:T(8,128)(2,1)S(1)}, bf16[256,576]{1,0:T(8,128)(2,1)S(1)}, u32[]{:S(2)}, u32[]{:S(2)}) collective-permute-start(bf16[256,576]{1,0:T(8,128)(2,1)S(1)} %bitcast.82), channel_id=1, source_target_pairs={{0,8},{4,12},{8,0},{12,4},{16,24},{20,28},{24,16},{28,20},{1,9},{5... | collective-permute-start | bytes 884744 | tf_op jit(solution)/shard_map/ppermute | solution.py:44
  4.9 1.5 collective-permute-start.1
  10.0 2.0 %collective-permute-start.3 = (bf16[1,232,128]{2,1,0:T(8,128)(2,1)S(1)}, bf16[1,232,128]{2,1,0:T(8,128)(2,1)S(1)}, u32[]{:S(2)}, u32[]{:S(2)}) collective-permute-start(bf16[1,232,128]{2,1,0:T(8,128)(2,1)S(1)} %maximum_bitcast_fusion), channel_id=1, source_target_pairs={{0,1},{1,0},{2,3},{3,2},{4,5},{5,4},{6,7},{7,6},{8,9},{9,8},{10,11... | collective-permute-start | bytes 178184 | tf_op jit(solution)/shard_map/ppermute | solution.py:44
  18.5 3.0 %collective-permute-start.4 = (bf16[2,232,128]{2,1,0:T(8,128)(2,1)S(1)}, bf16[2,232,128]{2,1,0:T(8,128)(2,1)S(1)}, u32[]{:S(2)}, u32[]{:S(2)}) collective-permute-start(bf16[2,232,128]{2,1,0:T(8,128)(2,1)S(1)} %pad_maximum_fusion.8), channel_id=1, source_target_pairs={{0,2},{1,3},{2,0},{3,1},{4,6},{5,7},{6,4},{7,5},{8,10},{9,11},{10,... | collective-permute-start | bytes 356360 | tf_op jit(solution)/shard_map/ppermute | solution.py:44
  21.7 4.3 %collective-permute-done.4 = bf16[2,232,128]{2,1,0:T(8,128)(2,1)S(1)} collective-permute-done((bf16[2,232,128]{2,1,0:T(8,128)(2,1)S(1)}, bf16[2,232,128]{2,1,0:T(8,128)(2,1)S(1)}, u32[]{:S(2)}, u32[]{:S(2)}) %collective-permute-start.4) | collective-permute-done | bytes 118816 | tf_op jit(solution)/shard_map/ppermute | solution.py:44
  26.8 1.5 collective-permute-start.6
  29.2 2.9 %shard_map.212.hidden_ref = bf16[4,256,576]{2,1,0:T(8,128)(2,1)} custom-call(bf16[256,576]{1,0:T(8,128)(2,1)} %bitcast.85, bf16[256,576]{1,0:T(8,128)(2,1)} %copy-done.32, bf16[256,576]{1,0:T(8,128)(2,1)} %copy-done.33, bf16[256,576]{1,0:T(8,128)(2,1)} %collective-permute-done.2.refs_3_, f32[1,576]{1,0:T(1,128)} %reshape.396.refs_4_), custom_call_target="tpu_custom_call" | custom-call | flops 3449999872 | bytes 1024 | tf_op jit(solution)/shard_map/pallas_call | solution.py:24
  32.0 1.5 collective-permute-start.8
  33.5 1.5 collective-permute-start.9
  35.8 3.4 %collective-permute-start.7 = (bf16[384,576]{1,0:T(8,128)(2,1)S(1)}, bf16[384,576]{1,0:T(8,128)(2,1)S(1)}, u32[]{:S(2)}, u32[]{:S(2)}) collective-permute-start(bf16[384,576]{1,0:T(8,128)(2,1)S(1)} %copy.49), channel_id=1, source_target_pairs={{0,2},{1,3},{6,4},{7,5},{8,10},{9,11},{14,12},{15,13},{16,18},{17,... | collective-permute-start | bytes 1327112 | tf_op jit(solution)/shard_map/ppermute | solution.py:98
  41.2 1.3 copy.50.cos_ref
  42.6 1.3 copy.51.sin_ref
  47.1 5.5 %shard_map.213 = (bf16[256,576]{1,0:T(8,128)(2,1)}, bf16[4,256,384]{2,1,0:T(8,128)(2,1)}, bf16[576,1024]{1,0:T(8,128)(2,1)}, bf16[576,576]{1,0:T(8,128)(2,1)}) custom-call(s32[8]{0:T(128)} %table_ref.5, bf16[4,256,576]{2,1,0:T(8,128)(2,1)} %shard_map.212.hidden_ref, f32[2048,128]{1,0:T(8,128)} %copy.50.cos_ref, f32[2048,128]{1,0:T(8,128)} %copy.51.sin_ref, ...), custom_call_target="tpu_custom_call" | custom-call | flops 5750000128 | bytes 1024 | tf_op jit(solution)/shard_map/pallas_call | solution.py:24
  52.6 1.7 collective-permute-start.15
  55.2 1.4 collective-permute-start.19
  56.6 1.5 collective-permute-start.20
  58.7 4.2 %collective-permute-start.18 = (bf16[1,384,576]{2,1,0:T(8,128)(2,1)S(1)}, bf16[1,384,576]{2,1,0:T(8,128)(2,1)S(1)}, u32[]{:S(2)}, u32[]{:S(2)}) collective-permute-start(bf16[1,384,576]{2,1,0:T(8,128)(2,1)S(1)} %select_bitcast_fusion), channel_id=1, source_target_pairs={{0,1},{1,0},{2,3},{3,2},{4,5},{5,4},{6,7},{7,6},{8,9},{9,8},{10,11... | collective-permute-start | bytes 1327112 | tf_op jit(solution)/shard_map/ppermute | solution.py:44
  63.8 7.2 %shard_map.214 = (f32[256,576]{1,0:T(8,128)}, f32[6,384]{1,0:T(8,128)}) custom-call(s32[4]{0:T(128)} %reshape.394.bounds_ref, s32[8]{0:T(128)} %table_ref.5, bf16[256,576]{1,0:T(8,128)(2,1)} %get-tuple-element.74.query_ref, bf16[4,256,384]{2,1,0:T(8,128)(2,1)} %get-tuple-element.75.own_ref, bf16[4,256,384]{2,1,0:T(8,128)(2,1)} %copy-done.28, ...), custom_call_target="tpu_custom_call" | custom-call | flops 13799999488 | bytes 1024 | tf_op jit(solution)/shard_map/pallas_call | solution.py:24
  71.0 2.9 %shard_map.215 = (f32[256,576]{1,0:T(8,128)}, bf16[256,576]{1,0:T(8,128)(2,1)}) custom-call(f32[256,576]{1,0:T(8,128)} %get-tuple-element.76.attended_ref, bf16[256,576]{1,0:T(8,128)(2,1)} %bitcast.86, bf16[576,576]{1,0:T(8,128)(2,1)} %get-tuple-element.77.out_w_ref, f32[1,576]{1,0:T(1,128)} %reshape.397.gain_ref), custom_call_target="tpu_custom_call" | custom-call | flops 2300000000 | bytes 1024 | tf_op jit(solution)/shard_map/pallas_call | solution.py:24
  73.9 4.1 %collective-permute-start.16 = (bf16[256,576]{1,0:T(8,128)(2,1)}, bf16[256,576]{1,0:T(8,128)(2,1)S(1)}, u32[]{:S(2)}, u32[]{:S(2)}) collective-permute-start(bf16[256,576]{1,0:T(8,128)(2,1)} %get-tuple-element.79.hidden_ref), channel_id=1, source_target_pairs={{0,4},{4,0},{8,12},{12,8},{16,20},{20,16},{24,28},{28,24},{1,5},{5... | collective-permute-start | bytes 884744 | tf_op jit(solution)/shard_map/ppermute | solution.py:44
  81.0 10.5 %shard_map.216 = (f32[256,576]{1,0:T(8,128)}, f32[256,576]{1,0:T(8,128)}, bf16[2,256,640]{2,1,0:T(8,128)(2,1)}, bf16[4,144,576]{2,1,0:T(8,128)(2,1)}, bf16[4,144...) custom-call(bf16[256,576]{1,0:T(8,128)(2,1)} %get-tuple-element.79.hidden_ref, ...), custom_call_target="tpu_custom_call" | custom-call | flops 13799999488 | bytes 1024 | tf_op jit(solution)/shard_map/pallas_call | solution.py:24
  92.0 3.7 %collective-permute-start.45 = (bf16[4,144,576]{2,1,0:T(8,128)(2,1)}, bf16[4,144,576]{2,1,0:T(8,128)(2,1)S(1)}, u32[]{:S(2)}, u32[]{:S(2)}) collective-permute-start(bf16[4,144,576]{2,1,0:T(8,128)(2,1)} %get-tuple-element.116), channel_id=1, source_target_pairs={{0,16},{4,20},{8,24},{12,28},{16,0},{20,4},{24,8},{28,12},{1,17},{... | collective-permute-start | bytes 1990664 | tf_op jit(solution)/shard_map/ppermute | solution.py:44
  96.5 4.1 %shard_map.217 = (bf16[576,256]{1,0:T(8,128)(2,1)}, f32[256,576]{1,0:T(8,128)}, bf16[256,576]{1,0:T(8,128)(2,1)}, bf16[576,576]{1,0:T(8,128)(2,1)}) custom-call(f32[256,576]{1,0:T(8,128)} %get-tuple-element.78.residual_ref, f32[256,576]{1,0:T(8,128)} %get-tuple-element.82.out_kept_ref, f32[256,576]{1,0:T(8,128)} %get-tuple-element.83.grad_kept_ref, ...), custom_call_target="tpu_custom_call" | custom-call | flops 4600000000 | bytes 1024 | tf_op jit(solution)/shard_map/pallas_call | solution.py:24
  100.6 11.8 %shard_map.218 = (bf16[256,576]{1,0:T(8,128)(2,1)}, bf16[576,576]{1,0:T(8,128)(2,1)}, bf16[4,256,384]{2,1,0:T(8,128)(2,1)}, bf16[256,384]{1,0:T(8,128)(2,1)}, bf...) custom-call(s32[4]{0:T(128)} %reshape.394.bounds_ref, s32[8]{0:T(128)} %table_ref.5, ...), custom_call_target="tpu_custom_call" | custom-call | flops 20700000256 | bytes 1024 | tf_op jit(solution)/shard_map/pallas_call | solution.py:24
  112.4 5.4 %collective-permute-start.23 = (bf16[256,384]{1,0:T(8,128)(2,1)}, bf16[256,384]{1,0:T(8,128)(2,1)S(1)}, u32[]{:S(2)}, u32[]{:S(2)}) collective-permute-start(bf16[256,384]{1,0:T(8,128)(2,1)} %get-tuple-element.92), channel_id=1, source_target_pairs={{0,4},{4,0},{8,12},{12,8},{16,20},{20,16},{24,28},{28,24},{1,5},{5... | collective-permute-start | bytes 589832 | tf_op jit(solution)/shard_map/ppermute | solution.py:44
  117.8 1.2 collective-permute-done.23.refs_0_
  121.8 5.1 %shard_map.219 = (bf16[768,128]{1,0:T(8,128)(2,1)}, bf16[768,128]{1,0:T(8,128)(2,1)}, bf16[768,128]{1,0:T(8,128)(2,1)}, bf16[768,128]{1,0:T(8,128)(2,1)}, bf16[4...) custom-call(bf16[4,256,384]{2,1,0:T(8,128)(2,1)} %get-tuple-element., ...), custom_call_target="tpu_custom_call" | custom-call | bytes 1024 | tf_op jit(solution)/shard_map/pallas_call | solution.py:24
  131.4 1.9 %collective-permute-start.33 = (bf16[1632,128]{1,0:T(8,128)(2,1)S(1)}, bf16[1632,128]{1,0:T(8,128)(2,1)S(1)}, u32[]{:S(2)}, u32[]{:S(2)}) collective-permute-start(bf16[1632,128]{1,0:T(8,128)(2,1)S(1)} %pad_maximum_fusion.4), channel_id=1, source_target_pairs={{0,24},{4,28},{8,16},{12,20},{16,8},{20,12},{24,0},{28,4},{1,25},{... | collective-permute-start | bytes 1253384 | tf_op jit(solution)/shard_map/ppermute | solution.py:44
  133.5 1.2 collective-permute-start.31
  135.6 4.3 %collective-permute-start.50 = (bf16[144,576]{1,0:T(8,128)(2,1)S(1)}, bf16[144,576]{1,0:T(8,128)(2,1)S(1)}, u32[]{:S(2)}, u32[]{:S(2)}) collective-permute-start(bf16[144,576]{1,0:T(8,128)(2,1)S(1)} %get-tuple-element.163), channel_id=1, source_target_pairs={{0,3},{1,2},{2,1},{3,0},{4,7},{5,6},{6,5},{7,4},{8,11},{9,10},{10,... | collective-permute-start | bytes 497672 | tf_op jit(solution)/shard_map/ppermute | solution.py:44
  139.9 1.3 collective-permute-start.29
  141.2 4.2 %collective-permute-done.50 = bf16[144,576]{1,0:T(8,128)(2,1)S(1)} collective-permute-done((bf16[144,576]{1,0:T(8,128)(2,1)S(1)}, bf16[144,576]{1,0:T(8,128)(2,1)S(1)}, u32[]{:S(2)}, u32[]{:S(2)}) %collective-permute-start.50) | collective-permute-done | bytes 165920 | tf_op jit(solution)/shard_map/ppermute | solution.py:44
  146.2 7.4 %collective-permute-start.48 = (bf16[144,576]{1,0:T(8,128)(2,1)}, bf16[144,576]{1,0:T(8,128)(2,1)}, u32[]{:S(2)}, u32[]{:S(2)}) collective-permute-start(bf16[144,576]{1,0:T(8,128)(2,1)} %get-tuple-element.162), channel_id=1, source_target_pairs={{0,1},{1,0},{2,3},{3,2},{4,5},{5,4},{6,7},{7,6},{8,9},{9,8},{10,11... | collective-permute-start | bytes 497672 | tf_op jit(solution)/shard_map/ppermute | solution.py:44
  153.7 2.0 %collective-permute-done.49 = bf16[144,576]{1,0:T(8,128)(2,1)} collective-permute-done((bf16[144,576]{1,0:T(8,128)(2,1)}, bf16[144,576]{1,0:T(8,128)(2,1)}, u32[]{:S(2)}, u32[]{:S(2)}) %collective-permute-start.49) | collective-permute-done | bytes 165920 | tf_op jit(solution)/shard_map/ppermute | solution.py:44
  155.7 3.8 %collective-permute-done.48 = bf16[144,576]{1,0:T(8,128)(2,1)} collective-permute-done((bf16[144,576]{1,0:T(8,128)(2,1)}, bf16[144,576]{1,0:T(8,128)(2,1)}, u32[]{:S(2)}, u32[]{:S(2)}) %collective-permute-start.48) | collective-permute-done | bytes 165920 | tf_op jit(solution)/shard_map/ppermute | solution.py:44
  159.5 1.2 fusion.18.refs_0_
  161.4 1.7 collective-permute-start.52
  163.1 1.2 collective-permute-start.53
  164.3 1.4 add_convert_fusion.1
  165.8 2.7 %collective-permute-start.36 = (bf16[216,128]{1,0:T(8,128)(2,1)S(1)}, bf16[216,128]{1,0:T(8,128)(2,1)S(1)}, u32[]{:S(2)}, u32[]{:S(2)}) collective-permute-start(bf16[216,128]{1,0:T(8,128)(2,1)S(1)} %get-tuple-element.175), channel_id=1, source_target_pairs={{0,3},{1,2},{2,1},{3,0},{4,7},{5,6},{6,5},{7,4},{8,11},{9,10},{10,... | collective-permute-start | bytes 165896 | tf_op jit(solution)/shard_map/ppermute | solution.py:44
  169.2 1.8 collective-permute-start.34
  172.3 1.3 collective-permute-done.35
  174.8 1.7 collective-permute-start.38
  176.5 1.2 collective-permute-start.39
  179.4 2.1 %collective-permute-done.39.refs_3_ = bf16[216,128]{1,0:T(8,128)(2,1)S(1)} collective-permute-done((bf16[216,128]{1,0:T(8,128)(2,1)S(1)}, bf16[216,128]{1,0:T(8,128)(2,1)S(1)}, u32[]{:S(2)}, u32[]{:S(2)}) %collective-permute-start.39) | collective-permute-done | bytes 55328 | tf_op jit(solution)/shard_map/ppermute | solution.py:44
  182.2 4.1 %shard_map.221 = (f32[144,1536]{1,0:T(8,128)}, f32[144,1536]{1,0:T(8,128)}, f32[576,384]{1,0:T(8,128)}, f32[1,144]{1,0:T(1,128)}) custom-call(bf16[144,576]{1,0:T(8,128)(2,1)} %copy-done.21, bf16[144,576]{1,0:T(8,128)(2,1)} %copy-done.44, bf16[144,576]{1,0:T(8,128)(2,1)} %collective-permute-done.52.refs_2_, bf16[144,576]{1,0:T(8,128)(2,1)} %copy-done.45, ...), custom_call_target="tpu_custom_call" | custom-call | flops 1150000000 | bytes 1024 | tf_op jit(solution)/shard_map/pallas_call | solution.py:24
  187.0 2.4 %shard_map.220 = (f32[144,576]{1,0:T(8,128)}, f32[144,192]{1,0:T(8,128)}, f32[144,192]{1,0:T(8,128)}, f32[144,576]{1,0:T(8,128)}, f32[1,144]{1,0:T(1,128)}) custom-call(bf16[216,128]{1,0:T(8,128)(2,1)} %copy-done.23, bf16[216,128]{1,0:T(8,128)(2,1)} %copy-done.50, bf16[216,128]{1,0:T(8,128)(2,1)} %copy-done.51, bf16[216,128]{1,0:T(8,128)(2,1)} %copy-done.52, ...), custom_call_target="tpu_custom_call" | custom-call | flops 1150000000 | bytes 1024 | tf_op jit(solution)/shard_map/pallas_call | solution.py:24
  (275 shorter events, 38.9 us)
Async XLA Ops:
  1.9 26.4 %collective-permute-start = (bf16[256,576]{1,0:T(8,128)(2,1)S(1)}, bf16[256,576]{1,0:T(8,128)(2,1)S(1)}, u32[]{:S(2)}, u32[]{:S(2)}) collective-permute-start(bf16[256,576]{1,0:T(8,128)(2,1)S(1)} %bitcast.82), channel_id=1, source_target_pairs={{0,8},{4,12},{8,0},{12,4},{16,24},{20,28},{24,16},{28,20},{1,9},{5... | collective-permute-start | bytes 884744 | tf_op jit(solution)/shard_map/ppermute | solution.py:44
  4.9 23.4 %collective-permute-start.1 = (bf16[256,576]{1,0:T(8,128)(2,1)S(1)}, bf16[256,576]{1,0:T(8,128)(2,1)S(1)}, u32[]{:S(2)}, u32[]{:S(2)}) collective-permute-start(bf16[256,576]{1,0:T(8,128)(2,1)S(1)} %bitcast.83), channel_id=1, source_target_pairs={{0,16},{4,20},{8,24},{12,28},{16,0},{20,4},{24,8},{28,12},{1,17},{... | collective-permute-start | bytes 884744 | tf_op jit(solution)/shard_map/ppermute | solution.py:44
  6.4 21.9 %collective-permute-start.2 = (bf16[256,576]{1,0:T(8,128)(2,1)S(1)}, bf16[256,576]{1,0:T(8,128)(2,1)}, u32[]{:S(2)}, u32[]{:S(2)}) collective-permute-start(bf16[256,576]{1,0:T(8,128)(2,1)S(1)} %bitcast.84), channel_id=1, source_target_pairs={{0,24},{4,28},{8,16},{12,20},{16,8},{20,12},{24,0},{28,4},{1,25},{... | collective-permute-start | bytes 884744 | tf_op jit(solution)/shard_map/ppermute | solution.py:44
  10.0 8.4 %collective-permute-start.3 = (bf16[1,232,128]{2,1,0:T(8,128)(2,1)S(1)}, bf16[1,232,128]{2,1,0:T(8,128)(2,1)S(1)}, u32[]{:S(2)}, u32[]{:S(2)}) collective-permute-start(bf16[1,232,128]{2,1,0:T(8,128)(2,1)S(1)} %maximum_bitcast_fusion), channel_id=1, source_target_pairs={{0,1},{1,0},{2,3},{3,2},{4,5},{5,4},{6,7},{7,6},{8,9},{9,8},{10,11... | collective-permute-start | bytes 178184 | tf_op jit(solution)/shard_map/ppermute | solution.py:44
  13.1 8.5 %collective-permute-start.5 = (bf16[1,144,384]{2,1,0:T(8,128)(2,1)S(1)}, bf16[1,144,384]{2,1,0:T(8,128)(2,1)S(1)}, u32[]{:S(2)}, u32[]{:S(2)}) collective-permute-start(bf16[1,144,384]{2,1,0:T(8,128)(2,1)S(1)} %fusion.20), channel_id=1, source_target_pairs={{0,1},{1,0},{2,3},{3,2},{4,5},{5,4},{6,7},{7,6},{8,9},{9,8},{10,11... | collective-permute-start | bytes 331784 | tf_op jit(solution)/shard_map/ppermute | solution.py:44
  18.5 7.4 %collective-permute-start.4 = (bf16[2,232,128]{2,1,0:T(8,128)(2,1)S(1)}, bf16[2,232,128]{2,1,0:T(8,128)(2,1)S(1)}, u32[]{:S(2)}, u32[]{:S(2)}) collective-permute-start(bf16[2,232,128]{2,1,0:T(8,128)(2,1)S(1)} %pad_maximum_fusion.8), channel_id=1, source_target_pairs={{0,2},{1,3},{2,0},{3,1},{4,6},{5,7},{6,4},{7,5},{8,10},{9,11},{10,... | collective-permute-start | bytes 356360 | tf_op jit(solution)/shard_map/ppermute | solution.py:44
  26.8 17.1 %collective-permute-start.6 = (bf16[2,144,384]{2,1,0:T(8,128)(2,1)S(1)}, bf16[2,144,384]{2,1,0:T(8,128)(2,1)S(1)}, u32[]{:S(2)}, u32[]{:S(2)}) collective-permute-start(bf16[2,144,384]{2,1,0:T(8,128)(2,1)S(1)} %pad_maximum_fusion.7), channel_id=1, source_target_pairs={{0,2},{1,3},{2,0},{3,1},{4,6},{5,7},{6,4},{7,5},{8,10},{9,11},{10,... | collective-permute-start | bytes 663560 | tf_op jit(solution)/shard_map/ppermute | solution.py:44
  32.0 12.0 %collective-permute-start.8 = (bf16[4,232,128]{2,1,0:T(8,128)(2,1)S(1)}, bf16[4,232,128]{2,1,0:T(8,128)(2,1)S(1)}, u32[]{:S(2)}, u32[]{:S(2)}) collective-permute-start(bf16[4,232,128]{2,1,0:T(8,128)(2,1)S(1)} %pad_maximum_fusion.6.refs_0_), channel_id=1, source_target_pairs={{0,8},{4,12},{8,0},{12,4},{16,24},{20,28},{24,16},{28,20},{1,9},{5... | collective-permute-start | bytes 712712 | tf_op jit(solution)/shard_map/ppermute | solution.py:44
  33.5 11.1 %collective-permute-start.9 = (bf16[4,232,128]{2,1,0:T(8,128)(2,1)S(1)}, bf16[4,232,128]{2,1,0:T(8,128)(2,1)}, u32[]{:S(2)}, u32[]{:S(2)}) collective-permute-start(bf16[4,232,128]{2,1,0:T(8,128)(2,1)S(1)} %pad_maximum_fusion.6.refs_0_), channel_id=1, source_target_pairs={{0,16},{4,20},{8,24},{12,28},{16,0},{20,4},{24,8},{28,12},{1,17},{... | collective-permute-start | bytes 712712 | tf_op jit(solution)/shard_map/ppermute | solution.py:44
  35.1 9.7 %collective-permute-start.10 = (bf16[4,232,128]{2,1,0:T(8,128)(2,1)S(1)}, bf16[4,232,128]{2,1,0:T(8,128)(2,1)}, u32[]{:S(2)}, u32[]{:S(2)}) collective-permute-start(bf16[4,232,128]{2,1,0:T(8,128)(2,1)S(1)} %pad_maximum_fusion.6.refs_0_), channel_id=1, source_target_pairs={{0,24},{4,28},{8,16},{12,20},{16,8},{20,12},{24,0},{28,4},{1,25},{... | collective-permute-start | bytes 712712 | tf_op jit(solution)/shard_map/ppermute | solution.py:44
  35.8 9.8 %collective-permute-start.7 = (bf16[384,576]{1,0:T(8,128)(2,1)S(1)}, bf16[384,576]{1,0:T(8,128)(2,1)S(1)}, u32[]{:S(2)}, u32[]{:S(2)}) collective-permute-start(bf16[384,576]{1,0:T(8,128)(2,1)S(1)} %copy.49), channel_id=1, source_target_pairs={{0,2},{1,3},{6,4},{7,5},{8,10},{9,11},{14,12},{15,13},{16,18},{17,... | collective-permute-start | bytes 1327112 | tf_op jit(solution)/shard_map/ppermute | solution.py:98
  52.6 10.3 %collective-permute-start.15 = (bf16[4,256,384]{2,1,0:T(8,128)(2,1)}, bf16[4,256,384]{2,1,0:T(8,128)(2,1)S(1)}, u32[]{:S(2)}, u32[]{:S(2)}) collective-permute-start(bf16[4,256,384]{2,1,0:T(8,128)(2,1)} %get-tuple-element.75.own_ref), channel_id=1, source_target_pairs={{0,4},{4,0},{8,12},{12,8},{16,20},{20,16},{24,28},{28,24},{1,5},{5... | collective-permute-start | bytes 2359304 | tf_op jit(solution)/shard_map/ppermute | solution.py:44
  55.2 24.1 %collective-permute-start.19 = (bf16[4,144,384]{2,1,0:T(8,128)(2,1)S(1)}, bf16[4,144,384]{2,1,0:T(8,128)(2,1)S(1)}, u32[]{:S(2)}, u32[]{:S(2)}) collective-permute-start(bf16[4,144,384]{2,1,0:T(8,128)(2,1)S(1)} %pad_maximum_fusion.1.refs_0_), channel_id=1, source_target_pairs={{0,8},{4,12},{8,0},{12,4},{16,24},{20,28},{24,16},{28,20},{1,9},{5... | collective-permute-start | bytes 1327112 | tf_op jit(solution)/shard_map/ppermute | solution.py:44
  56.6 22.7 %collective-permute-start.20 = (bf16[4,144,384]{2,1,0:T(8,128)(2,1)S(1)}, bf16[4,144,384]{2,1,0:T(8,128)(2,1)S(1)}, u32[]{:S(2)}, u32[]{:S(2)}) collective-permute-start(bf16[4,144,384]{2,1,0:T(8,128)(2,1)S(1)} %pad_maximum_fusion.1.refs_0_), channel_id=1, source_target_pairs={{0,16},{4,20},{8,24},{12,28},{16,0},{20,4},{24,8},{28,12},{1,17},{... | collective-permute-start | bytes 1327112 | tf_op jit(solution)/shard_map/ppermute | solution.py:44
  58.1 21.2 %collective-permute-start.21 = (bf16[4,144,384]{2,1,0:T(8,128)(2,1)S(1)}, bf16[4,144,384]{2,1,0:T(8,128)(2,1)}, u32[]{:S(2)}, u32[]{:S(2)}) collective-permute-start(bf16[4,144,384]{2,1,0:T(8,128)(2,1)S(1)} %pad_maximum_fusion.1.refs_0_), channel_id=1, source_target_pairs={{0,24},{4,28},{8,16},{12,20},{16,8},{20,12},{24,0},{28,4},{1,25},{... | collective-permute-start | bytes 1327112 | tf_op jit(solution)/shard_map/ppermute | solution.py:44
  58.7 19.3 %collective-permute-start.18 = (bf16[1,384,576]{2,1,0:T(8,128)(2,1)S(1)}, bf16[1,384,576]{2,1,0:T(8,128)(2,1)S(1)}, u32[]{:S(2)}, u32[]{:S(2)}) collective-permute-start(bf16[1,384,576]{2,1,0:T(8,128)(2,1)S(1)} %select_bitcast_fusion), channel_id=1, source_target_pairs={{0,1},{1,0},{2,3},{3,2},{4,5},{5,4},{6,7},{7,6},{8,9},{9,8},{10,11... | collective-permute-start | bytes 1327112 | tf_op jit(solution)/shard_map/ppermute | solution.py:44
  73.9 5.6 %collective-permute-start.16 = (bf16[256,576]{1,0:T(8,128)(2,1)}, bf16[256,576]{1,0:T(8,128)(2,1)S(1)}, u32[]{:S(2)}, u32[]{:S(2)}) collective-permute-start(bf16[256,576]{1,0:T(8,128)(2,1)} %get-tuple-element.79.hidden_ref), channel_id=1, source_target_pairs={{0,4},{4,0},{8,12},{12,8},{16,20},{20,16},{24,28},{28,24},{1,5},{5... | collective-permute-start | bytes 884744 | tf_op jit(solution)/shard_map/ppermute | solution.py:44
  91.5 4.1 %collective-permute-start.22 = (bf16[2,256,640]{2,1,0:T(8,128)(2,1)}, bf16[2,256,640]{2,1,0:T(8,128)(2,1)S(1)}, u32[]{:S(2)}, u32[]{:S(2)}) collective-permute-start(bf16[2,256,640]{2,1,0:T(8,128)(2,1)} %get-tuple-element.84), channel_id=1, source_target_pairs={{0,4},{4,0},{8,12},{12,8},{16,20},{20,16},{24,28},{28,24},{1,5},{5... | collective-permute-start | bytes 1966088 | tf_op jit(solution)/shard_map/ppermute | solution.py:44
  92.0 34.9 %collective-permute-start.44 = (bf16[4,144,576]{2,1,0:T(8,128)(2,1)}, bf16[4,144,576]{2,1,0:T(8,128)(2,1)S(1)}, u32[]{:S(2)}, u32[]{:S(2)}) collective-permute-start(bf16[4,144,576]{2,1,0:T(8,128)(2,1)} %get-tuple-element.115), channel_id=1, source_target_pairs={{0,8},{4,12},{8,0},{12,4},{16,24},{20,28},{24,16},{28,20},{1,9},{5... | collective-permute-start | bytes 1990664 | tf_op jit(solution)/shard_map/ppermute | solution.py:44
  92.0 35.9 %collective-permute-start.45 = (bf16[4,144,576]{2,1,0:T(8,128)(2,1)}, bf16[4,144,576]{2,1,0:T(8,128)(2,1)S(1)}, u32[]{:S(2)}, u32[]{:S(2)}) collective-permute-start(bf16[4,144,576]{2,1,0:T(8,128)(2,1)} %get-tuple-element.116), channel_id=1, source_target_pairs={{0,16},{4,20},{8,24},{12,28},{16,0},{20,4},{24,8},{28,12},{1,17},{... | collective-permute-start | bytes 1990664 | tf_op jit(solution)/shard_map/ppermute | solution.py:44
  95.7 32.8 %collective-permute-start.46 = (bf16[4,144,576]{2,1,0:T(8,128)(2,1)}, bf16[4,144,576]{2,1,0:T(8,128)(2,1)S(1)}, u32[]{:S(2)}, u32[]{:S(2)}) collective-permute-start(bf16[4,144,576]{2,1,0:T(8,128)(2,1)} %get-tuple-element.117), channel_id=1, source_target_pairs={{0,24},{4,28},{8,16},{12,20},{16,8},{20,12},{24,0},{28,4},{1,25},{... | collective-permute-start | bytes 1990664 | tf_op jit(solution)/shard_map/ppermute | solution.py:44
  112.4 6.7 %collective-permute-start.23 = (bf16[256,384]{1,0:T(8,128)(2,1)}, bf16[256,384]{1,0:T(8,128)(2,1)S(1)}, u32[]{:S(2)}, u32[]{:S(2)}) collective-permute-start(bf16[256,384]{1,0:T(8,128)(2,1)} %get-tuple-element.92), channel_id=1, source_target_pairs={{0,4},{4,0},{8,12},{12,8},{16,20},{20,16},{24,28},{28,24},{1,5},{5... | collective-permute-start | bytes 589832 | tf_op jit(solution)/shard_map/ppermute | solution.py:44
  129.9 3.4 %collective-permute-start.30 = (bf16[4,216,128]{2,1,0:T(8,128)(2,1)S(1)}, bf16[4,216,128]{2,1,0:T(8,128)(2,1)S(1)}, u32[]{:S(2)}, u32[]{:S(2)}) collective-permute-start(bf16[4,216,128]{2,1,0:T(8,128)(2,1)S(1)} %copy-done.42), channel_id=1, source_target_pairs={{0,4},{4,0},{8,12},{12,8},{16,20},{20,16},{24,28},{28,24},{1,5},{5... | collective-permute-start | bytes 663560 | tf_op jit(solution)/shard_map/ppermute | solution.py:44
  130.3 4.3 %collective-permute-start.28 = (bf16[4,216,128]{2,1,0:T(8,128)(2,1)S(1)}, bf16[4,216,128]{2,1,0:T(8,128)(2,1)S(1)}, u32[]{:S(2)}, u32[]{:S(2)}) collective-permute-start(bf16[4,216,128]{2,1,0:T(8,128)(2,1)S(1)} %copy-done.41), channel_id=1, source_target_pairs={{0,4},{4,0},{8,12},{12,8},{16,20},{20,16},{24,28},{28,24},{1,5},{5... | collective-permute-start | bytes 663560 | tf_op jit(solution)/shard_map/ppermute | solution.py:44
  130.5 4.3 %collective-permute-start.27 = (bf16[4,216,128]{2,1,0:T(8,128)(2,1)S(1)}, bf16[4,216,128]{2,1,0:T(8,128)(2,1)S(1)}, u32[]{:S(2)}, u32[]{:S(2)}) collective-permute-start(bf16[4,216,128]{2,1,0:T(8,128)(2,1)S(1)} %copy-done.40), channel_id=1, source_target_pairs={{0,4},{4,0},{8,12},{12,8},{16,20},{20,16},{24,28},{28,24},{1,5},{5... | collective-permute-start | bytes 663560 | tf_op jit(solution)/shard_map/ppermute | solution.py:44
  131.4 31.7 %collective-permute-start.33 = (bf16[1632,128]{1,0:T(8,128)(2,1)S(1)}, bf16[1632,128]{1,0:T(8,128)(2,1)S(1)}, u32[]{:S(2)}, u32[]{:S(2)}) collective-permute-start(bf16[1632,128]{1,0:T(8,128)(2,1)S(1)} %pad_maximum_fusion.4), channel_id=1, source_target_pairs={{0,24},{4,28},{8,16},{12,20},{16,8},{20,12},{24,0},{28,4},{1,25},{... | collective-permute-start | bytes 1253384 | tf_op jit(solution)/shard_map/ppermute | solution.py:44
  133.5 30.8 %collective-permute-start.31 = (bf16[1632,128]{1,0:T(8,128)(2,1)S(1)}, bf16[1632,128]{1,0:T(8,128)(2,1)S(1)}, u32[]{:S(2)}, u32[]{:S(2)}) collective-permute-start(bf16[1632,128]{1,0:T(8,128)(2,1)S(1)} %pad_maximum_fusion.3), channel_id=1, source_target_pairs={{0,16},{4,20},{8,24},{12,28},{16,0},{20,4},{24,8},{28,12},{1,17},{... | collective-permute-start | bytes 1253384 | tf_op jit(solution)/shard_map/ppermute | solution.py:44
  135.6 9.9 %collective-permute-start.50 = (bf16[144,576]{1,0:T(8,128)(2,1)S(1)}, bf16[144,576]{1,0:T(8,128)(2,1)S(1)}, u32[]{:S(2)}, u32[]{:S(2)}) collective-permute-start(bf16[144,576]{1,0:T(8,128)(2,1)S(1)} %get-tuple-element.163), channel_id=1, source_target_pairs={{0,3},{1,2},{2,1},{3,0},{4,7},{5,6},{6,5},{7,4},{8,11},{9,10},{10,... | collective-permute-start | bytes 497672 | tf_op jit(solution)/shard_map/ppermute | solution.py:44
  139.9 24.3 %collective-permute-start.29 = (bf16[1632,128]{1,0:T(8,128)(2,1)S(1)}, bf16[1632,128]{1,0:T(8,128)(2,1)}, u32[]{:S(2)}, u32[]{:S(2)}) collective-permute-start(bf16[1632,128]{1,0:T(8,128)(2,1)S(1)} %pad_maximum_fusion.2), channel_id=1, source_target_pairs={{0,8},{4,12},{8,0},{12,4},{16,24},{20,28},{24,16},{28,20},{1,9},{5... | collective-permute-start | bytes 1253384 | tf_op jit(solution)/shard_map/ppermute | solution.py:44
  141.2 14.4 %collective-permute-start.49 = (bf16[144,576]{1,0:T(8,128)(2,1)}, bf16[144,576]{1,0:T(8,128)(2,1)}, u32[]{:S(2)}, u32[]{:S(2)}) collective-permute-start(bf16[144,576]{1,0:T(8,128)(2,1)} %get-tuple-element.164), channel_id=1, source_target_pairs={{0,2},{1,3},{2,0},{3,1},{4,6},{5,7},{6,4},{7,5},{8,10},{9,11},{10,... | collective-permute-start | bytes 497672 | tf_op jit(solution)/shard_map/ppermute | solution.py:44
  146.2 13.3 %collective-permute-start.48 = (bf16[144,576]{1,0:T(8,128)(2,1)}, bf16[144,576]{1,0:T(8,128)(2,1)}, u32[]{:S(2)}, u32[]{:S(2)}) collective-permute-start(bf16[144,576]{1,0:T(8,128)(2,1)} %get-tuple-element.162), channel_id=1, source_target_pairs={{0,1},{1,0},{2,3},{3,2},{4,5},{5,4},{6,7},{7,6},{8,9},{9,8},{10,11... | collective-permute-start | bytes 497672 | tf_op jit(solution)/shard_map/ppermute | solution.py:44
  160.7 8.5 %collective-permute-start.51 = (bf16[144,576]{1,0:T(8,128)(2,1)S(1)}, bf16[144,576]{1,0:T(8,128)(2,1)S(1)}, u32[]{:S(2)}, u32[]{:S(2)}) collective-permute-start(bf16[144,576]{1,0:T(8,128)(2,1)S(1)} %fusion.18.refs_0_), channel_id=1, source_target_pairs={{0,8},{4,12},{8,0},{12,4},{16,24},{20,28},{24,16},{28,20},{1,9},{5... | collective-permute-start | bytes 497672 | tf_op jit(solution)/shard_map/ppermute | solution.py:44
  161.4 10.3 %collective-permute-start.52 = (bf16[144,576]{1,0:T(8,128)(2,1)S(1)}, bf16[144,576]{1,0:T(8,128)(2,1)}, u32[]{:S(2)}, u32[]{:S(2)}) collective-permute-start(bf16[144,576]{1,0:T(8,128)(2,1)S(1)} %fusion.18.refs_0_), channel_id=1, source_target_pairs={{0,16},{4,20},{8,24},{12,28},{16,0},{20,4},{24,8},{28,12},{1,17},{... | collective-permute-start | bytes 497672 | tf_op jit(solution)/shard_map/ppermute | solution.py:44
  163.1 8.6 %collective-permute-start.53 = (bf16[144,576]{1,0:T(8,128)(2,1)S(1)}, bf16[144,576]{1,0:T(8,128)(2,1)S(1)}, u32[]{:S(2)}, u32[]{:S(2)}) collective-permute-start(bf16[144,576]{1,0:T(8,128)(2,1)S(1)} %fusion.18.refs_0_), channel_id=1, source_target_pairs={{0,24},{4,28},{8,16},{12,20},{16,8},{20,12},{24,0},{28,4},{1,25},{... | collective-permute-start | bytes 497672 | tf_op jit(solution)/shard_map/ppermute | solution.py:44
  165.8 6.5 %collective-permute-start.36 = (bf16[216,128]{1,0:T(8,128)(2,1)S(1)}, bf16[216,128]{1,0:T(8,128)(2,1)S(1)}, u32[]{:S(2)}, u32[]{:S(2)}) collective-permute-start(bf16[216,128]{1,0:T(8,128)(2,1)S(1)} %get-tuple-element.175), channel_id=1, source_target_pairs={{0,3},{1,2},{2,1},{3,0},{4,7},{5,6},{6,5},{7,4},{8,11},{9,10},{10,... | collective-permute-start | bytes 165896 | tf_op jit(solution)/shard_map/ppermute | solution.py:44
  168.5 5.2 %collective-permute-start.35 = (bf16[216,128]{1,0:T(8,128)(2,1)S(1)}, bf16[216,128]{1,0:T(8,128)(2,1)S(1)}, u32[]{:S(2)}, u32[]{:S(2)}) collective-permute-start(bf16[216,128]{1,0:T(8,128)(2,1)S(1)} %get-tuple-element.176), channel_id=1, source_target_pairs={{0,2},{1,3},{2,0},{3,1},{4,6},{5,7},{6,4},{7,5},{8,10},{9,11},{10,... | collective-permute-start | bytes 165896 | tf_op jit(solution)/shard_map/ppermute | solution.py:44
  169.2 4.8 %collective-permute-start.34 = (bf16[216,128]{1,0:T(8,128)(2,1)S(1)}, bf16[216,128]{1,0:T(8,128)(2,1)S(1)}, u32[]{:S(2)}, u32[]{:S(2)}) collective-permute-start(bf16[216,128]{1,0:T(8,128)(2,1)S(1)} %get-tuple-element.174), channel_id=1, source_target_pairs={{0,1},{1,0},{2,3},{3,2},{4,5},{5,4},{6,7},{7,6},{8,9},{9,8},{10,11... | collective-permute-start | bytes 165896 | tf_op jit(solution)/shard_map/ppermute | solution.py:44
  171.7 3.0 %collective-permute-start.54 = (bf16[144,576]{1,0:T(8,128)(2,1)S(1)}, bf16[144,576]{1,0:T(8,128)(2,1)S(1)}, u32[]{:S(2)}, u32[]{:S(2)}) collective-permute-start(bf16[144,576]{1,0:T(8,128)(2,1)S(1)} %fusion.18.refs_0_), channel_id=1, source_target_pairs={{0,4},{4,0},{8,12},{12,8},{16,20},{20,16},{24,28},{28,24},{1,5},{5... | collective-permute-start | bytes 497672 | tf_op jit(solution)/shard_map/ppermute | solution.py:44
  171.7 4.7 %collective-permute-start.55 = (bf16[144,576]{1,0:T(8,128)(2,1)S(1)}, bf16[144,576]{1,0:T(8,128)(2,1)S(1)}, u32[]{:S(2)}, u32[]{:S(2)}) collective-permute-start(bf16[144,576]{1,0:T(8,128)(2,1)S(1)} %collective-permute-done.51.refs_1_), channel_id=1, source_target_pairs={{0,4},{4,0},{8,12},{12,8},{16,20},{20,16},{24,28},{28,24},{1,5},{5... | collective-permute-start | bytes 497672 | tf_op jit(solution)/shard_map/ppermute | solution.py:44
  172.2 6.5 %collective-permute-start.56 = (bf16[144,576]{1,0:T(8,128)(2,1)}, bf16[144,576]{1,0:T(8,128)(2,1)S(1)}, u32[]{:S(2)}, u32[]{:S(2)}) collective-permute-start(bf16[144,576]{1,0:T(8,128)(2,1)} %collective-permute-done.52.refs_2_), channel_id=1, source_target_pairs={{0,4},{4,0},{8,12},{12,8},{16,20},{20,16},{24,28},{28,24},{1,5},{5... | collective-permute-start | bytes 497672 | tf_op jit(solution)/shard_map/ppermute | solution.py:44
  173.6 7.9 %collective-permute-start.57 = (bf16[144,576]{1,0:T(8,128)(2,1)S(1)}, bf16[144,576]{1,0:T(8,128)(2,1)S(1)}, u32[]{:S(2)}, u32[]{:S(2)}) collective-permute-start(bf16[144,576]{1,0:T(8,128)(2,1)S(1)} %collective-permute-done.53.refs_3_), channel_id=1, source_target_pairs={{0,4},{4,0},{8,12},{12,8},{16,20},{20,16},{24,28},{28,24},{1,5},{5... | collective-permute-start | bytes 497672 | tf_op jit(solution)/shard_map/ppermute | solution.py:44
  174.1 4.8 %collective-permute-start.37 = (bf16[216,128]{1,0:T(8,128)(2,1)S(1)}, bf16[216,128]{1,0:T(8,128)(2,1)S(1)}, u32[]{:S(2)}, u32[]{:S(2)}) collective-permute-start(bf16[216,128]{1,0:T(8,128)(2,1)S(1)} %fusion.23.refs_0_), channel_id=1, source_target_pairs={{0,8},{4,12},{8,0},{12,4},{16,24},{20,28},{24,16},{28,20},{1,9},{5... | collective-permute-start | bytes 165896 | tf_op jit(solution)/shard_map/ppermute | solution.py:44
  174.8 4.6 %collective-permute-start.38 = (bf16[216,128]{1,0:T(8,128)(2,1)S(1)}, bf16[216,128]{1,0:T(8,128)(2,1)S(1)}, u32[]{:S(2)}, u32[]{:S(2)}) collective-permute-start(bf16[216,128]{1,0:T(8,128)(2,1)S(1)} %fusion.23.refs_0_), channel_id=1, source_target_pairs={{0,16},{4,20},{8,24},{12,28},{16,0},{20,4},{24,8},{28,12},{1,17},{... | collective-permute-start | bytes 165896 | tf_op jit(solution)/shard_map/ppermute | solution.py:44
  176.5 5.1 %collective-permute-start.39 = (bf16[216,128]{1,0:T(8,128)(2,1)S(1)}, bf16[216,128]{1,0:T(8,128)(2,1)S(1)}, u32[]{:S(2)}, u32[]{:S(2)}) collective-permute-start(bf16[216,128]{1,0:T(8,128)(2,1)S(1)} %fusion.23.refs_0_), channel_id=1, source_target_pairs={{0,24},{4,28},{8,16},{12,20},{16,8},{20,12},{24,0},{28,4},{1,25},{... | collective-permute-start | bytes 165896 | tf_op jit(solution)/shard_map/ppermute | solution.py:44
  178.8 7.6 %collective-permute-start.40 = (bf16[216,128]{1,0:T(8,128)(2,1)S(1)}, bf16[216,128]{1,0:T(8,128)(2,1)S(1)}, u32[]{:S(2)}, u32[]{:S(2)}) collective-permute-start(bf16[216,128]{1,0:T(8,128)(2,1)S(1)} %fusion.23.refs_0_), channel_id=1, source_target_pairs={{0,4},{4,0},{8,12},{12,8},{16,20},{20,16},{24,28},{28,24},{1,5},{5... | collective-permute-start | bytes 165896 | tf_op jit(solution)/shard_map/ppermute | solution.py:44
  178.9 7.5 %collective-permute-start.41 = (bf16[216,128]{1,0:T(8,128)(2,1)S(1)}, bf16[216,128]{1,0:T(8,128)(2,1)S(1)}, u32[]{:S(2)}, u32[]{:S(2)}) collective-permute-start(bf16[216,128]{1,0:T(8,128)(2,1)S(1)} %collective-permute-done.37.refs_1_), channel_id=1, source_target_pairs={{0,4},{4,0},{8,12},{12,8},{16,20},{20,16},{24,28},{28,24},{1,5},{5... | collective-permute-start | bytes 165896 | tf_op jit(solution)/shard_map/ppermute | solution.py:44
  179.3 7.0 %collective-permute-start.42 = (bf16[216,128]{1,0:T(8,128)(2,1)S(1)}, bf16[216,128]{1,0:T(8,128)(2,1)S(1)}, u32[]{:S(2)}, u32[]{:S(2)}) collective-permute-start(bf16[216,128]{1,0:T(8,128)(2,1)S(1)} %collective-permute-done.38.refs_2_), channel_id=1, source_target_pairs={{0,4},{4,0},{8,12},{12,8},{16,20},{20,16},{24,28},{28,24},{1,5},{5... | collective-permute-start | bytes 165896 | tf_op jit(solution)/shard_map/ppermute | solution.py:44
  181.5 4.8 %collective-permute-start.43 = (bf16[216,128]{1,0:T(8,128)(2,1)S(1)}, bf16[216,128]{1,0:T(8,128)(2,1)S(1)}, u32[]{:S(2)}, u32[]{:S(2)}) collective-permute-start(bf16[216,128]{1,0:T(8,128)(2,1)S(1)} %collective-permute-done.39.refs_3_), channel_id=1, source_target_pairs={{0,4},{4,0},{8,12},{12,8},{16,20},{20,16},{24,28},{28,24},{1,5},{5... | collective-permute-start | bytes 165896 | tf_op jit(solution)/shard_map/ppermute | solution.py:44
  (71 other events, 341.3 us)

commit v4 on v3

--- a/solution.py
+++ b/solution.py
@@ -12,6 +12,7 @@
 GROUPS = HEADS // KV_HEADS
 KV_WIDTH = KV_HEADS * HEAD
 TILE = 128
+DOCS = 4
 
 epsilon = 1e-05
 rope_base = 100000.0
@@ -252,6 +253,7 @@
             ((1, rows), jnp.float32),
         ],
         [*pieces, shard, gain],
+        microseconds=2,
         scratch=[pltpu.VMEM((rows, count * TILE), jnp.float32)],
     )
 
@@ -298,6 +300,7 @@
             ((1, rows), jnp.float32),
         ],
         [*pieces, w_gate, w_up, gain],
+        microseconds=4,
         scratch=[
             pltpu.VMEM((rows, lanes), jnp.float32),
             pltpu.VMEM((count * down_rows, D), jnp.float32),
@@ -460,19 +463,40 @@
     )
 
 
-def attention_forward(bounds, table, query_rot, pair_halves, first_key, last_key):
+def visible_keys(table_ref, docs_ref, b):
+    count, block_len = docs_ref.shape
+    chip, core = rank()
+    block = table_ref[chip * 2 + core]
+    block = block if b == 0 else count - 1 - block
+    docs = docs_ref[...]
+    own = docs_ref[pl.ds(block, 1), :]
+    first = jnp.zeros((1, block_len), jnp.float32)
+    for doc in range(1, DOCS):
+        before = jnp.sum((docs < doc).astype(jnp.float32), axis=0, keepdims=True)
+        start = jnp.sum(before, axis=1, keepdims=True)
+        first = jnp.where(own == doc, start, first)
+    begin = jnp.min(first).astype(jnp.int32) // (2 * block_len)
+    first = first.astype(jnp.int32)
+    last = block * block_len + lax.broadcasted_iota(jnp.int32, (1, block_len), 1)
+    return (
+        jnp.concatenate([first] * GROUPS, axis=1),
+        jnp.concatenate([last] * GROUPS, axis=1),
+        begin,
+        block // 2 + 1,
+    )
+
+
+def attention_forward(table, docs, query_rot, pair_halves):
     row_count = query_rot.shape[0]
     block_len = row_count // 2
     wide = GROUPS * block_len
 
     def kernel(
-        bounds_ref,
         table_ref,
+        docs_ref,
         query_ref,
         own_ref,
         other_ref,
-        first_ref,
-        last_ref,
         out_ref,
         log_ref,
         pairs_ref,
@@ -482,8 +506,7 @@
             rows = slice(b * block_len, (b + 1) * block_len)
             query_block = query_ref[rows, :]
             queries = [heads_to_rows(query_block, g) for g in range(KV_HEADS)]
-            first = jnp.concatenate([first_ref[b : b + 1, :]] * GROUPS, axis=1)
-            last = jnp.concatenate([last_ref[b : b + 1, :]] * GROUPS, axis=1)
+            first, last, begin, end = visible_keys(table_ref, docs_ref, b)
 
             def step(j, state):
                 start = pl.multiple_of(j * row_count, row_count)
@@ -506,8 +529,8 @@
                 return tuple(result)
 
             state = lax.fori_loop(
-                bounds_ref[2 * b],
-                bounds_ref[2 * b + 1],
+                begin,
+                end,
                 step,
                 tuple(
                     (
@@ -530,8 +553,8 @@
     return run_kernel(
         kernel,
         [((row_count, D), jnp.float32), ((2 * KV_HEADS, wide), jnp.float32)],
-        [bounds, table, query_rot, *pair_halves, first_key, last_key],
-        scalars=2,
+        [table, docs, query_rot, *pair_halves],
+        scalars=1,
         scratch=[pltpu.VMEM((table.shape[0] * row_count, 2 * KV_WIDTH), jnp.bfloat16)],
         microseconds=12,
     )
@@ -715,12 +738,10 @@
 
 
 def attention_backward(
-    bounds,
     table,
+    docs,
     query_rot,
     pair_halves,
-    first_key,
-    last_key,
     log_total,
     attended,
     grad_attended,
@@ -738,13 +759,11 @@
     half = HEAD // 2
 
     def kernel(
-        bounds_ref,
         table_ref,
+        docs_ref,
         query_ref,
         own_ref,
         other_ref,
-        first_ref,
-        last_ref,
         log_ref,
         attended_ref,
         grad_ref,
@@ -773,8 +792,7 @@
                 jnp.sum(heads_to_rows(product, g).T, axis=0, keepdims=True)
                 for g in range(KV_HEADS)
             ]
-            first = jnp.concatenate([first_ref[b : b + 1, :]] * GROUPS, axis=1)
-            last = jnp.concatenate([last_ref[b : b + 1, :]] * GROUPS, axis=1)
+            first, last, begin, end = visible_keys(table_ref, docs_ref, b)
 
             def step(j, state):
                 start = pl.multiple_of(j * row_count, row_count)
@@ -802,8 +820,8 @@
                 return tuple(result)
 
             state = lax.fori_loop(
-                bounds_ref[2 * b],
-                bounds_ref[2 * b + 1],
+                begin,
+                end,
                 step,
                 tuple(jnp.zeros((HEAD, wide), jnp.float32) for _ in range(KV_HEADS)),
             )
@@ -838,12 +856,10 @@
         [((row_count, D), jnp.bfloat16), ((D, D), jnp.bfloat16), half_shape]
         + [((row_count, 2 * KV_WIDTH), jnp.bfloat16)] * chips,
         [
-            bounds,
             table,
+            docs,
             query_rot,
             *pair_halves,
-            first_key,
-            last_key,
             log_total,
             attended,
             grad_attended,
@@ -853,7 +869,7 @@
             sin_own,
             hidden_half,
         ],
-        scalars=2,
+        scalars=1,
         scratch=[
             pltpu.VMEM((slots * row_count, 2 * KV_WIDTH), jnp.bfloat16),
             pltpu.VMEM((slots * row_count, 2 * KV_WIDTH), jnp.float32),
@@ -984,22 +1000,10 @@
         ]
         first = [mixed_all, jnp.concatenate([*units, mixed_all[:, 2 * KV_WIDTH + D :]], axis=1)]
 
+    docs = seq_ids[0].reshape(2 * count, block_len)
     own_block = lax.dynamic_index_in_dim(slot_table, index, 0, keepdims=False)
     own_blocks = jnp.stack([own_block, 2 * count - 1 - own_block])
     block_pos = own_blocks[:, None] * block_len + jnp.arange(block_len, dtype=jnp.int32)[None, :]
-    documents = seq_ids[0]
-    query_doc = jnp.stack(
-        [
-            lax.dynamic_slice(documents, (own_blocks[i] * block_len,), (block_len,))
-            for i in range(2)
-        ]
-    )
-    first_key = jnp.sum(
-        (documents[None, :, None] < query_doc[:, None, :]).astype(jnp.int32), axis=1
-    )
-    bounds = jnp.stack(
-        [jnp.min(first_key, axis=1) // row_count, own_blocks // 2 + 1], axis=1
-    ).reshape(4)
     half_width = after(jnp.arange(HEAD // 2, dtype=jnp.float32), hidden_half)
     frequencies = rope_base ** (-(half_width * 2.0 / HEAD))
     angles = jnp.arange(length, dtype=jnp.int32).astype(jnp.float32)[:, None] * frequencies[None, :]
@@ -1010,15 +1014,13 @@
 
     wide_rows = in_order(wide_own, wide_received, shards // 2)
     query_rot, own_pairs, mixed, out_w_all = project(
-        direct, slot_table, after(hidden_half, wide_rows, low_start, bounds, first_key, block_pos, cos_own, sin_own), first, cos_all, sin_all
+        direct, slot_table, after(hidden_half, wide_rows, low_start, cos_own, sin_own), first, cos_all, sin_all
     )
     pair_halves = (own_pairs, core_swap(own_pairs))
     wide_pieces = gather_same_core(wide_rows)
     low_own = finish_gather_half(after(low_start, wide_rows))
     grad_out = cotangent[0]
-    attended, log_total = attention_forward(
-        bounds, slot_table, query_rot, pair_halves, first_key, block_pos
-    )
+    attended, log_total = attention_forward(slot_table, docs, query_rot, pair_halves)
     grad_other = core_swap(after(grad_out, attended))
     residual, hidden_two = mix(attended, tokens_low, out_w_all, gain_two)
     if direct:
@@ -1071,12 +1073,10 @@
     )
 
     grad_query, query_w, pairs_kept, *pairs_sent = attention_backward(
-        bounds,
         slot_table,
+        docs,
         query_rot,
         pair_halves,
-        first_key,
-        block_pos,
         log_total,
         attended,
         grad_attended,
@@ -1121,7 +1121,7 @@
         first_sum = sum_chips(mixed_sums).astype(jnp.bfloat16)
         owned = sum_chips(pair_sums).astype(jnp.bfloat16)
     first_part = sum_rows(first_sum).astype(jnp.bfloat16)
-    first_all = gather_chips(first_part)
+    first_mine = gather_same_core(first_part)
     wide_sum = sum_chips(wide_grads, pair_sums[0]).astype(jnp.bfloat16)
     wide_sum = jnp.concatenate(
         [wide_sum[:, :, :lanes], by_core_slices(wide_sum[:, :, lanes:])], axis=2
@@ -1143,6 +1143,7 @@
             wide_all, w_gate, w_up, gain_rows[1], pile
         )
         down_grad = down_grad.T
+        first_all = first_mine + [core_swap(v) for v in after(tuple(first_mine), gain_grad_two)]
         query_w, key_w, value_w, out_w, gain_grad_one = finish_first(
             first_all, mixed_shard, gain_rows[0]
         )
@@ -1158,7 +1159,7 @@
             ).astype(jnp.float32)
             for n in (0, chips // 2)
         )
-        ordered = in_rank_order(first_all)
+        ordered = in_rank_order(first_mine + [core_swap(v) for v in first_mine])
         first_grad = jnp.concatenate([v[:rows] for v in ordered], axis=1).astype(jnp.float32)
         units = [
             v[rows:].reshape(rows // 2, 2, -1).transpose(1, 0, 2).reshape(rows, -1) for v in ordered

time: 190 us -> 185 us (0.974)
  waiting for transfers between devices: 24.3 us -> 21.7 us
    ppermute x57, waiting for transfers between devices: 23.9 us -> 21.4 us  [swap(): return lax.ppermute(value, axis, [(i, i ^ offset) for i in range(count)])]
  transfers between devices with their start and end apart: 58 -> 58, of which waited for: 19 -> 18; matrix products, arithmetic and copies ran while one was open for 12% -> 11% of each run, Pallas kernels for 20% -> 21%
where the time goes in v4:
time: 185 us; the launch traced here: 184 us
  starting transfers between devices  72.3 us (39%)
  Pallas kernels  56.8 us (31%)
  waiting for transfers between devices  21.7 us (12%)
  local copies, waits for them, and re-layouts  18.4 us (10%)
  other arithmetic  12.1 us (7%)
  between operations  2.14 us (1%)
    ppermute x57, starting transfers between devices, swap(): return lax.ppermute(value, axis, [(i, i ^ offset) for i in range(count)])  68.6 us
    pallas_call x10, Pallas kernels, run_kernel(): pl.pallas_call(kernel, out_shape=tuple((jax.ShapeDtypeStruct(*out) for ou...  56.8 us
    ppermute x57, waiting for transfers between devices, swap(): return lax.ppermute(value, axis, [(i, i ^ offset) for i in range(count)])  21.4 us
    unnamed x124, local copies, waits for them, and re-layouts  11.3 us
    ppermute x1, starting transfers between devices, start_gather_half(): received = lax.ppermute(piece, ('ctx', 'fsdp'), half_pairs())  3.79 us
  transfers between devices with their start and end apart: 58, of which 18 were waited for; matrix products, arithmetic and copies ran while one was open for 11% of the time, Pallas kernels for 21%

profile of v4, /device:TPU:0, one launch (start us, length us, event | category | flops | bytes accessed | tf_op | source)
XLA Modules:
  0.0 184.1 jit_solution(18434860767996406577)
XLA Ops:
  0.7 1.2 copy.32
  1.9 3.0 %collective-permute-start = (bf16[256,576]{1,0:T(8,128)(2,1)S(1)}, bf16[256,576]{1,0:T(8,128)(2,1)S(1)}, u32[]{:S(2)}, u32[]{:S(2)}) collective-permute-start(bf16[256,576]{1,0:T(8,128)(2,1)S(1)} %bitcast.70), channel_id=1, source_target_pairs={{0,8},{4,12},{8,0},{12,4},{16,24},{20,28},{24,16},{28,20},{1,9},{5... | collective-permute-start | bytes 884744 | tf_op jit(solution)/shard_map/ppermute | solution.py:45
  4.9 1.5 collective-permute-start.1
  7.9 1.1 pad_maximum_fusion.5.refs_8_
  10.0 2.0 %collective-permute-start.3 = (bf16[1,232,128]{2,1,0:T(8,128)(2,1)S(1)}, bf16[1,232,128]{2,1,0:T(8,128)(2,1)S(1)}, u32[]{:S(2)}, u32[]{:S(2)}) collective-permute-start(bf16[1,232,128]{2,1,0:T(8,128)(2,1)S(1)} %maximum_bitcast_fusion), channel_id=1, source_target_pairs={{0,1},{1,0},{2,3},{3,2},{4,5},{5,4},{6,7},{7,6},{8,9},{9,8},{10,11... | collective-permute-start | bytes 178184 | tf_op jit(solution)/shard_map/ppermute | solution.py:45
  15.3 3.0 %collective-permute-start.4 = (bf16[2,232,128]{2,1,0:T(8,128)(2,1)S(1)}, bf16[2,232,128]{2,1,0:T(8,128)(2,1)S(1)}, u32[]{:S(2)}, u32[]{:S(2)}) collective-permute-start(bf16[2,232,128]{2,1,0:T(8,128)(2,1)S(1)} %pad_maximum_fusion.8), channel_id=1, source_target_pairs={{0,2},{1,3},{2,0},{3,1},{4,6},{5,7},{6,4},{7,5},{8,10},{9,11},{10,... | collective-permute-start | bytes 356360 | tf_op jit(solution)/shard_map/ppermute | solution.py:45
  19.1 4.0 %collective-permute-done.4 = bf16[2,232,128]{2,1,0:T(8,128)(2,1)S(1)} collective-permute-done((bf16[2,232,128]{2,1,0:T(8,128)(2,1)S(1)}, bf16[2,232,128]{2,1,0:T(8,128)(2,1)S(1)}, u32[]{:S(2)}, u32[]{:S(2)}) %collective-permute-start.4) | collective-permute-done | bytes 118816 | tf_op jit(solution)/shard_map/ppermute | solution.py:45
  24.0 1.1 collective-permute-start.6
  26.7 2.9 %shard_map.212.hidden_ref = bf16[4,256,576]{2,1,0:T(8,128)(2,1)} custom-call(bf16[256,576]{1,0:T(8,128)(2,1)} %bitcast.73, bf16[256,576]{1,0:T(8,128)(2,1)} %copy-done.30, bf16[256,576]{1,0:T(8,128)(2,1)} %copy-done.31, bf16[256,576]{1,0:T(8,128)(2,1)} %copy-done.32, f32[1,576]{1,0:T(1,128)} %reshape.185.refs_4_), custom_call_target="tpu_custom_call" | custom-call | flops 3449999872 | bytes 1024 | tf_op jit(solution)/shard_map/pallas_call | solution.py:25
  29.5 1.5 collective-permute-start.8
  31.0 1.5 collective-permute-start.9
  33.3 3.8 %collective-permute-start.7 = (bf16[384,576]{1,0:T(8,128)(2,1)S(1)}, bf16[384,576]{1,0:T(8,128)(2,1)S(1)}, u32[]{:S(2)}, u32[]{:S(2)}) collective-permute-start(bf16[384,576]{1,0:T(8,128)(2,1)S(1)} %copy.34), channel_id=1, source_target_pairs={{0,2},{1,3},{6,4},{7,5},{8,10},{9,11},{14,12},{15,13},{16,18},{17,... | collective-permute-start | bytes 1327112 | tf_op jit(solution)/shard_map/ppermute | solution.py:99
  39.0 1.4 copy.35.cos_ref
  40.5 1.3 copy.36.sin_ref
  45.0 5.5 %shard_map.213 = (bf16[256,576]{1,0:T(8,128)(2,1)}, bf16[4,256,384]{2,1,0:T(8,128)(2,1)}, bf16[576,1024]{1,0:T(8,128)(2,1)}, bf16[576,576]{1,0:T(8,128)(2,1)}) custom-call(s32[8]{0:T(128)} %table_ref.5, bf16[4,256,576]{2,1,0:T(8,128)(2,1)} %shard_map.212.hidden_ref, f32[2048,128]{1,0:T(8,128)} %copy.35.cos_ref, f32[2048,128]{1,0:T(8,128)} %copy.36.sin_ref, ...), custom_call_target="tpu_custom_call" | custom-call | flops 5750000128 | bytes 1024 | tf_op jit(solution)/shard_map/pallas_call | solution.py:25
  50.5 1.4 collective-permute-start.15
  52.8 1.5 collective-permute-start.19
  54.3 1.5 collective-permute-start.20
  56.3 4.1 %collective-permute-start.18 = (bf16[1,384,576]{2,1,0:T(8,128)(2,1)S(1)}, bf16[1,384,576]{2,1,0:T(8,128)(2,1)S(1)}, u32[]{:S(2)}, u32[]{:S(2)}) collective-permute-start(bf16[1,384,576]{2,1,0:T(8,128)(2,1)S(1)} %select_bitcast_fusion), channel_id=1, source_target_pairs={{0,1},{1,0},{2,3},{3,2},{4,5},{5,4},{6,7},{7,6},{8,9},{9,8},{10,11... | collective-permute-start | bytes 1327112 | tf_op jit(solution)/shard_map/ppermute | solution.py:45
  61.2 7.4 %shard_map.214 = (f32[256,576]{1,0:T(8,128)}, f32[6,384]{1,0:T(8,128)}) custom-call(s32[8]{0:T(128)} %table_ref.5, s32[16,128]{1,0:T(8,128)} %bitcast.87, bf16[256,576]{1,0:T(8,128)(2,1)} %get-tuple-element.78.query_ref, bf16[4,256,384]{2,1,0:T(8,128)(2,1)} %get-tuple-element.79.own_ref, bf16[4,256,384]{2,1,0:T(8,128)(2,1)} %copy-done.26), custom_call_target="tpu_custom_call" | custom-call | flops 13799999488 | bytes 1024 | tf_op jit(solution)/shard_map/pallas_call | solution.py:25
  68.6 2.9 %shard_map.215 = (f32[256,576]{1,0:T(8,128)}, bf16[256,576]{1,0:T(8,128)(2,1)}) custom-call(f32[256,576]{1,0:T(8,128)} %get-tuple-element.80.attended_ref, bf16[256,576]{1,0:T(8,128)(2,1)} %bitcast.74, bf16[576,576]{1,0:T(8,128)(2,1)} %get-tuple-element.81.out_w_ref, f32[1,576]{1,0:T(1,128)} %reshape.186.gain_ref), custom_call_target="tpu_custom_call" | custom-call | flops 2300000000 | bytes 1024 | tf_op jit(solution)/shard_map/pallas_call | solution.py:25
  71.5 4.1 %collective-permute-start.16 = (bf16[256,576]{1,0:T(8,128)(2,1)}, bf16[256,576]{1,0:T(8,128)(2,1)S(1)}, u32[]{:S(2)}, u32[]{:S(2)}) collective-permute-start(bf16[256,576]{1,0:T(8,128)(2,1)} %get-tuple-element.83.hidden_ref), channel_id=1, source_target_pairs={{0,4},{4,0},{8,12},{12,8},{16,20},{20,16},{24,28},{28,24},{1,5},{5... | collective-permute-start | bytes 884744 | tf_op jit(solution)/shard_map/ppermute | solution.py:45
  78.7 10.5 %shard_map.216 = (f32[256,576]{1,0:T(8,128)}, f32[256,576]{1,0:T(8,128)}, bf16[2,256,640]{2,1,0:T(8,128)(2,1)}, bf16[4,144,576]{2,1,0:T(8,128)(2,1)}, bf16[4,144...) custom-call(bf16[256,576]{1,0:T(8,128)(2,1)} %get-tuple-element.83.hidden_ref, ...), custom_call_target="tpu_custom_call" | custom-call | flops 13799999488 | bytes 1024 | tf_op jit(solution)/shard_map/pallas_call | solution.py:25
  89.6 1.5 collective-permute-start.40
  91.1 2.0 %collective-permute-start.42 = (bf16[4,144,576]{2,1,0:T(8,128)(2,1)}, bf16[4,144,576]{2,1,0:T(8,128)(2,1)S(1)}, u32[]{:S(2)}, u32[]{:S(2)}) collective-permute-start(bf16[4,144,576]{2,1,0:T(8,128)(2,1)} %get-tuple-element.117), channel_id=1, source_target_pairs={{0,24},{4,28},{8,16},{12,20},{16,8},{20,12},{24,0},{28,4},{1,25},{... | collective-permute-start | bytes 1990664 | tf_op jit(solution)/shard_map/ppermute | solution.py:45
  93.9 4.1 %shard_map.217 = (bf16[576,256]{1,0:T(8,128)(2,1)}, f32[256,576]{1,0:T(8,128)}, bf16[256,576]{1,0:T(8,128)(2,1)}, bf16[576,576]{1,0:T(8,128)(2,1)}) custom-call(f32[256,576]{1,0:T(8,128)} %get-tuple-element.82.residual_ref, f32[256,576]{1,0:T(8,128)} %get-tuple-element.86.out_kept_ref, f32[256,576]{1,0:T(8,128)} %get-tuple-element.87.grad_kept_ref, ...), custom_call_target="tpu_custom_call" | custom-call | flops 4600000000 | bytes 1024 | tf_op jit(solution)/shard_map/pallas_call | solution.py:25
  98.0 11.9 %shard_map.218 = (bf16[256,576]{1,0:T(8,128)(2,1)}, bf16[576,576]{1,0:T(8,128)(2,1)}, bf16[4,256,384]{2,1,0:T(8,128)(2,1)}, bf16[256,384]{1,0:T(8,128)(2,1)}, bf...) custom-call(s32[8]{0:T(128)} %table_ref.5, s32[16,128]{1,0:T(8,128)} %bitcast.88, ...), custom_call_target="tpu_custom_call" | custom-call | flops 20700000256 | bytes 1024 | tf_op jit(solution)/shard_map/pallas_call | solution.py:25
  109.9 4.7 %collective-permute-start.23 = (bf16[256,384]{1,0:T(8,128)(2,1)}, bf16[256,384]{1,0:T(8,128)(2,1)S(1)}, u32[]{:S(2)}, u32[]{:S(2)}) collective-permute-start(bf16[256,384]{1,0:T(8,128)(2,1)} %get-tuple-element.96), channel_id=1, source_target_pairs={{0,4},{4,0},{8,12},{12,8},{16,20},{20,16},{24,28},{28,24},{1,5},{5... | collective-permute-start | bytes 589832 | tf_op jit(solution)/shard_map/ppermute | solution.py:45
  114.7 1.2 collective-permute-done.23.refs_0_
  118.6 5.1 %shard_map.219 = (bf16[768,128]{1,0:T(8,128)(2,1)}, bf16[768,128]{1,0:T(8,128)(2,1)}, bf16[768,128]{1,0:T(8,128)(2,1)}, bf16[768,128]{1,0:T(8,128)(2,1)}, bf16[4...) custom-call(bf16[4,256,384]{2,1,0:T(8,128)(2,1)} %get-tuple-element., ...), custom_call_target="tpu_custom_call" | custom-call | bytes 1024 | tf_op jit(solution)/shard_map/pallas_call | solution.py:25
  123.7 1.6 collective-permute-done.41
  128.3 1.2 collective-permute-start.33
  131.5 5.9 %collective-permute-start.46 = (bf16[144,576]{1,0:T(8,128)(2,1)S(1)}, bf16[144,576]{1,0:T(8,128)(2,1)S(1)}, u32[]{:S(2)}, u32[]{:S(2)}) collective-permute-start(bf16[144,576]{1,0:T(8,128)(2,1)S(1)} %get-tuple-element.160), channel_id=1, source_target_pairs={{0,3},{1,2},{2,1},{3,0},{4,7},{5,6},{6,5},{7,4},{8,11},{9,10},{10,... | collective-permute-start | bytes 497672 | tf_op jit(solution)/shard_map/ppermute | solution.py:45
  137.4 1.3 collective-permute-start.29
  138.7 4.2 %collective-permute-done.46 = bf16[144,576]{1,0:T(8,128)(2,1)S(1)} collective-permute-done((bf16[144,576]{1,0:T(8,128)(2,1)S(1)}, bf16[144,576]{1,0:T(8,128)(2,1)S(1)}, u32[]{:S(2)}, u32[]{:S(2)}) %collective-permute-start.46) | collective-permute-done | bytes 165920 | tf_op jit(solution)/shard_map/ppermute | solution.py:45
  143.7 7.0 %collective-permute-start.44 = (bf16[144,576]{1,0:T(8,128)(2,1)}, bf16[144,576]{1,0:T(8,128)(2,1)}, u32[]{:S(2)}, u32[]{:S(2)}) collective-permute-start(bf16[144,576]{1,0:T(8,128)(2,1)} %get-tuple-element.159), channel_id=1, source_target_pairs={{0,1},{1,0},{2,3},{3,2},{4,5},{5,4},{6,7},{7,6},{8,9},{9,8},{10,11... | collective-permute-start | bytes 497672 | tf_op jit(solution)/shard_map/ppermute | solution.py:45
  150.8 1.6 collective-permute-done.45
  152.4 3.8 %collective-permute-done.44 = bf16[144,576]{1,0:T(8,128)(2,1)} collective-permute-done((bf16[144,576]{1,0:T(8,128)(2,1)}, bf16[144,576]{1,0:T(8,128)(2,1)}, u32[]{:S(2)}, u32[]{:S(2)}) %collective-permute-start.44) | collective-permute-done | bytes 165920 | tf_op jit(solution)/shard_map/ppermute | solution.py:45
  156.3 1.2 fusion.18.refs_0_
  157.5 1.3 collective-permute-start.47
  159.6 1.4 collective-permute-start.49
  161.1 1.4 add_convert_fusion.1
  162.5 1.6 collective-permute-start.36
  165.1 2.7 %collective-permute-start.34 = (bf16[216,128]{1,0:T(8,128)(2,1)S(1)}, bf16[216,128]{1,0:T(8,128)(2,1)S(1)}, u32[]{:S(2)}, u32[]{:S(2)}) collective-permute-start(bf16[216,128]{1,0:T(8,128)(2,1)S(1)} %get-tuple-element.171), channel_id=1, source_target_pairs={{0,1},{1,0},{2,3},{3,2},{4,5},{5,4},{6,7},{7,6},{8,9},{9,8},{10,11... | collective-permute-start | bytes 165896 | tf_op jit(solution)/shard_map/ppermute | solution.py:45
  170.3 1.5 collective-permute-start.37
  172.4 1.5 collective-permute-start.39
  174.6 4.1 %shard_map.220 = (f32[144,1536]{1,0:T(8,128)}, f32[144,1536]{1,0:T(8,128)}, f32[576,384]{1,0:T(8,128)}, f32[1,144]{1,0:T(1,128)}) custom-call(bf16[144,576]{1,0:T(8,128)(2,1)} %copy-done.21, bf16[144,576]{1,0:T(8,128)(2,1)} %copy-done.43, bf16[144,576]{1,0:T(8,128)(2,1)} %copy-done.44, bf16[144,576]{1,0:T(8,128)(2,1)} %copy-done.45, ...), custom_call_target="tpu_custom_call" | custom-call | flops 4600000000 | bytes 1024 | tf_op jit(solution)/shard_map/pallas_call | solution.py:25
  181.7 2.4 %shard_map.221 = (f32[144,576]{1,0:T(8,128)}, f32[144,192]{1,0:T(8,128)}, f32[144,192]{1,0:T(8,128)}, f32[144,576]{1,0:T(8,128)}, f32[1,144]{1,0:T(1,128)}) custom-call(bf16[216,128]{1,0:T(8,128)(2,1)} %copy-done.23, bf16[216,128]{1,0:T(8,128)(2,1)} %copy-done.50, bf16[216,128]{1,0:T(8,128)(2,1)} %copy-done.51, bf16[216,128]{1,0:T(8,128)(2,1)} %copy-done.52, ...), custom_call_target="tpu_custom_call" | custom-call | flops 2300000000 | bytes 1024 | tf_op jit(solution)/shard_map/pallas_call | solution.py:25
  (267 shorter events, 37.3 us)
Async XLA Ops:
  1.9 23.2 %collective-permute-start = (bf16[256,576]{1,0:T(8,128)(2,1)S(1)}, bf16[256,576]{1,0:T(8,128)(2,1)S(1)}, u32[]{:S(2)}, u32[]{:S(2)}) collective-permute-start(bf16[256,576]{1,0:T(8,128)(2,1)S(1)} %bitcast.70), channel_id=1, source_target_pairs={{0,8},{4,12},{8,0},{12,4},{16,24},{20,28},{24,16},{28,20},{1,9},{5... | collective-permute-start | bytes 884744 | tf_op jit(solution)/shard_map/ppermute | solution.py:45
  4.9 20.2 %collective-permute-start.1 = (bf16[256,576]{1,0:T(8,128)(2,1)S(1)}, bf16[256,576]{1,0:T(8,128)(2,1)S(1)}, u32[]{:S(2)}, u32[]{:S(2)}) collective-permute-start(bf16[256,576]{1,0:T(8,128)(2,1)S(1)} %bitcast.71), channel_id=1, source_target_pairs={{0,16},{4,20},{8,24},{12,28},{16,0},{20,4},{24,8},{28,12},{1,17},{... | collective-permute-start | bytes 884744 | tf_op jit(solution)/shard_map/ppermute | solution.py:45
  6.4 18.7 %collective-permute-start.2 = (bf16[256,576]{1,0:T(8,128)(2,1)S(1)}, bf16[256,576]{1,0:T(8,128)(2,1)S(1)}, u32[]{:S(2)}, u32[]{:S(2)}) collective-permute-start(bf16[256,576]{1,0:T(8,128)(2,1)S(1)} %bitcast.72), channel_id=1, source_target_pairs={{0,24},{4,28},{8,16},{12,20},{16,8},{20,12},{24,0},{28,4},{1,25},{... | collective-permute-start | bytes 884744 | tf_op jit(solution)/shard_map/ppermute | solution.py:45
  10.0 5.2 %collective-permute-start.3 = (bf16[1,232,128]{2,1,0:T(8,128)(2,1)S(1)}, bf16[1,232,128]{2,1,0:T(8,128)(2,1)S(1)}, u32[]{:S(2)}, u32[]{:S(2)}) collective-permute-start(bf16[1,232,128]{2,1,0:T(8,128)(2,1)S(1)} %maximum_bitcast_fusion), channel_id=1, source_target_pairs={{0,1},{1,0},{2,3},{3,2},{4,5},{5,4},{6,7},{7,6},{8,9},{9,8},{10,11... | collective-permute-start | bytes 178184 | tf_op jit(solution)/shard_map/ppermute | solution.py:45
  13.0 6.0 %collective-permute-start.5 = (bf16[1,144,384]{2,1,0:T(8,128)(2,1)S(1)}, bf16[1,144,384]{2,1,0:T(8,128)(2,1)S(1)}, u32[]{:S(2)}, u32[]{:S(2)}) collective-permute-start(bf16[1,144,384]{2,1,0:T(8,128)(2,1)S(1)} %fusion.20), channel_id=1, source_target_pairs={{0,1},{1,0},{2,3},{3,2},{4,5},{5,4},{6,7},{7,6},{8,9},{9,8},{10,11... | collective-permute-start | bytes 331784 | tf_op jit(solution)/shard_map/ppermute | solution.py:45
  15.3 7.8 %collective-permute-start.4 = (bf16[2,232,128]{2,1,0:T(8,128)(2,1)S(1)}, bf16[2,232,128]{2,1,0:T(8,128)(2,1)S(1)}, u32[]{:S(2)}, u32[]{:S(2)}) collective-permute-start(bf16[2,232,128]{2,1,0:T(8,128)(2,1)S(1)} %pad_maximum_fusion.8), channel_id=1, source_target_pairs={{0,2},{1,3},{2,0},{3,1},{4,6},{5,7},{6,4},{7,5},{8,10},{9,11},{10,... | collective-permute-start | bytes 356360 | tf_op jit(solution)/shard_map/ppermute | solution.py:45
  24.0 17.9 %collective-permute-start.6 = (bf16[2,144,384]{2,1,0:T(8,128)(2,1)S(1)}, bf16[2,144,384]{2,1,0:T(8,128)(2,1)S(1)}, u32[]{:S(2)}, u32[]{:S(2)}) collective-permute-start(bf16[2,144,384]{2,1,0:T(8,128)(2,1)S(1)} %pad_maximum_fusion.7), channel_id=1, source_target_pairs={{0,2},{1,3},{2,0},{3,1},{4,6},{5,7},{6,4},{7,5},{8,10},{9,11},{10,... | collective-permute-start | bytes 663560 | tf_op jit(solution)/shard_map/ppermute | solution.py:45
  29.5 12.4 %collective-permute-start.8 = (bf16[4,232,128]{2,1,0:T(8,128)(2,1)S(1)}, bf16[4,232,128]{2,1,0:T(8,128)(2,1)S(1)}, u32[]{:S(2)}, u32[]{:S(2)}) collective-permute-start(bf16[4,232,128]{2,1,0:T(8,128)(2,1)S(1)} %pad_maximum_fusion.6.refs_0_), channel_id=1, source_target_pairs={{0,8},{4,12},{8,0},{12,4},{16,24},{20,28},{24,16},{28,20},{1,9},{5... | collective-permute-start | bytes 712712 | tf_op jit(solution)/shard_map/ppermute | solution.py:45
  31.0 11.5 %collective-permute-start.9 = (bf16[4,232,128]{2,1,0:T(8,128)(2,1)S(1)}, bf16[4,232,128]{2,1,0:T(8,128)(2,1)}, u32[]{:S(2)}, u32[]{:S(2)}) collective-permute-start(bf16[4,232,128]{2,1,0:T(8,128)(2,1)S(1)} %pad_maximum_fusion.6.refs_0_), channel_id=1, source_target_pairs={{0,16},{4,20},{8,24},{12,28},{16,0},{20,4},{24,8},{28,12},{1,17},{... | collective-permute-start | bytes 712712 | tf_op jit(solution)/shard_map/ppermute | solution.py:45
  32.5 10.1 %collective-permute-start.10 = (bf16[4,232,128]{2,1,0:T(8,128)(2,1)S(1)}, bf16[4,232,128]{2,1,0:T(8,128)(2,1)}, u32[]{:S(2)}, u32[]{:S(2)}) collective-permute-start(bf16[4,232,128]{2,1,0:T(8,128)(2,1)S(1)} %pad_maximum_fusion.6.refs_0_), channel_id=1, source_target_pairs={{0,24},{4,28},{8,16},{12,20},{16,8},{20,12},{24,0},{28,4},{1,25},{... | collective-permute-start | bytes 712712 | tf_op jit(solution)/shard_map/ppermute | solution.py:45
  33.3 10.1 %collective-permute-start.7 = (bf16[384,576]{1,0:T(8,128)(2,1)S(1)}, bf16[384,576]{1,0:T(8,128)(2,1)S(1)}, u32[]{:S(2)}, u32[]{:S(2)}) collective-permute-start(bf16[384,576]{1,0:T(8,128)(2,1)S(1)} %copy.34), channel_id=1, source_target_pairs={{0,2},{1,3},{6,4},{7,5},{8,10},{9,11},{14,12},{15,13},{16,18},{17,... | collective-permute-start | bytes 1327112 | tf_op jit(solution)/shard_map/ppermute | solution.py:99
  42.6 2.1 %collective-permute-start.14 = (bf16[4,232,128]{2,1,0:T(8,128)(2,1)}, bf16[4,232,128]{2,1,0:T(8,128)(2,1)}, u32[]{:S(2)}, u32[]{:S(2)}) collective-permute-start(bf16[4,232,128]{2,1,0:T(8,128)(2,1)} %collective-permute-done.10.refs_3_), channel_id=1, source_target_pairs={{0,4},{4,0},{8,12},{12,8},{16,20},{20,16},{24,28},{28,24},{1,5},{5... | collective-permute-start | bytes 712712 | tf_op jit(solution)/shard_map/ppermute | solution.py:45
  50.5 9.8 %collective-permute-start.15 = (bf16[4,256,384]{2,1,0:T(8,128)(2,1)}, bf16[4,256,384]{2,1,0:T(8,128)(2,1)S(1)}, u32[]{:S(2)}, u32[]{:S(2)}) collective-permute-start(bf16[4,256,384]{2,1,0:T(8,128)(2,1)} %get-tuple-element.79.own_ref), channel_id=1, source_target_pairs={{0,4},{4,0},{8,12},{12,8},{16,20},{20,16},{24,28},{28,24},{1,5},{5... | collective-permute-start | bytes 2359304 | tf_op jit(solution)/shard_map/ppermute | solution.py:45
  52.8 24.1 %collective-permute-start.19 = (bf16[4,144,384]{2,1,0:T(8,128)(2,1)S(1)}, bf16[4,144,384]{2,1,0:T(8,128)(2,1)S(1)}, u32[]{:S(2)}, u32[]{:S(2)}) collective-permute-start(bf16[4,144,384]{2,1,0:T(8,128)(2,1)S(1)} %pad_maximum_fusion.1.refs_0_), channel_id=1, source_target_pairs={{0,8},{4,12},{8,0},{12,4},{16,24},{20,28},{24,16},{28,20},{1,9},{5... | collective-permute-start | bytes 1327112 | tf_op jit(solution)/shard_map/ppermute | solution.py:45
  54.3 22.7 %collective-permute-start.20 = (bf16[4,144,384]{2,1,0:T(8,128)(2,1)S(1)}, bf16[4,144,384]{2,1,0:T(8,128)(2,1)S(1)}, u32[]{:S(2)}, u32[]{:S(2)}) collective-permute-start(bf16[4,144,384]{2,1,0:T(8,128)(2,1)S(1)} %pad_maximum_fusion.1.refs_0_), channel_id=1, source_target_pairs={{0,16},{4,20},{8,24},{12,28},{16,0},{20,4},{24,8},{28,12},{1,17},{... | collective-permute-start | bytes 1327112 | tf_op jit(solution)/shard_map/ppermute | solution.py:45
  55.8 21.1 %collective-permute-start.21 = (bf16[4,144,384]{2,1,0:T(8,128)(2,1)S(1)}, bf16[4,144,384]{2,1,0:T(8,128)(2,1)}, u32[]{:S(2)}, u32[]{:S(2)}) collective-permute-start(bf16[4,144,384]{2,1,0:T(8,128)(2,1)S(1)} %pad_maximum_fusion.1.refs_0_), channel_id=1, source_target_pairs={{0,24},{4,28},{8,16},{12,20},{16,8},{20,12},{24,0},{28,4},{1,25},{... | collective-permute-start | bytes 1327112 | tf_op jit(solution)/shard_map/ppermute | solution.py:45
  56.3 19.4 %collective-permute-start.18 = (bf16[1,384,576]{2,1,0:T(8,128)(2,1)S(1)}, bf16[1,384,576]{2,1,0:T(8,128)(2,1)S(1)}, u32[]{:S(2)}, u32[]{:S(2)}) collective-permute-start(bf16[1,384,576]{2,1,0:T(8,128)(2,1)S(1)} %select_bitcast_fusion), channel_id=1, source_target_pairs={{0,1},{1,0},{2,3},{3,2},{4,5},{5,4},{6,7},{7,6},{8,9},{9,8},{10,11... | collective-permute-start | bytes 1327112 | tf_op jit(solution)/shard_map/ppermute | solution.py:45
  71.5 5.6 %collective-permute-start.16 = (bf16[256,576]{1,0:T(8,128)(2,1)}, bf16[256,576]{1,0:T(8,128)(2,1)S(1)}, u32[]{:S(2)}, u32[]{:S(2)}) collective-permute-start(bf16[256,576]{1,0:T(8,128)(2,1)} %get-tuple-element.83.hidden_ref), channel_id=1, source_target_pairs={{0,4},{4,0},{8,12},{12,8},{16,20},{20,16},{24,28},{28,24},{1,5},{5... | collective-permute-start | bytes 884744 | tf_op jit(solution)/shard_map/ppermute | solution.py:45
  89.2 3.9 %collective-permute-start.22 = (bf16[2,256,640]{2,1,0:T(8,128)(2,1)}, bf16[2,256,640]{2,1,0:T(8,128)(2,1)S(1)}, u32[]{:S(2)}, u32[]{:S(2)}) collective-permute-start(bf16[2,256,640]{2,1,0:T(8,128)(2,1)} %get-tuple-element.88), channel_id=1, source_target_pairs={{0,4},{4,0},{8,12},{12,8},{16,20},{20,16},{24,28},{28,24},{1,5},{5... | collective-permute-start | bytes 1966088 | tf_op jit(solution)/shard_map/ppermute | solution.py:45
  89.6 34.1 %collective-permute-start.40 = (bf16[4,144,576]{2,1,0:T(8,128)(2,1)}, bf16[4,144,576]{2,1,0:T(8,128)(2,1)S(1)}, u32[]{:S(2)}, u32[]{:S(2)}) collective-permute-start(bf16[4,144,576]{2,1,0:T(8,128)(2,1)} %get-tuple-element.115), channel_id=1, source_target_pairs={{0,8},{4,12},{8,0},{12,4},{16,24},{20,28},{24,16},{28,20},{1,9},{5... | collective-permute-start | bytes 1990664 | tf_op jit(solution)/shard_map/ppermute | solution.py:45
  91.1 34.2 %collective-permute-start.41 = (bf16[4,144,576]{2,1,0:T(8,128)(2,1)}, bf16[4,144,576]{2,1,0:T(8,128)(2,1)S(1)}, u32[]{:S(2)}, u32[]{:S(2)}) collective-permute-start(bf16[4,144,576]{2,1,0:T(8,128)(2,1)} %get-tuple-element.116), channel_id=1, source_target_pairs={{0,16},{4,20},{8,24},{12,28},{16,0},{20,4},{24,8},{28,12},{1,17},{... | collective-permute-start | bytes 1990664 | tf_op jit(solution)/shard_map/ppermute | solution.py:45
  91.1 34.2 %collective-permute-start.42 = (bf16[4,144,576]{2,1,0:T(8,128)(2,1)}, bf16[4,144,576]{2,1,0:T(8,128)(2,1)S(1)}, u32[]{:S(2)}, u32[]{:S(2)}) collective-permute-start(bf16[4,144,576]{2,1,0:T(8,128)(2,1)} %get-tuple-element.117), channel_id=1, source_target_pairs={{0,24},{4,28},{8,16},{12,20},{16,8},{20,12},{24,0},{28,4},{1,25},{... | collective-permute-start | bytes 1990664 | tf_op jit(solution)/shard_map/ppermute | solution.py:45
  109.9 6.0 %collective-permute-start.23 = (bf16[256,384]{1,0:T(8,128)(2,1)}, bf16[256,384]{1,0:T(8,128)(2,1)S(1)}, u32[]{:S(2)}, u32[]{:S(2)}) collective-permute-start(bf16[256,384]{1,0:T(8,128)(2,1)} %get-tuple-element.96), channel_id=1, source_target_pairs={{0,4},{4,0},{8,12},{12,8},{16,20},{20,16},{24,28},{28,24},{1,5},{5... | collective-permute-start | bytes 589832 | tf_op jit(solution)/shard_map/ppermute | solution.py:45
  125.8 1.9 %collective-permute-start.43 = (bf16[2,144,192]{2,1,0:T(8,128)(2,1)S(1)}, bf16[2,144,192]{2,1,0:T(8,128)(2,1)S(1)}, u32[]{:S(2)}, u32[]{:S(2)}) collective-permute-start(bf16[2,144,192]{2,1,0:T(8,128)(2,1)S(1)} %dynamic-slice_bitcast_fusion.3), channel_id=1, source_target_pairs={{0,4},{4,0},{8,12},{12,8},{16,20},{20,16},{24,28},{28,24},{1,5},{5... | collective-permute-start | bytes 331784 | tf_op jit(solution)/shard_map/ppermute | solution.py:45
  126.8 2.8 %collective-permute-start.30 = (bf16[4,216,128]{2,1,0:T(8,128)(2,1)S(1)}, bf16[4,216,128]{2,1,0:T(8,128)(2,1)S(1)}, u32[]{:S(2)}, u32[]{:S(2)}) collective-permute-start(bf16[4,216,128]{2,1,0:T(8,128)(2,1)S(1)} %copy-done.41), channel_id=1, source_target_pairs={{0,4},{4,0},{8,12},{12,8},{16,20},{20,16},{24,28},{28,24},{1,5},{5... | collective-permute-start | bytes 663560 | tf_op jit(solution)/shard_map/ppermute | solution.py:45
  127.2 3.4 %collective-permute-start.28 = (bf16[4,216,128]{2,1,0:T(8,128)(2,1)S(1)}, bf16[4,216,128]{2,1,0:T(8,128)(2,1)S(1)}, u32[]{:S(2)}, u32[]{:S(2)}) collective-permute-start(bf16[4,216,128]{2,1,0:T(8,128)(2,1)S(1)} %copy-done.40), channel_id=1, source_target_pairs={{0,4},{4,0},{8,12},{12,8},{16,20},{20,16},{24,28},{28,24},{1,5},{5... | collective-permute-start | bytes 663560 | tf_op jit(solution)/shard_map/ppermute | solution.py:45
  127.3 3.3 %collective-permute-start.27 = (bf16[4,216,128]{2,1,0:T(8,128)(2,1)S(1)}, bf16[4,216,128]{2,1,0:T(8,128)(2,1)S(1)}, u32[]{:S(2)}, u32[]{:S(2)}) collective-permute-start(bf16[4,216,128]{2,1,0:T(8,128)(2,1)S(1)} %copy-done.39), channel_id=1, source_target_pairs={{0,4},{4,0},{8,12},{12,8},{16,20},{20,16},{24,28},{28,24},{1,5},{5... | collective-permute-start | bytes 663560 | tf_op jit(solution)/shard_map/ppermute | solution.py:45
  128.3 31.3 %collective-permute-start.33 = (bf16[1632,128]{1,0:T(8,128)(2,1)S(1)}, bf16[1632,128]{1,0:T(8,128)(2,1)S(1)}, u32[]{:S(2)}, u32[]{:S(2)}) collective-permute-start(bf16[1632,128]{1,0:T(8,128)(2,1)S(1)} %pad_maximum_fusion.4), channel_id=1, source_target_pairs={{0,24},{4,28},{8,16},{12,20},{16,8},{20,12},{24,0},{28,4},{1,25},{... | collective-permute-start | bytes 1253384 | tf_op jit(solution)/shard_map/ppermute | solution.py:45
  129.6 31.4 %collective-permute-start.31 = (bf16[1632,128]{1,0:T(8,128)(2,1)S(1)}, bf16[1632,128]{1,0:T(8,128)(2,1)S(1)}, u32[]{:S(2)}, u32[]{:S(2)}) collective-permute-start(bf16[1632,128]{1,0:T(8,128)(2,1)S(1)} %pad_maximum_fusion.3), channel_id=1, source_target_pairs={{0,16},{4,20},{8,24},{12,28},{16,0},{20,4},{24,8},{28,12},{1,17},{... | collective-permute-start | bytes 1253384 | tf_op jit(solution)/shard_map/ppermute | solution.py:45
  131.5 11.5 %collective-permute-start.46 = (bf16[144,576]{1,0:T(8,128)(2,1)S(1)}, bf16[144,576]{1,0:T(8,128)(2,1)S(1)}, u32[]{:S(2)}, u32[]{:S(2)}) collective-permute-start(bf16[144,576]{1,0:T(8,128)(2,1)S(1)} %get-tuple-element.160), channel_id=1, source_target_pairs={{0,3},{1,2},{2,1},{3,0},{4,7},{5,6},{6,5},{7,4},{8,11},{9,10},{10,... | collective-permute-start | bytes 497672 | tf_op jit(solution)/shard_map/ppermute | solution.py:45
  137.4 23.6 %collective-permute-start.29 = (bf16[1632,128]{1,0:T(8,128)(2,1)S(1)}, bf16[1632,128]{1,0:T(8,128)(2,1)}, u32[]{:S(2)}, u32[]{:S(2)}) collective-permute-start(bf16[1632,128]{1,0:T(8,128)(2,1)S(1)} %pad_maximum_fusion.2), channel_id=1, source_target_pairs={{0,8},{4,12},{8,0},{12,4},{16,24},{20,28},{24,16},{28,20},{1,9},{5... | collective-permute-start | bytes 1253384 | tf_op jit(solution)/shard_map/ppermute | solution.py:45
  138.7 13.7 %collective-permute-start.45 = (bf16[144,576]{1,0:T(8,128)(2,1)}, bf16[144,576]{1,0:T(8,128)(2,1)}, u32[]{:S(2)}, u32[]{:S(2)}) collective-permute-start(bf16[144,576]{1,0:T(8,128)(2,1)} %get-tuple-element.161), channel_id=1, source_target_pairs={{0,2},{1,3},{2,0},{3,1},{4,6},{5,7},{6,4},{7,5},{8,10},{9,11},{10,... | collective-permute-start | bytes 497672 | tf_op jit(solution)/shard_map/ppermute | solution.py:45
  143.7 12.6 %collective-permute-start.44 = (bf16[144,576]{1,0:T(8,128)(2,1)}, bf16[144,576]{1,0:T(8,128)(2,1)}, u32[]{:S(2)}, u32[]{:S(2)}) collective-permute-start(bf16[144,576]{1,0:T(8,128)(2,1)} %get-tuple-element.159), channel_id=1, source_target_pairs={{0,1},{1,0},{2,3},{3,2},{4,5},{5,4},{6,7},{7,6},{8,9},{9,8},{10,11... | collective-permute-start | bytes 497672 | tf_op jit(solution)/shard_map/ppermute | solution.py:45
  157.5 7.6 %collective-permute-start.47 = (bf16[144,576]{1,0:T(8,128)(2,1)S(1)}, bf16[144,576]{1,0:T(8,128)(2,1)S(1)}, u32[]{:S(2)}, u32[]{:S(2)}) collective-permute-start(bf16[144,576]{1,0:T(8,128)(2,1)S(1)} %fusion.18.refs_0_), channel_id=1, source_target_pairs={{0,8},{4,12},{8,0},{12,4},{16,24},{20,28},{24,16},{28,20},{1,9},{5... | collective-permute-start | bytes 497672 | tf_op jit(solution)/shard_map/ppermute | solution.py:45
  158.8 9.0 %collective-permute-start.48 = (bf16[144,576]{1,0:T(8,128)(2,1)S(1)}, bf16[144,576]{1,0:T(8,128)(2,1)S(1)}, u32[]{:S(2)}, u32[]{:S(2)}) collective-permute-start(bf16[144,576]{1,0:T(8,128)(2,1)S(1)} %fusion.18.refs_0_), channel_id=1, source_target_pairs={{0,16},{4,20},{8,24},{12,28},{16,0},{20,4},{24,8},{28,12},{1,17},{... | collective-permute-start | bytes 497672 | tf_op jit(solution)/shard_map/ppermute | solution.py:45
  159.6 9.3 %collective-permute-start.49 = (bf16[144,576]{1,0:T(8,128)(2,1)S(1)}, bf16[144,576]{1,0:T(8,128)(2,1)S(1)}, u32[]{:S(2)}, u32[]{:S(2)}) collective-permute-start(bf16[144,576]{1,0:T(8,128)(2,1)S(1)} %fusion.18.refs_0_), channel_id=1, source_target_pairs={{0,24},{4,28},{8,16},{12,20},{16,8},{20,12},{24,0},{28,4},{1,25},{... | collective-permute-start | bytes 497672 | tf_op jit(solution)/shard_map/ppermute | solution.py:45
  162.5 6.4 %collective-permute-start.36 = (bf16[216,128]{1,0:T(8,128)(2,1)S(1)}, bf16[216,128]{1,0:T(8,128)(2,1)S(1)}, u32[]{:S(2)}, u32[]{:S(2)}) collective-permute-start(bf16[216,128]{1,0:T(8,128)(2,1)S(1)} %get-tuple-element.172), channel_id=1, source_target_pairs={{0,3},{1,2},{2,1},{3,0},{4,7},{5,6},{6,5},{7,4},{8,11},{9,10},{10,... | collective-permute-start | bytes 165896 | tf_op jit(solution)/shard_map/ppermute | solution.py:45
  164.1 5.9 %collective-permute-start.35 = (bf16[216,128]{1,0:T(8,128)(2,1)S(1)}, bf16[216,128]{1,0:T(8,128)(2,1)S(1)}, u32[]{:S(2)}, u32[]{:S(2)}) collective-permute-start(bf16[216,128]{1,0:T(8,128)(2,1)S(1)} %get-tuple-element.173), channel_id=1, source_target_pairs={{0,2},{1,3},{2,0},{3,1},{4,6},{5,7},{6,4},{7,5},{8,10},{9,11},{10,... | collective-permute-start | bytes 165896 | tf_op jit(solution)/shard_map/ppermute | solution.py:45
  165.1 5.2 %collective-permute-start.34 = (bf16[216,128]{1,0:T(8,128)(2,1)S(1)}, bf16[216,128]{1,0:T(8,128)(2,1)S(1)}, u32[]{:S(2)}, u32[]{:S(2)}) collective-permute-start(bf16[216,128]{1,0:T(8,128)(2,1)S(1)} %get-tuple-element.171), channel_id=1, source_target_pairs={{0,1},{1,0},{2,3},{3,2},{4,5},{5,4},{6,7},{7,6},{8,9},{9,8},{10,11... | collective-permute-start | bytes 165896 | tf_op jit(solution)/shard_map/ppermute | solution.py:45
  167.8 4.0 %collective-permute-start.50 = (bf16[144,576]{1,0:T(8,128)(2,1)S(1)}, bf16[144,576]{1,0:T(8,128)(2,1)S(1)}, u32[]{:S(2)}, u32[]{:S(2)}) collective-permute-start(bf16[144,576]{1,0:T(8,128)(2,1)S(1)} %fusion.18.refs_0_), channel_id=1, source_target_pairs={{0,4},{4,0},{8,12},{12,8},{16,20},{20,16},{24,28},{28,24},{1,5},{5... | collective-permute-start | bytes 497672 | tf_op jit(solution)/shard_map/ppermute | solution.py:45
  168.9 3.5 %collective-permute-start.51 = (bf16[144,576]{1,0:T(8,128)(2,1)S(1)}, bf16[144,576]{1,0:T(8,128)(2,1)S(1)}, u32[]{:S(2)}, u32[]{:S(2)}) collective-permute-start(bf16[144,576]{1,0:T(8,128)(2,1)S(1)} %collective-permute-done.47.refs_1_), channel_id=1, source_target_pairs={{0,4},{4,0},{8,12},{12,8},{16,20},{20,16},{24,28},{28,24},{1,5},{5... | collective-permute-start | bytes 497672 | tf_op jit(solution)/shard_map/ppermute | solution.py:45
  168.9 5.0 %collective-permute-start.52 = (bf16[144,576]{1,0:T(8,128)(2,1)S(1)}, bf16[144,576]{1,0:T(8,128)(2,1)S(1)}, u32[]{:S(2)}, u32[]{:S(2)}) collective-permute-start(bf16[144,576]{1,0:T(8,128)(2,1)S(1)} %collective-permute-done.48.refs_2_), channel_id=1, source_target_pairs={{0,4},{4,0},{8,12},{12,8},{16,20},{20,16},{24,28},{28,24},{1,5},{5... | collective-permute-start | bytes 497672 | tf_op jit(solution)/shard_map/ppermute | solution.py:45
  170.1 3.8 %collective-permute-start.53 = (bf16[144,576]{1,0:T(8,128)(2,1)S(1)}, bf16[144,576]{1,0:T(8,128)(2,1)S(1)}, u32[]{:S(2)}, u32[]{:S(2)}) collective-permute-start(bf16[144,576]{1,0:T(8,128)(2,1)S(1)} %collective-permute-done.49.refs_3_), channel_id=1, source_target_pairs={{0,4},{4,0},{8,12},{12,8},{16,20},{20,16},{24,28},{28,24},{1,5},{5... | collective-permute-start | bytes 497672 | tf_op jit(solution)/shard_map/ppermute | solution.py:45
  170.3 8.5 %collective-permute-start.37 = (bf16[216,128]{1,0:T(8,128)(2,1)S(1)}, bf16[216,128]{1,0:T(8,128)(2,1)S(1)}, u32[]{:S(2)}, u32[]{:S(2)}) collective-permute-start(bf16[216,128]{1,0:T(8,128)(2,1)S(1)} %fusion.23.refs_0_), channel_id=1, source_target_pairs={{0,8},{4,12},{8,0},{12,4},{16,24},{20,28},{24,16},{28,20},{1,9},{5... | collective-permute-start | bytes 165896 | tf_op jit(solution)/shard_map/ppermute | solution.py:45
  171.8 7.0 %collective-permute-start.38 = (bf16[216,128]{1,0:T(8,128)(2,1)S(1)}, bf16[216,128]{1,0:T(8,128)(2,1)S(1)}, u32[]{:S(2)}, u32[]{:S(2)}) collective-permute-start(bf16[216,128]{1,0:T(8,128)(2,1)S(1)} %fusion.23.refs_0_), channel_id=1, source_target_pairs={{0,16},{4,20},{8,24},{12,28},{16,0},{20,4},{24,8},{28,12},{1,17},{... | collective-permute-start | bytes 165896 | tf_op jit(solution)/shard_map/ppermute | solution.py:45
  172.4 6.4 %collective-permute-start.39 = (bf16[216,128]{1,0:T(8,128)(2,1)S(1)}, bf16[216,128]{1,0:T(8,128)(2,1)S(1)}, u32[]{:S(2)}, u32[]{:S(2)}) collective-permute-start(bf16[216,128]{1,0:T(8,128)(2,1)S(1)} %fusion.23.refs_0_), channel_id=1, source_target_pairs={{0,24},{4,28},{8,16},{12,20},{16,8},{20,12},{24,0},{28,4},{1,25},{... | collective-permute-start | bytes 165896 | tf_op jit(solution)/shard_map/ppermute | solution.py:45
  178.8 2.2 %collective-permute-start.54 = (bf16[216,128]{1,0:T(8,128)(2,1)S(1)}, bf16[216,128]{1,0:T(8,128)(2,1)S(1)}, u32[]{:S(2)}, u32[]{:S(2)}) collective-permute-start(bf16[216,128]{1,0:T(8,128)(2,1)S(1)} %fusion.23.refs_0_), channel_id=1, source_target_pairs={{0,4},{4,0},{8,12},{12,8},{16,20},{20,16},{24,28},{28,24},{1,5},{5... | collective-permute-start | bytes 165896 | tf_op jit(solution)/shard_map/ppermute | solution.py:45
  178.9 2.1 %collective-permute-start.55 = (bf16[216,128]{1,0:T(8,128)(2,1)S(1)}, bf16[216,128]{1,0:T(8,128)(2,1)S(1)}, u32[]{:S(2)}, u32[]{:S(2)}) collective-permute-start(bf16[216,128]{1,0:T(8,128)(2,1)S(1)} %collective-permute-done.37.refs_1_), channel_id=1, source_target_pairs={{0,4},{4,0},{8,12},{12,8},{16,20},{20,16},{24,28},{28,24},{1,5},{5... | collective-permute-start | bytes 165896 | tf_op jit(solution)/shard_map/ppermute | solution.py:45
  (71 other events, 282.0 us)

commit v5 on v4

--- a/solution.py
+++ b/solution.py
@@ -164,7 +164,7 @@
         return lax.dynamic_index_in_dim(values, index ^ offset, 0, keepdims=False)
 
     total = pick(0).astype(jnp.float32)
-    for i in range(1, count):
+    for i in reversed(range(1, count)):
         total = total + swap(pick(i), "fsdp", i).astype(jnp.float32)
     return total
 
@@ -587,8 +587,9 @@
     rows = D // shards
     down_rows = ff // shards
     half = shards // 2
-    steps = 2
+    steps = 1 if direct else 2
     chunk = width // steps
+    per = chunk // down_rows
     slice_rows = down_rows // (2 * chips)
     pile = rows // slice_rows
 
@@ -633,11 +634,13 @@
             low = dot(activation.T, grad_all)
             if direct:
                 low_ref_f32[...] = low
-                for i in range(chips):
-                    for g in range(2):
-                        start = pl.multiple_of(((chip ^ i) * 2 + g) * slice_rows, 16)
-                        part = low_ref_f32[pl.ds(start, slice_rows), :].astype(jnp.bfloat16)
-                        wide_grads[i][2 * j + g, :, lanes:] = stack_down(part, pile)
+                for n in range(per):
+                    for i in range(chips):
+                        for g in range(2):
+                            start = n * down_rows + ((chip ^ i) * 2 + g) * slice_rows
+                            source = pl.ds(pl.multiple_of(start, 16), slice_rows)
+                            part = low_ref_f32[source, :].astype(jnp.bfloat16)
+                            wide_grads[i][2 * (j * per + n) + g, :, lanes:] = stack_down(part, pile)
             else:
                 refs[5][columns, :] = low.astype(jnp.bfloat16)
         out_ref[...] = result[:row_count]

time: 185 us -> 184 us (level)
  Pallas kernels: 56.8 us -> 66.4 us
  starting transfers between devices: 72.3 us -> 63.4 us
    pallas_call x10, Pallas kernels: 56.8 us -> 66.4 us  [run_kernel(): pl.pallas_call(kernel, out_shape=tuple((jax.ShapeDtypeStruct(*out) for ou...]
    ppermute x57, starting transfers between devices: 68.6 us -> 59.6 us  [swap(): return lax.ppermute(value, axis, [(i, i ^ offset) for i in range(count)])]
  transfers between devices with their start and end apart: 58 -> 58, of which waited for: 18 -> 16; matrix products, arithmetic and copies ran while one was open for 11% -> 11% of each run, Pallas kernels for 21% -> 26%
where the time goes in v5:
time: 184 us
  Pallas kernels  66.4 us (36%)
  starting transfers between devices  63.4 us (34%)
  waiting for transfers between devices  20.4 us (11%)
  local copies, waits for them, and re-layouts  18.4 us (10%)
  other arithmetic  12.1 us (7%)
  between operations  2.17 us (1%)
    pallas_call x10, Pallas kernels, run_kernel(): pl.pallas_call(kernel, out_shape=tuple((jax.ShapeDtypeStruct(*out) for ou...  66.4 us
    ppermute x57, starting transfers between devices, swap(): return lax.ppermute(value, axis, [(i, i ^ offset) for i in range(count)])  59.6 us
    ppermute x57, waiting for transfers between devices, swap(): return lax.ppermute(value, axis, [(i, i ^ offset) for i in range(count)])  20 us
    unnamed x124, local copies, waits for them, and re-layouts  11.4 us
    ppermute x1, starting transfers between devices, start_gather_half(): received = lax.ppermute(piece, ('ctx', 'fsdp'), half_pairs())  3.79 us
  transfers between devices with their start and end apart: 58, of which 16 were waited for; matrix products, arithmetic and copies ran while one was open for 11% of the time, Pallas kernels for 26%

profile of v5, /device:TPU:0, one launch (start us, length us, event | category | flops | bytes accessed | tf_op | source)
XLA Modules:
  0.0 183.5 jit_solution(15223768949208575043)
XLA Ops:
  0.7 1.2 copy.32
  1.9 3.0 %collective-permute-start = (bf16[256,576]{1,0:T(8,128)(2,1)S(1)}, bf16[256,576]{1,0:T(8,128)(2,1)S(1)}, u32[]{:S(2)}, u32[]{:S(2)}) collective-permute-start(bf16[256,576]{1,0:T(8,128)(2,1)S(1)} %bitcast.70), channel_id=1, source_target_pairs={{0,8},{4,12},{8,0},{12,4},{16,24},{20,28},{24,16},{28,20},{1,9},{5... | collective-permute-start | bytes 884744 | tf_op jit(solution)/shard_map/ppermute | solution.py:45
  4.9 1.5 collective-permute-start.1
  7.9 1.1 pad_maximum_fusion.5.refs_8_
  10.0 2.0 %collective-permute-start.3 = (bf16[1,232,128]{2,1,0:T(8,128)(2,1)S(1)}, bf16[1,232,128]{2,1,0:T(8,128)(2,1)S(1)}, u32[]{:S(2)}, u32[]{:S(2)}) collective-permute-start(bf16[1,232,128]{2,1,0:T(8,128)(2,1)S(1)} %maximum_bitcast_fusion), channel_id=1, source_target_pairs={{0,1},{1,0},{2,3},{3,2},{4,5},{5,4},{6,7},{7,6},{8,9},{9,8},{10,11... | collective-permute-start | bytes 178184 | tf_op jit(solution)/shard_map/ppermute | solution.py:45
  15.3 3.0 %collective-permute-start.4 = (bf16[2,232,128]{2,1,0:T(8,128)(2,1)S(1)}, bf16[2,232,128]{2,1,0:T(8,128)(2,1)S(1)}, u32[]{:S(2)}, u32[]{:S(2)}) collective-permute-start(bf16[2,232,128]{2,1,0:T(8,128)(2,1)S(1)} %pad_maximum_fusion.8), channel_id=1, source_target_pairs={{0,2},{1,3},{2,0},{3,1},{4,6},{5,7},{6,4},{7,5},{8,10},{9,11},{10,... | collective-permute-start | bytes 356360 | tf_op jit(solution)/shard_map/ppermute | solution.py:45
  19.1 4.0 %collective-permute-done.4 = bf16[2,232,128]{2,1,0:T(8,128)(2,1)S(1)} collective-permute-done((bf16[2,232,128]{2,1,0:T(8,128)(2,1)S(1)}, bf16[2,232,128]{2,1,0:T(8,128)(2,1)S(1)}, u32[]{:S(2)}, u32[]{:S(2)}) %collective-permute-start.4) | collective-permute-done | bytes 118816 | tf_op jit(solution)/shard_map/ppermute | solution.py:45
  24.0 1.1 collective-permute-start.6
  26.7 2.9 %shard_map.212.hidden_ref = bf16[4,256,576]{2,1,0:T(8,128)(2,1)} custom-call(bf16[256,576]{1,0:T(8,128)(2,1)} %bitcast.73, bf16[256,576]{1,0:T(8,128)(2,1)} %copy-done.30, bf16[256,576]{1,0:T(8,128)(2,1)} %copy-done.31, bf16[256,576]{1,0:T(8,128)(2,1)} %copy-done.32, f32[1,576]{1,0:T(1,128)} %reshape.185.refs_4_), custom_call_target="tpu_custom_call" | custom-call | flops 3449999872 | bytes 1024 | tf_op jit(solution)/shard_map/pallas_call | solution.py:25
  29.5 1.5 collective-permute-start.8
  31.0 1.5 collective-permute-start.9
  33.3 3.8 %collective-permute-start.7 = (bf16[384,576]{1,0:T(8,128)(2,1)S(1)}, bf16[384,576]{1,0:T(8,128)(2,1)S(1)}, u32[]{:S(2)}, u32[]{:S(2)}) collective-permute-start(bf16[384,576]{1,0:T(8,128)(2,1)S(1)} %copy.34), channel_id=1, source_target_pairs={{0,2},{1,3},{6,4},{7,5},{8,10},{9,11},{14,12},{15,13},{16,18},{17,... | collective-permute-start | bytes 1327112 | tf_op jit(solution)/shard_map/ppermute | solution.py:99
  39.0 1.4 copy.35.cos_ref
  40.5 1.3 copy.36.sin_ref
  45.0 5.5 %shard_map.213 = (bf16[256,576]{1,0:T(8,128)(2,1)}, bf16[4,256,384]{2,1,0:T(8,128)(2,1)}, bf16[576,1024]{1,0:T(8,128)(2,1)}, bf16[576,576]{1,0:T(8,128)(2,1)}) custom-call(s32[8]{0:T(128)} %table_ref.5, bf16[4,256,576]{2,1,0:T(8,128)(2,1)} %shard_map.212.hidden_ref, f32[2048,128]{1,0:T(8,128)} %copy.35.cos_ref, f32[2048,128]{1,0:T(8,128)} %copy.36.sin_ref, ...), custom_call_target="tpu_custom_call" | custom-call | flops 5750000128 | bytes 1024 | tf_op jit(solution)/shard_map/pallas_call | solution.py:25
  50.5 1.4 collective-permute-start.15
  52.8 1.5 collective-permute-start.19
  54.3 1.5 collective-permute-start.20
  56.3 4.1 %collective-permute-start.18 = (bf16[1,384,576]{2,1,0:T(8,128)(2,1)S(1)}, bf16[1,384,576]{2,1,0:T(8,128)(2,1)S(1)}, u32[]{:S(2)}, u32[]{:S(2)}) collective-permute-start(bf16[1,384,576]{2,1,0:T(8,128)(2,1)S(1)} %select_bitcast_fusion), channel_id=1, source_target_pairs={{0,1},{1,0},{2,3},{3,2},{4,5},{5,4},{6,7},{7,6},{8,9},{9,8},{10,11... | collective-permute-start | bytes 1327112 | tf_op jit(solution)/shard_map/ppermute | solution.py:45
  61.2 12.2 %shard_map.214 = (f32[256,576]{1,0:T(8,128)}, f32[6,384]{1,0:T(8,128)}) custom-call(s32[8]{0:T(128)} %table_ref.5, s32[16,128]{1,0:T(8,128)} %bitcast.87, bf16[256,576]{1,0:T(8,128)(2,1)} %get-tuple-element.78.query_ref, bf16[4,256,384]{2,1,0:T(8,128)(2,1)} %get-tuple-element.79.own_ref, bf16[4,256,384]{2,1,0:T(8,128)(2,1)} %copy-done.26), custom_call_target="tpu_custom_call" | custom-call | flops 13799999488 | bytes 1024 | tf_op jit(solution)/shard_map/pallas_call | solution.py:25
  73.4 2.9 %shard_map.215 = (f32[256,576]{1,0:T(8,128)}, bf16[256,576]{1,0:T(8,128)(2,1)}) custom-call(f32[256,576]{1,0:T(8,128)} %get-tuple-element.80.attended_ref, bf16[256,576]{1,0:T(8,128)(2,1)} %bitcast.74, bf16[576,576]{1,0:T(8,128)(2,1)} %get-tuple-element.81.out_w_ref, f32[1,576]{1,0:T(1,128)} %reshape.186.gain_ref), custom_call_target="tpu_custom_call" | custom-call | flops 2300000000 | bytes 1024 | tf_op jit(solution)/shard_map/pallas_call | solution.py:25
  76.9 1.1 pad_maximum_fusion.low_ref
  79.7 9.9 %shard_map.216 = (f32[256,576]{1,0:T(8,128)}, f32[256,576]{1,0:T(8,128)}, bf16[2,256,640]{2,1,0:T(8,128)(2,1)}, bf16[4,144,576]{2,1,0:T(8,128)(2,1)}, bf16[4,144...) custom-call(bf16[256,576]{1,0:T(8,128)(2,1)} %get-tuple-element.83.hidden_ref, ...), custom_call_target="tpu_custom_call" | custom-call | flops 13799999488 | bytes 1024 | tf_op jit(solution)/shard_map/pallas_call | solution.py:25
  90.5 1.5 collective-permute-start.41
  92.0 1.2 collective-permute-start.42
  94.0 4.1 %shard_map.217 = (bf16[576,256]{1,0:T(8,128)(2,1)}, f32[256,576]{1,0:T(8,128)}, bf16[256,576]{1,0:T(8,128)(2,1)}, bf16[576,576]{1,0:T(8,128)(2,1)}) custom-call(f32[256,576]{1,0:T(8,128)} %get-tuple-element.82.residual_ref, f32[256,576]{1,0:T(8,128)} %get-tuple-element.86.out_kept_ref, f32[256,576]{1,0:T(8,128)} %get-tuple-element.87.grad_kept_ref, ...), custom_call_target="tpu_custom_call" | custom-call | flops 4600000000 | bytes 1024 | tf_op jit(solution)/shard_map/pallas_call | solution.py:25
  98.1 17.4 %shard_map.218 = (bf16[256,576]{1,0:T(8,128)(2,1)}, bf16[576,576]{1,0:T(8,128)(2,1)}, bf16[4,256,384]{2,1,0:T(8,128)(2,1)}, bf16[256,384]{1,0:T(8,128)(2,1)}, bf...) custom-call(s32[8]{0:T(128)} %table_ref.5, s32[16,128]{1,0:T(8,128)} %bitcast.88, ...), custom_call_target="tpu_custom_call" | custom-call | flops 20700000256 | bytes 1024 | tf_op jit(solution)/shard_map/pallas_call | solution.py:25
  116.0 1.1 collective-permute-done.23.refs_0_
  119.7 5.1 %shard_map.219 = (bf16[768,128]{1,0:T(8,128)(2,1)}, bf16[768,128]{1,0:T(8,128)(2,1)}, bf16[768,128]{1,0:T(8,128)(2,1)}, bf16[768,128]{1,0:T(8,128)(2,1)}, bf16[4...) custom-call(bf16[4,256,384]{2,1,0:T(8,128)(2,1)} %get-tuple-element., ...), custom_call_target="tpu_custom_call" | custom-call | bytes 1024 | tf_op jit(solution)/shard_map/pallas_call | solution.py:25
  128.5 1.8 %collective-permute-start.33 = (bf16[1632,128]{1,0:T(8,128)(2,1)S(1)}, bf16[1632,128]{1,0:T(8,128)(2,1)S(1)}, u32[]{:S(2)}, u32[]{:S(2)}) collective-permute-start(bf16[1632,128]{1,0:T(8,128)(2,1)S(1)} %pad_maximum_fusion.4), channel_id=1, source_target_pairs={{0,24},{4,28},{8,16},{12,20},{16,8},{20,12},{24,0},{28,4},{1,25},{... | collective-permute-start | bytes 1253384 | tf_op jit(solution)/shard_map/ppermute | solution.py:45
  132.0 2.0 %collective-permute-start.46 = (bf16[144,576]{1,0:T(8,128)(2,1)S(1)}, bf16[144,576]{1,0:T(8,128)(2,1)S(1)}, u32[]{:S(2)}, u32[]{:S(2)}) collective-permute-start(bf16[144,576]{1,0:T(8,128)(2,1)S(1)} %get-tuple-element.160), channel_id=1, source_target_pairs={{0,1},{1,0},{2,3},{3,2},{4,5},{5,4},{6,7},{7,6},{8,9},{9,8},{10,11... | collective-permute-start | bytes 497672 | tf_op jit(solution)/shard_map/ppermute | solution.py:45
  134.0 1.3 collective-permute-start.29
  135.3 3.4 %collective-permute-start.45 = (bf16[144,576]{1,0:T(8,128)(2,1)}, bf16[144,576]{1,0:T(8,128)(2,1)}, u32[]{:S(2)}, u32[]{:S(2)}) collective-permute-start(bf16[144,576]{1,0:T(8,128)(2,1)} %get-tuple-element.161), channel_id=1, source_target_pairs={{0,2},{1,3},{2,0},{3,1},{4,6},{5,7},{6,4},{7,5},{8,10},{9,11},{10,... | collective-permute-start | bytes 497672 | tf_op jit(solution)/shard_map/ppermute | solution.py:45
  139.3 5.7 %collective-permute-start.44 = (bf16[144,576]{1,0:T(8,128)(2,1)}, bf16[144,576]{1,0:T(8,128)(2,1)}, u32[]{:S(2)}, u32[]{:S(2)}) collective-permute-start(bf16[144,576]{1,0:T(8,128)(2,1)} %get-tuple-element.159), channel_id=1, source_target_pairs={{0,3},{1,2},{2,1},{3,0},{4,7},{5,6},{6,5},{7,4},{8,11},{9,10},{10,... | collective-permute-start | bytes 497672 | tf_op jit(solution)/shard_map/ppermute | solution.py:45
  145.1 7.2 %collective-permute-done.45 = bf16[144,576]{1,0:T(8,128)(2,1)} collective-permute-done((bf16[144,576]{1,0:T(8,128)(2,1)}, bf16[144,576]{1,0:T(8,128)(2,1)}, u32[]{:S(2)}, u32[]{:S(2)}) %collective-permute-start.45) | collective-permute-done | bytes 165920 | tf_op jit(solution)/shard_map/ppermute | solution.py:45
  152.3 1.2 fusion.18.refs_0_
  154.0 2.0 %collective-permute-start.48 = (bf16[144,576]{1,0:T(8,128)(2,1)S(1)}, bf16[144,576]{1,0:T(8,128)(2,1)S(1)}, u32[]{:S(2)}, u32[]{:S(2)}) collective-permute-start(bf16[144,576]{1,0:T(8,128)(2,1)S(1)} %fusion.18.refs_0_), channel_id=1, source_target_pairs={{0,16},{4,20},{8,24},{12,28},{16,0},{20,4},{24,8},{28,12},{1,17},{... | collective-permute-start | bytes 497672 | tf_op jit(solution)/shard_map/ppermute | solution.py:45
  155.9 1.1 collective-permute-start.49
  157.1 1.4 add_convert_fusion.1
  158.6 3.2 %collective-permute-start.36 = (bf16[216,128]{1,0:T(8,128)(2,1)S(1)}, bf16[216,128]{1,0:T(8,128)(2,1)S(1)}, u32[]{:S(2)}, u32[]{:S(2)}) collective-permute-start(bf16[216,128]{1,0:T(8,128)(2,1)S(1)} %get-tuple-element.172), channel_id=1, source_target_pairs={{0,1},{1,0},{2,3},{3,2},{4,5},{5,4},{6,7},{7,6},{8,9},{9,8},{10,11... | collective-permute-start | bytes 165896 | tf_op jit(solution)/shard_map/ppermute | solution.py:45
  161.8 1.0 collective-permute-start.35
  163.5 1.5 collective-permute-start.34
  165.7 2.0 %collective-permute-done.35 = bf16[216,128]{1,0:T(8,128)(2,1)S(1)} collective-permute-done((bf16[216,128]{1,0:T(8,128)(2,1)S(1)}, bf16[216,128]{1,0:T(8,128)(2,1)S(1)}, u32[]{:S(2)}, u32[]{:S(2)}) %collective-permute-start.35) | collective-permute-done | bytes 55328 | tf_op jit(solution)/shard_map/ppermute | solution.py:45
  167.7 1.9 %collective-permute-done.34 = bf16[216,128]{1,0:T(8,128)(2,1)S(1)} collective-permute-done((bf16[216,128]{1,0:T(8,128)(2,1)S(1)}, bf16[216,128]{1,0:T(8,128)(2,1)S(1)}, u32[]{:S(2)}, u32[]{:S(2)}) %collective-permute-start.34) | collective-permute-done | bytes 55328 | tf_op jit(solution)/shard_map/ppermute | solution.py:45
  170.6 1.5 collective-permute-start.38
  172.1 1.2 collective-permute-start.39
  174.0 4.1 %shard_map.220 = (f32[144,1536]{1,0:T(8,128)}, f32[144,1536]{1,0:T(8,128)}, f32[576,384]{1,0:T(8,128)}, f32[1,144]{1,0:T(1,128)}) custom-call(bf16[144,576]{1,0:T(8,128)(2,1)} %copy-done.21, bf16[144,576]{1,0:T(8,128)(2,1)} %copy-done.43, bf16[144,576]{1,0:T(8,128)(2,1)} %copy-done.44, bf16[144,576]{1,0:T(8,128)(2,1)} %copy-done.45, ...), custom_call_target="tpu_custom_call" | custom-call | flops 4600000000 | bytes 1024 | tf_op jit(solution)/shard_map/pallas_call | solution.py:25
  181.1 2.4 %shard_map.221 = (f32[144,576]{1,0:T(8,128)}, f32[144,192]{1,0:T(8,128)}, f32[144,192]{1,0:T(8,128)}, f32[144,576]{1,0:T(8,128)}, f32[1,144]{1,0:T(1,128)}) custom-call(bf16[216,128]{1,0:T(8,128)(2,1)} %copy-done.23, bf16[216,128]{1,0:T(8,128)(2,1)} %copy-done.50, bf16[216,128]{1,0:T(8,128)(2,1)} %copy-done.51, bf16[216,128]{1,0:T(8,128)(2,1)} %copy-done.52, ...), custom_call_target="tpu_custom_call" | custom-call | flops 2300000000 | bytes 1024 | tf_op jit(solution)/shard_map/pallas_call | solution.py:25
  (267 shorter events, 35.6 us)
Async XLA Ops:
  1.9 23.2 %collective-permute-start = (bf16[256,576]{1,0:T(8,128)(2,1)S(1)}, bf16[256,576]{1,0:T(8,128)(2,1)S(1)}, u32[]{:S(2)}, u32[]{:S(2)}) collective-permute-start(bf16[256,576]{1,0:T(8,128)(2,1)S(1)} %bitcast.70), channel_id=1, source_target_pairs={{0,8},{4,12},{8,0},{12,4},{16,24},{20,28},{24,16},{28,20},{1,9},{5... | collective-permute-start | bytes 884744 | tf_op jit(solution)/shard_map/ppermute | solution.py:45
  4.9 20.2 %collective-permute-start.1 = (bf16[256,576]{1,0:T(8,128)(2,1)S(1)}, bf16[256,576]{1,0:T(8,128)(2,1)S(1)}, u32[]{:S(2)}, u32[]{:S(2)}) collective-permute-start(bf16[256,576]{1,0:T(8,128)(2,1)S(1)} %bitcast.71), channel_id=1, source_target_pairs={{0,16},{4,20},{8,24},{12,28},{16,0},{20,4},{24,8},{28,12},{1,17},{... | collective-permute-start | bytes 884744 | tf_op jit(solution)/shard_map/ppermute | solution.py:45
  6.4 18.7 %collective-permute-start.2 = (bf16[256,576]{1,0:T(8,128)(2,1)S(1)}, bf16[256,576]{1,0:T(8,128)(2,1)S(1)}, u32[]{:S(2)}, u32[]{:S(2)}) collective-permute-start(bf16[256,576]{1,0:T(8,128)(2,1)S(1)} %bitcast.72), channel_id=1, source_target_pairs={{0,24},{4,28},{8,16},{12,20},{16,8},{20,12},{24,0},{28,4},{1,25},{... | collective-permute-start | bytes 884744 | tf_op jit(solution)/shard_map/ppermute | solution.py:45
  10.0 5.2 %collective-permute-start.3 = (bf16[1,232,128]{2,1,0:T(8,128)(2,1)S(1)}, bf16[1,232,128]{2,1,0:T(8,128)(2,1)S(1)}, u32[]{:S(2)}, u32[]{:S(2)}) collective-permute-start(bf16[1,232,128]{2,1,0:T(8,128)(2,1)S(1)} %maximum_bitcast_fusion), channel_id=1, source_target_pairs={{0,1},{1,0},{2,3},{3,2},{4,5},{5,4},{6,7},{7,6},{8,9},{9,8},{10,11... | collective-permute-start | bytes 178184 | tf_op jit(solution)/shard_map/ppermute | solution.py:45
  13.0 6.0 %collective-permute-start.5 = (bf16[1,144,384]{2,1,0:T(8,128)(2,1)S(1)}, bf16[1,144,384]{2,1,0:T(8,128)(2,1)S(1)}, u32[]{:S(2)}, u32[]{:S(2)}) collective-permute-start(bf16[1,144,384]{2,1,0:T(8,128)(2,1)S(1)} %fusion.20), channel_id=1, source_target_pairs={{0,1},{1,0},{2,3},{3,2},{4,5},{5,4},{6,7},{7,6},{8,9},{9,8},{10,11... | collective-permute-start | bytes 331784 | tf_op jit(solution)/shard_map/ppermute | solution.py:45
  15.3 7.8 %collective-permute-start.4 = (bf16[2,232,128]{2,1,0:T(8,128)(2,1)S(1)}, bf16[2,232,128]{2,1,0:T(8,128)(2,1)S(1)}, u32[]{:S(2)}, u32[]{:S(2)}) collective-permute-start(bf16[2,232,128]{2,1,0:T(8,128)(2,1)S(1)} %pad_maximum_fusion.8), channel_id=1, source_target_pairs={{0,2},{1,3},{2,0},{3,1},{4,6},{5,7},{6,4},{7,5},{8,10},{9,11},{10,... | collective-permute-start | bytes 356360 | tf_op jit(solution)/shard_map/ppermute | solution.py:45
  24.0 17.9 %collective-permute-start.6 = (bf16[2,144,384]{2,1,0:T(8,128)(2,1)S(1)}, bf16[2,144,384]{2,1,0:T(8,128)(2,1)S(1)}, u32[]{:S(2)}, u32[]{:S(2)}) collective-permute-start(bf16[2,144,384]{2,1,0:T(8,128)(2,1)S(1)} %pad_maximum_fusion.7), channel_id=1, source_target_pairs={{0,2},{1,3},{2,0},{3,1},{4,6},{5,7},{6,4},{7,5},{8,10},{9,11},{10,... | collective-permute-start | bytes 663560 | tf_op jit(solution)/shard_map/ppermute | solution.py:45
  29.5 12.4 %collective-permute-start.8 = (bf16[4,232,128]{2,1,0:T(8,128)(2,1)S(1)}, bf16[4,232,128]{2,1,0:T(8,128)(2,1)S(1)}, u32[]{:S(2)}, u32[]{:S(2)}) collective-permute-start(bf16[4,232,128]{2,1,0:T(8,128)(2,1)S(1)} %pad_maximum_fusion.6.refs_0_), channel_id=1, source_target_pairs={{0,8},{4,12},{8,0},{12,4},{16,24},{20,28},{24,16},{28,20},{1,9},{5... | collective-permute-start | bytes 712712 | tf_op jit(solution)/shard_map/ppermute | solution.py:45
  31.0 11.5 %collective-permute-start.9 = (bf16[4,232,128]{2,1,0:T(8,128)(2,1)S(1)}, bf16[4,232,128]{2,1,0:T(8,128)(2,1)}, u32[]{:S(2)}, u32[]{:S(2)}) collective-permute-start(bf16[4,232,128]{2,1,0:T(8,128)(2,1)S(1)} %pad_maximum_fusion.6.refs_0_), channel_id=1, source_target_pairs={{0,16},{4,20},{8,24},{12,28},{16,0},{20,4},{24,8},{28,12},{1,17},{... | collective-permute-start | bytes 712712 | tf_op jit(solution)/shard_map/ppermute | solution.py:45
  32.5 10.1 %collective-permute-start.10 = (bf16[4,232,128]{2,1,0:T(8,128)(2,1)S(1)}, bf16[4,232,128]{2,1,0:T(8,128)(2,1)}, u32[]{:S(2)}, u32[]{:S(2)}) collective-permute-start(bf16[4,232,128]{2,1,0:T(8,128)(2,1)S(1)} %pad_maximum_fusion.6.refs_0_), channel_id=1, source_target_pairs={{0,24},{4,28},{8,16},{12,20},{16,8},{20,12},{24,0},{28,4},{1,25},{... | collective-permute-start | bytes 712712 | tf_op jit(solution)/shard_map/ppermute | solution.py:45
  33.3 10.1 %collective-permute-start.7 = (bf16[384,576]{1,0:T(8,128)(2,1)S(1)}, bf16[384,576]{1,0:T(8,128)(2,1)S(1)}, u32[]{:S(2)}, u32[]{:S(2)}) collective-permute-start(bf16[384,576]{1,0:T(8,128)(2,1)S(1)} %copy.34), channel_id=1, source_target_pairs={{0,2},{1,3},{6,4},{7,5},{8,10},{9,11},{14,12},{15,13},{16,18},{17,... | collective-permute-start | bytes 1327112 | tf_op jit(solution)/shard_map/ppermute | solution.py:99
  42.6 2.1 %collective-permute-start.14 = (bf16[4,232,128]{2,1,0:T(8,128)(2,1)}, bf16[4,232,128]{2,1,0:T(8,128)(2,1)}, u32[]{:S(2)}, u32[]{:S(2)}) collective-permute-start(bf16[4,232,128]{2,1,0:T(8,128)(2,1)} %collective-permute-done.10.refs_3_), channel_id=1, source_target_pairs={{0,4},{4,0},{8,12},{12,8},{16,20},{20,16},{24,28},{28,24},{1,5},{5... | collective-permute-start | bytes 712712 | tf_op jit(solution)/shard_map/ppermute | solution.py:45
  50.5 9.8 %collective-permute-start.15 = (bf16[4,256,384]{2,1,0:T(8,128)(2,1)}, bf16[4,256,384]{2,1,0:T(8,128)(2,1)S(1)}, u32[]{:S(2)}, u32[]{:S(2)}) collective-permute-start(bf16[4,256,384]{2,1,0:T(8,128)(2,1)} %get-tuple-element.79.own_ref), channel_id=1, source_target_pairs={{0,4},{4,0},{8,12},{12,8},{16,20},{20,16},{24,28},{28,24},{1,5},{5... | collective-permute-start | bytes 2359304 | tf_op jit(solution)/shard_map/ppermute | solution.py:45
  52.8 25.2 %collective-permute-start.19 = (bf16[4,144,384]{2,1,0:T(8,128)(2,1)S(1)}, bf16[4,144,384]{2,1,0:T(8,128)(2,1)S(1)}, u32[]{:S(2)}, u32[]{:S(2)}) collective-permute-start(bf16[4,144,384]{2,1,0:T(8,128)(2,1)S(1)} %pad_maximum_fusion.1.refs_0_), channel_id=1, source_target_pairs={{0,8},{4,12},{8,0},{12,4},{16,24},{20,28},{24,16},{28,20},{1,9},{5... | collective-permute-start | bytes 1327112 | tf_op jit(solution)/shard_map/ppermute | solution.py:45
  54.3 23.7 %collective-permute-start.20 = (bf16[4,144,384]{2,1,0:T(8,128)(2,1)S(1)}, bf16[4,144,384]{2,1,0:T(8,128)(2,1)S(1)}, u32[]{:S(2)}, u32[]{:S(2)}) collective-permute-start(bf16[4,144,384]{2,1,0:T(8,128)(2,1)S(1)} %pad_maximum_fusion.1.refs_0_), channel_id=1, source_target_pairs={{0,16},{4,20},{8,24},{12,28},{16,0},{20,4},{24,8},{28,12},{1,17},{... | collective-permute-start | bytes 1327112 | tf_op jit(solution)/shard_map/ppermute | solution.py:45
  55.8 22.2 %collective-permute-start.21 = (bf16[4,144,384]{2,1,0:T(8,128)(2,1)S(1)}, bf16[4,144,384]{2,1,0:T(8,128)(2,1)}, u32[]{:S(2)}, u32[]{:S(2)}) collective-permute-start(bf16[4,144,384]{2,1,0:T(8,128)(2,1)S(1)} %pad_maximum_fusion.1.refs_0_), channel_id=1, source_target_pairs={{0,24},{4,28},{8,16},{12,20},{16,8},{20,12},{24,0},{28,4},{1,25},{... | collective-permute-start | bytes 1327112 | tf_op jit(solution)/shard_map/ppermute | solution.py:45
  56.3 20.0 %collective-permute-start.18 = (bf16[1,384,576]{2,1,0:T(8,128)(2,1)S(1)}, bf16[1,384,576]{2,1,0:T(8,128)(2,1)S(1)}, u32[]{:S(2)}, u32[]{:S(2)}) collective-permute-start(bf16[1,384,576]{2,1,0:T(8,128)(2,1)S(1)} %select_bitcast_fusion), channel_id=1, source_target_pairs={{0,1},{1,0},{2,3},{3,2},{4,5},{5,4},{6,7},{7,6},{8,9},{9,8},{10,11... | collective-permute-start | bytes 1327112 | tf_op jit(solution)/shard_map/ppermute | solution.py:45
  76.3 2.1 %collective-permute-start.17 = (bf16[256,576]{1,0:T(8,128)(2,1)S(1)}, bf16[256,576]{1,0:T(8,128)(2,1)S(1)}, u32[]{:S(2)}, u32[]{:S(2)}) collective-permute-start(bf16[256,576]{1,0:T(8,128)(2,1)S(1)} %bitcast.83), channel_id=1, source_target_pairs={{0,4},{4,0},{8,12},{12,8},{16,20},{20,16},{24,28},{28,24},{1,5},{5... | collective-permute-start | bytes 884744 | tf_op jit(solution)/shard_map/ppermute | solution.py:45
  89.6 3.6 %collective-permute-start.22 = (bf16[2,256,640]{2,1,0:T(8,128)(2,1)}, bf16[2,256,640]{2,1,0:T(8,128)(2,1)S(1)}, u32[]{:S(2)}, u32[]{:S(2)}) collective-permute-start(bf16[2,256,640]{2,1,0:T(8,128)(2,1)} %get-tuple-element.88), channel_id=1, source_target_pairs={{0,4},{4,0},{8,12},{12,8},{16,20},{20,16},{24,28},{28,24},{1,5},{5... | collective-permute-start | bytes 1966088 | tf_op jit(solution)/shard_map/ppermute | solution.py:45
  89.7 35.1 %collective-permute-start.40 = (bf16[4,144,576]{2,1,0:T(8,128)(2,1)}, bf16[4,144,576]{2,1,0:T(8,128)(2,1)S(1)}, u32[]{:S(2)}, u32[]{:S(2)}) collective-permute-start(bf16[4,144,576]{2,1,0:T(8,128)(2,1)} %get-tuple-element.115), channel_id=1, source_target_pairs={{0,8},{4,12},{8,0},{12,4},{16,24},{20,28},{24,16},{28,20},{1,9},{5... | collective-permute-start | bytes 1990664 | tf_op jit(solution)/shard_map/ppermute | solution.py:45
  90.5 34.3 %collective-permute-start.41 = (bf16[4,144,576]{2,1,0:T(8,128)(2,1)}, bf16[4,144,576]{2,1,0:T(8,128)(2,1)S(1)}, u32[]{:S(2)}, u32[]{:S(2)}) collective-permute-start(bf16[4,144,576]{2,1,0:T(8,128)(2,1)} %get-tuple-element.116), channel_id=1, source_target_pairs={{0,16},{4,20},{8,24},{12,28},{16,0},{20,4},{24,8},{28,12},{1,17},{... | collective-permute-start | bytes 1990664 | tf_op jit(solution)/shard_map/ppermute | solution.py:45
  92.0 33.5 %collective-permute-start.42 = (bf16[4,144,576]{2,1,0:T(8,128)(2,1)}, bf16[4,144,576]{2,1,0:T(8,128)(2,1)S(1)}, u32[]{:S(2)}, u32[]{:S(2)}) collective-permute-start(bf16[4,144,576]{2,1,0:T(8,128)(2,1)} %get-tuple-element.117), channel_id=1, source_target_pairs={{0,24},{4,28},{8,16},{12,20},{16,8},{20,12},{24,0},{28,4},{1,25},{... | collective-permute-start | bytes 1990664 | tf_op jit(solution)/shard_map/ppermute | solution.py:45
  115.4 1.9 %collective-permute-start.24 = (bf16[256,384]{1,0:T(8,128)(2,1)}, bf16[256,384]{1,0:T(8,128)(2,1)S(1)}, u32[]{:S(2)}, u32[]{:S(2)}) collective-permute-start(bf16[256,384]{1,0:T(8,128)(2,1)} %get-tuple-element.97), channel_id=1, source_target_pairs={{0,4},{4,0},{8,12},{12,8},{16,20},{20,16},{24,28},{28,24},{1,5},{5... | collective-permute-start | bytes 589832 | tf_op jit(solution)/shard_map/ppermute | solution.py:45
  126.0 1.9 %collective-permute-start.43 = (bf16[2,144,192]{2,1,0:T(8,128)(2,1)S(1)}, bf16[2,144,192]{2,1,0:T(8,128)(2,1)S(1)}, u32[]{:S(2)}, u32[]{:S(2)}) collective-permute-start(bf16[2,144,192]{2,1,0:T(8,128)(2,1)S(1)} %dynamic-slice_bitcast_fusion.3), channel_id=1, source_target_pairs={{0,4},{4,0},{8,12},{12,8},{16,20},{20,16},{24,28},{28,24},{1,5},{5... | collective-permute-start | bytes 331784 | tf_op jit(solution)/shard_map/ppermute | solution.py:45
  127.0 3.3 %collective-permute-start.30 = (bf16[4,216,128]{2,1,0:T(8,128)(2,1)S(1)}, bf16[4,216,128]{2,1,0:T(8,128)(2,1)S(1)}, u32[]{:S(2)}, u32[]{:S(2)}) collective-permute-start(bf16[4,216,128]{2,1,0:T(8,128)(2,1)S(1)} %copy-done.41), channel_id=1, source_target_pairs={{0,4},{4,0},{8,12},{12,8},{16,20},{20,16},{24,28},{28,24},{1,5},{5... | collective-permute-start | bytes 663560 | tf_op jit(solution)/shard_map/ppermute | solution.py:45
  127.4 3.6 %collective-permute-start.28 = (bf16[4,216,128]{2,1,0:T(8,128)(2,1)S(1)}, bf16[4,216,128]{2,1,0:T(8,128)(2,1)S(1)}, u32[]{:S(2)}, u32[]{:S(2)}) collective-permute-start(bf16[4,216,128]{2,1,0:T(8,128)(2,1)S(1)} %copy-done.40), channel_id=1, source_target_pairs={{0,4},{4,0},{8,12},{12,8},{16,20},{20,16},{24,28},{28,24},{1,5},{5... | collective-permute-start | bytes 663560 | tf_op jit(solution)/shard_map/ppermute | solution.py:45
  127.5 3.6 %collective-permute-start.27 = (bf16[4,216,128]{2,1,0:T(8,128)(2,1)S(1)}, bf16[4,216,128]{2,1,0:T(8,128)(2,1)S(1)}, u32[]{:S(2)}, u32[]{:S(2)}) collective-permute-start(bf16[4,216,128]{2,1,0:T(8,128)(2,1)S(1)} %copy-done.39), channel_id=1, source_target_pairs={{0,4},{4,0},{8,12},{12,8},{16,20},{20,16},{24,28},{28,24},{1,5},{5... | collective-permute-start | bytes 663560 | tf_op jit(solution)/shard_map/ppermute | solution.py:45
  128.5 27.5 %collective-permute-start.33 = (bf16[1632,128]{1,0:T(8,128)(2,1)S(1)}, bf16[1632,128]{1,0:T(8,128)(2,1)S(1)}, u32[]{:S(2)}, u32[]{:S(2)}) collective-permute-start(bf16[1632,128]{1,0:T(8,128)(2,1)S(1)} %pad_maximum_fusion.4), channel_id=1, source_target_pairs={{0,24},{4,28},{8,16},{12,20},{16,8},{20,12},{24,0},{28,4},{1,25},{... | collective-permute-start | bytes 1253384 | tf_op jit(solution)/shard_map/ppermute | solution.py:45
  130.4 26.6 %collective-permute-start.31 = (bf16[1632,128]{1,0:T(8,128)(2,1)S(1)}, bf16[1632,128]{1,0:T(8,128)(2,1)S(1)}, u32[]{:S(2)}, u32[]{:S(2)}) collective-permute-start(bf16[1632,128]{1,0:T(8,128)(2,1)S(1)} %pad_maximum_fusion.3), channel_id=1, source_target_pairs={{0,16},{4,20},{8,24},{12,28},{16,0},{20,4},{24,8},{28,12},{1,17},{... | collective-permute-start | bytes 1253384 | tf_op jit(solution)/shard_map/ppermute | solution.py:45
  132.0 6.7 %collective-permute-start.46 = (bf16[144,576]{1,0:T(8,128)(2,1)S(1)}, bf16[144,576]{1,0:T(8,128)(2,1)S(1)}, u32[]{:S(2)}, u32[]{:S(2)}) collective-permute-start(bf16[144,576]{1,0:T(8,128)(2,1)S(1)} %get-tuple-element.160), channel_id=1, source_target_pairs={{0,1},{1,0},{2,3},{3,2},{4,5},{5,4},{6,7},{7,6},{8,9},{9,8},{10,11... | collective-permute-start | bytes 497672 | tf_op jit(solution)/shard_map/ppermute | solution.py:45
  134.0 23.1 %collective-permute-start.29 = (bf16[1632,128]{1,0:T(8,128)(2,1)S(1)}, bf16[1632,128]{1,0:T(8,128)(2,1)}, u32[]{:S(2)}, u32[]{:S(2)}) collective-permute-start(bf16[1632,128]{1,0:T(8,128)(2,1)S(1)} %pad_maximum_fusion.2), channel_id=1, source_target_pairs={{0,8},{4,12},{8,0},{12,4},{16,24},{20,28},{24,16},{28,20},{1,9},{5... | collective-permute-start | bytes 1253384 | tf_op jit(solution)/shard_map/ppermute | solution.py:45
  135.3 17.0 %collective-permute-start.45 = (bf16[144,576]{1,0:T(8,128)(2,1)}, bf16[144,576]{1,0:T(8,128)(2,1)}, u32[]{:S(2)}, u32[]{:S(2)}) collective-permute-start(bf16[144,576]{1,0:T(8,128)(2,1)} %get-tuple-element.161), channel_id=1, source_target_pairs={{0,2},{1,3},{2,0},{3,1},{4,6},{5,7},{6,4},{7,5},{8,10},{9,11},{10,... | collective-permute-start | bytes 497672 | tf_op jit(solution)/shard_map/ppermute | solution.py:45
  139.3 13.0 %collective-permute-start.44 = (bf16[144,576]{1,0:T(8,128)(2,1)}, bf16[144,576]{1,0:T(8,128)(2,1)}, u32[]{:S(2)}, u32[]{:S(2)}) collective-permute-start(bf16[144,576]{1,0:T(8,128)(2,1)} %get-tuple-element.159), channel_id=1, source_target_pairs={{0,3},{1,2},{2,1},{3,0},{4,7},{5,6},{6,5},{7,4},{8,11},{9,10},{10,... | collective-permute-start | bytes 497672 | tf_op jit(solution)/shard_map/ppermute | solution.py:45
  153.5 10.0 %collective-permute-start.47 = (bf16[144,576]{1,0:T(8,128)(2,1)S(1)}, bf16[144,576]{1,0:T(8,128)(2,1)S(1)}, u32[]{:S(2)}, u32[]{:S(2)}) collective-permute-start(bf16[144,576]{1,0:T(8,128)(2,1)S(1)} %fusion.18.refs_0_), channel_id=1, source_target_pairs={{0,8},{4,12},{8,0},{12,4},{16,24},{20,28},{24,16},{28,20},{1,9},{5... | collective-permute-start | bytes 497672 | tf_op jit(solution)/shard_map/ppermute | solution.py:45
  154.0 11.1 %collective-permute-start.48 = (bf16[144,576]{1,0:T(8,128)(2,1)S(1)}, bf16[144,576]{1,0:T(8,128)(2,1)S(1)}, u32[]{:S(2)}, u32[]{:S(2)}) collective-permute-start(bf16[144,576]{1,0:T(8,128)(2,1)S(1)} %fusion.18.refs_0_), channel_id=1, source_target_pairs={{0,16},{4,20},{8,24},{12,28},{16,0},{20,4},{24,8},{28,12},{1,17},{... | collective-permute-start | bytes 497672 | tf_op jit(solution)/shard_map/ppermute | solution.py:45
  155.9 9.2 %collective-permute-start.49 = (bf16[144,576]{1,0:T(8,128)(2,1)S(1)}, bf16[144,576]{1,0:T(8,128)(2,1)S(1)}, u32[]{:S(2)}, u32[]{:S(2)}) collective-permute-start(bf16[144,576]{1,0:T(8,128)(2,1)S(1)} %fusion.18.refs_0_), channel_id=1, source_target_pairs={{0,24},{4,28},{8,16},{12,20},{16,8},{20,12},{24,0},{28,4},{1,25},{... | collective-permute-start | bytes 497672 | tf_op jit(solution)/shard_map/ppermute | solution.py:45
  158.6 7.1 %collective-permute-start.36 = (bf16[216,128]{1,0:T(8,128)(2,1)S(1)}, bf16[216,128]{1,0:T(8,128)(2,1)S(1)}, u32[]{:S(2)}, u32[]{:S(2)}) collective-permute-start(bf16[216,128]{1,0:T(8,128)(2,1)S(1)} %get-tuple-element.172), channel_id=1, source_target_pairs={{0,1},{1,0},{2,3},{3,2},{4,5},{5,4},{6,7},{7,6},{8,9},{9,8},{10,11... | collective-permute-start | bytes 165896 | tf_op jit(solution)/shard_map/ppermute | solution.py:45
  161.8 6.0 %collective-permute-start.35 = (bf16[216,128]{1,0:T(8,128)(2,1)S(1)}, bf16[216,128]{1,0:T(8,128)(2,1)S(1)}, u32[]{:S(2)}, u32[]{:S(2)}) collective-permute-start(bf16[216,128]{1,0:T(8,128)(2,1)S(1)} %get-tuple-element.173), channel_id=1, source_target_pairs={{0,2},{1,3},{2,0},{3,1},{4,6},{5,7},{6,4},{7,5},{8,10},{9,11},{10,... | collective-permute-start | bytes 165896 | tf_op jit(solution)/shard_map/ppermute | solution.py:45
  163.5 6.1 %collective-permute-start.34 = (bf16[216,128]{1,0:T(8,128)(2,1)S(1)}, bf16[216,128]{1,0:T(8,128)(2,1)S(1)}, u32[]{:S(2)}, u32[]{:S(2)}) collective-permute-start(bf16[216,128]{1,0:T(8,128)(2,1)S(1)} %get-tuple-element.171), channel_id=1, source_target_pairs={{0,3},{1,2},{2,1},{3,0},{4,7},{5,6},{6,5},{7,4},{8,11},{9,10},{10,... | collective-permute-start | bytes 165896 | tf_op jit(solution)/shard_map/ppermute | solution.py:45
  165.0 5.5 %collective-permute-start.50 = (bf16[144,576]{1,0:T(8,128)(2,1)S(1)}, bf16[144,576]{1,0:T(8,128)(2,1)S(1)}, u32[]{:S(2)}, u32[]{:S(2)}) collective-permute-start(bf16[144,576]{1,0:T(8,128)(2,1)S(1)} %fusion.18.refs_0_), channel_id=1, source_target_pairs={{0,4},{4,0},{8,12},{12,8},{16,20},{20,16},{24,28},{28,24},{1,5},{5... | collective-permute-start | bytes 497672 | tf_op jit(solution)/shard_map/ppermute | solution.py:45
  165.1 7.0 %collective-permute-start.51 = (bf16[144,576]{1,0:T(8,128)(2,1)S(1)}, bf16[144,576]{1,0:T(8,128)(2,1)S(1)}, u32[]{:S(2)}, u32[]{:S(2)}) collective-permute-start(bf16[144,576]{1,0:T(8,128)(2,1)S(1)} %collective-permute-done.47.refs_1_), channel_id=1, source_target_pairs={{0,4},{4,0},{8,12},{12,8},{16,20},{20,16},{24,28},{28,24},{1,5},{5... | collective-permute-start | bytes 497672 | tf_op jit(solution)/shard_map/ppermute | solution.py:45
  165.6 7.7 %collective-permute-start.52 = (bf16[144,576]{1,0:T(8,128)(2,1)S(1)}, bf16[144,576]{1,0:T(8,128)(2,1)S(1)}, u32[]{:S(2)}, u32[]{:S(2)}) collective-permute-start(bf16[144,576]{1,0:T(8,128)(2,1)S(1)} %collective-permute-done.48.refs_2_), channel_id=1, source_target_pairs={{0,4},{4,0},{8,12},{12,8},{16,20},{20,16},{24,28},{28,24},{1,5},{5... | collective-permute-start | bytes 497672 | tf_op jit(solution)/shard_map/ppermute | solution.py:45
  167.7 5.6 %collective-permute-start.53 = (bf16[144,576]{1,0:T(8,128)(2,1)S(1)}, bf16[144,576]{1,0:T(8,128)(2,1)S(1)}, u32[]{:S(2)}, u32[]{:S(2)}) collective-permute-start(bf16[144,576]{1,0:T(8,128)(2,1)S(1)} %collective-permute-done.49.refs_3_), channel_id=1, source_target_pairs={{0,4},{4,0},{8,12},{12,8},{16,20},{20,16},{24,28},{28,24},{1,5},{5... | collective-permute-start | bytes 497672 | tf_op jit(solution)/shard_map/ppermute | solution.py:45
  169.7 8.5 %collective-permute-start.37 = (bf16[216,128]{1,0:T(8,128)(2,1)S(1)}, bf16[216,128]{1,0:T(8,128)(2,1)S(1)}, u32[]{:S(2)}, u32[]{:S(2)}) collective-permute-start(bf16[216,128]{1,0:T(8,128)(2,1)S(1)} %fusion.23.refs_0_), channel_id=1, source_target_pairs={{0,8},{4,12},{8,0},{12,4},{16,24},{20,28},{24,16},{28,20},{1,9},{5... | collective-permute-start | bytes 165896 | tf_op jit(solution)/shard_map/ppermute | solution.py:45
  170.6 7.6 %collective-permute-start.38 = (bf16[216,128]{1,0:T(8,128)(2,1)S(1)}, bf16[216,128]{1,0:T(8,128)(2,1)S(1)}, u32[]{:S(2)}, u32[]{:S(2)}) collective-permute-start(bf16[216,128]{1,0:T(8,128)(2,1)S(1)} %fusion.23.refs_0_), channel_id=1, source_target_pairs={{0,16},{4,20},{8,24},{12,28},{16,0},{20,4},{24,8},{28,12},{1,17},{... | collective-permute-start | bytes 165896 | tf_op jit(solution)/shard_map/ppermute | solution.py:45
  172.1 6.1 %collective-permute-start.39 = (bf16[216,128]{1,0:T(8,128)(2,1)S(1)}, bf16[216,128]{1,0:T(8,128)(2,1)S(1)}, u32[]{:S(2)}, u32[]{:S(2)}) collective-permute-start(bf16[216,128]{1,0:T(8,128)(2,1)S(1)} %fusion.23.refs_0_), channel_id=1, source_target_pairs={{0,24},{4,28},{8,16},{12,20},{16,8},{20,12},{24,0},{28,4},{1,25},{... | collective-permute-start | bytes 165896 | tf_op jit(solution)/shard_map/ppermute | solution.py:45
  178.2 2.2 %collective-permute-start.54 = (bf16[216,128]{1,0:T(8,128)(2,1)S(1)}, bf16[216,128]{1,0:T(8,128)(2,1)S(1)}, u32[]{:S(2)}, u32[]{:S(2)}) collective-permute-start(bf16[216,128]{1,0:T(8,128)(2,1)S(1)} %fusion.23.refs_0_), channel_id=1, source_target_pairs={{0,4},{4,0},{8,12},{12,8},{16,20},{20,16},{24,28},{28,24},{1,5},{5... | collective-permute-start | bytes 165896 | tf_op jit(solution)/shard_map/ppermute | solution.py:45
  178.3 2.1 %collective-permute-start.55 = (bf16[216,128]{1,0:T(8,128)(2,1)S(1)}, bf16[216,128]{1,0:T(8,128)(2,1)S(1)}, u32[]{:S(2)}, u32[]{:S(2)}) collective-permute-start(bf16[216,128]{1,0:T(8,128)(2,1)S(1)} %collective-permute-done.37.refs_1_), channel_id=1, source_target_pairs={{0,4},{4,0},{8,12},{12,8},{16,20},{20,16},{24,28},{28,24},{1,5},{5... | collective-permute-start | bytes 165896 | tf_op jit(solution)/shard_map/ppermute | solution.py:45
  (71 other events, 293.8 us)
